TPU v7x, 32 devices: a whole 2x2x4 slice. The times are simulated.
32 devices in a mesh: batch: 4 (over z), seq: 8 (over y, x, core).
Axes of the slice: x: 2, y: 2, z: 4, core: 2. Of those that a mesh axis runs over, the one named last changes fastest.
Arguments:
- token_ids: int32 [4, 4096], P('batch', 'seq'), may hold values from 0 to 31999
- book_lengths: int32 [4, 8], P('batch'), may hold values from 1 to 4089, as said below
- loss_mask: int32 [4, 4096], P('batch', 'seq'), may hold values from 0 to 1, as said below
- table_master: float32 [32000, 1024], P(('batch', 'seq')), may hold values from -0.375 to 0.375
- attn_in_master: float32 [1024, 3072], P(('batch', 'seq')), may hold values from -0.1875 to 0.1875
- attn_out_master: float32 [1024, 1024], P(('batch', 'seq')), may hold values from -3 to 3
- compress_master: float32 [3072, 1024], P(('batch', 'seq')), may hold values from -0.109375 to 0.109375
- ffn_in_master: float32 [1024, 4096], P(('batch', 'seq')), may hold values from -0.1875 to 0.1875
- ffn_out_master: float32 [4096, 1024], P(('batch', 'seq')), may hold values from -0.25 to 0.25
- gains_master: float32 [1024, 3], P(('batch', 'seq')), may hold values from 0.5 to 1.5
- table_first: float32 [32000, 1024], P(('batch', 'seq')), may hold values from -0.00021362305 to 0.00021362305
- attn_in_first: float32 [1024, 3072], P(('batch', 'seq')), may hold values from -0.0009765625 to 0.0009765625
- attn_out_first: float32 [1024, 1024], P(('batch', 'seq')), may hold values from -0.0009765625 to 0.0009765625
- compress_first: float32 [3072, 1024], P(('batch', 'seq')), may hold values from -0.0009765625 to 0.0009765625
- ffn_in_first: float32 [1024, 4096], P(('batch', 'seq')), may hold values from -0.0009765625 to 0.0009765625
- ffn_out_first: float32 [4096, 1024], P(('batch', 'seq')), may hold values from -0.0009765625 to 0.0009765625
- gains_first: float32 [1024, 3], P(('batch', 'seq')), may hold values from -0.001953125 to 0.001953125
- table_second: float32 [32000, 1024], P(('batch', 'seq')), may hold values from 4.8828124e-09 to 1.953125e-08
- attn_in_second: float32 [1024, 3072], P(('batch', 'seq')), may hold values from 3.8146973e-06 to 6.1035156e-05
- attn_out_second: float32 [1024, 1024], P(('batch', 'seq')), may hold values from 1.5258789e-07 to 6.1035155e-07
- compress_second: float32 [3072, 1024], P(('batch', 'seq')), may hold values from 1.5258789e-07 to 6.1035155e-07
- ffn_in_second: float32 [1024, 4096], P(('batch', 'seq')), may hold values from 1.5258789e-07 to 6.1035155e-07
- ffn_out_second: float32 [4096, 1024], P(('batch', 'seq')), may hold values from 1.5258789e-07 to 6.1035155e-07
- gains_second: float32 [1024, 3], P(('batch', 'seq')), may hold values from 6.1035155e-07 to 2.4414062e-06
Outputs:
- loss: float32 [], replicated
- table_first_new: float32 [32000, 1024], P(('batch', 'seq'))
- table_second_new: float32 [32000, 1024], P(('batch', 'seq'))
- table_new: float32 [32000, 1024], P(('batch', 'seq'))
- attn_in_first_new: float32 [1024, 3072], P(('batch', 'seq'))
- attn_in_second_new: float32 [1024, 3072], P(('batch', 'seq'))
- attn_in_new: float32 [1024, 3072], P(('batch', 'seq'))
- attn_out_first_new: float32 [1024, 1024], P(('batch', 'seq'))
- attn_out_second_new: float32 [1024, 1024], P(('batch', 'seq'))
- attn_out_new: float32 [1024, 1024], P(('batch', 'seq'))
- compress_first_new: float32 [3072, 1024], P(('batch', 'seq'))
- compress_second_new: float32 [3072, 1024], P(('batch', 'seq'))
- compress_new: float32 [3072, 1024], P(('batch', 'seq'))
- ffn_in_first_new: float32 [1024, 4096], P(('batch', 'seq'))
- ffn_in_second_new: float32 [1024, 4096], P(('batch', 'seq'))
- ffn_in_new: float32 [1024, 4096], P(('batch', 'seq'))
- ffn_out_first_new: float32 [4096, 1024], P(('batch', 'seq'))
- ffn_out_second_new: float32 [4096, 1024], P(('batch', 'seq'))
- ffn_out_new: float32 [4096, 1024], P(('batch', 'seq'))
- gains_first_new: float32 [1024, 3], P(('batch', 'seq'))
- gains_second_new: float32 [1024, 3], P(('batch', 'seq'))
- gains_new: float32 [1024, 3], P(('batch', 'seq'))
Inputs may be any that keep to these rules, and one draw needn't show every extreme that they name: `book_lengths`: a row's lengths sum to 4096; its fourth book starts within the first 512 positions and ends within the last 512; in some row every other book has length 1. `loss_mask`: each aligned run of 512 positions of a row holds at most 256 ones, the last run of every row exactly that many.
All inputs are finite; a program needn't handle non-finite values.
Results may differ from a plain program's by a relative error of at most 0.018.
The roundings to bfloat16 on the way count: a program that leaves them out, or rounds other values in their place, can miss the bound.
Values may be sent and summed in bfloat16 or wider, within the bound.
No kernel may reach another device: no remote copies, remote signals or barrier semaphores. Data moves between devices by JAX's collectives and lax.ppermute only.
A program may use at most 576 MiB of HBM per device.

v0:
```python
import jax
import jax.numpy as jnp
from jax import lax
from jax.sharding import PartitionSpec as P

MODEL_WIDTH = 1024
HEADS = 8
HEAD = 128
NBOOK = 8
STEP = 5


EPSILON = 1e-05
NEGATIVE = -1e30
BETA_ONE = 0.9
BETA_TWO = 0.95
ADAM_EPSILON = 1e-08
WEIGHT_DECAY = 0.1
STEP_RATES = (0.06, 0.03, 0.4, 0.02, 0.03, 0.04, 0.5)


def passed_along(value, axis, steps):
    count = lax.axis_size(axis)
    initial, last = (max(0, -steps), min(count, count - steps))
    return lax.ppermute(value, axis, [(source, source + steps) for source in range(initial, last)])


def norm_forward(values, gain):
    center = values - jnp.mean(values, -1, keepdims=True)
    scaler = lax.rsqrt(jnp.mean(center * center, -1, keepdims=True) + EPSILON)
    unit_rows = center * scaler
    return (unit_rows * gain, unit_rows, scaler)


def norm_backward(grad_out, unit_rows, scaler, gain):
    scaled = grad_out * gain
    grad_gain = jnp.sum(grad_out * unit_rows, axis=(0, 1))
    grad_in = scaler * (
        scaled
        - jnp.mean(scaled, -1, keepdims=True)
        - unit_rows * jnp.mean(scaled * unit_rows, -1, keepdims=True)
    )
    return (grad_in, grad_gain)


def book_number(positions, book_ends):
    spread = jnp.broadcast_to(positions, (book_ends.shape[0], positions.shape[-1]))
    inside = jnp.sum((spread[:, :, None] >= book_ends[:, None, :]).astype(jnp.int32), -1)
    return jnp.where(spread < 0, -1, inside)


def vocab_place(token_rows, vocab_block, seq_count):
    block_index = token_rows // vocab_block
    return (
        block_index % seq_count,
        block_index // seq_count * vocab_block + token_rows % vocab_block,
    )


def project(left_operand, right_operand):
    return jnp.einsum(
        "hwj,jv->hwv", left_operand, right_operand, preferred_element_type=jnp.float32
    )


def split_heads(rows):
    return rows.reshape(rows.shape[0], rows.shape[1], HEADS, HEAD)


def attention_scores(query, key_side, allowed):
    scores = jnp.einsum(
        "sqhd,skhd->shqk",
        split_heads(query),
        split_heads(key_side[..., :MODEL_WIDTH]),
        preferred_element_type=jnp.float32,
    ) * HEAD ** (-0.5)
    return jnp.where(allowed[:, None], scores, NEGATIVE)


def adam_update(master, first, second, grad, rate):
    new_first = BETA_ONE * first + (1.0 - BETA_ONE) * grad
    new_second = BETA_TWO * second + (1.0 - BETA_TWO) * grad * grad
    first_hat = new_first / (1.0 - BETA_ONE**STEP)
    second_hat = new_second / (1.0 - BETA_TWO**STEP)
    new_master = master - rate * (
        first_hat / (jnp.sqrt(second_hat) + ADAM_EPSILON) + WEIGHT_DECAY * master
    )
    return [new_first, new_second, new_master]


def per_device(
    token_ids,
    book_lengths,
    loss_mask,
    table_master,
    attn_in_master,
    attn_out_master,
    compress_master,
    ffn_in_master,
    ffn_out_master,
    gains_master,
    table_first,
    attn_in_first,
    attn_out_first,
    compress_first,
    ffn_in_first,
    ffn_out_first,
    gains_first,
    table_second,
    attn_in_second,
    attn_out_second,
    compress_second,
    ffn_in_second,
    ffn_out_second,
    gains_second,
):
    masters = (
        table_master,
        attn_in_master,
        attn_out_master,
        compress_master,
        ffn_in_master,
        ffn_out_master,
        gains_master,
    )
    firsts = (
        table_first,
        attn_in_first,
        attn_out_first,
        compress_first,
        ffn_in_first,
        ffn_out_first,
        gains_first,
    )
    seconds = (
        table_second,
        attn_in_second,
        attn_out_second,
        compress_second,
        ffn_in_second,
        ffn_out_second,
        gains_second,
    )
    attention_input_weight, attention_output_weight, w_compress, w_ffn_in, w_ffn_out, gains = (
        lax.all_gather(attn_in_master.astype(jnp.bfloat16), ("batch", "seq"), axis=0, tiled=True),
        lax.all_gather(attn_out_master.astype(jnp.bfloat16), ("batch", "seq"), axis=0, tiled=True),
        lax.all_gather(compress_master.astype(jnp.bfloat16), ("batch", "seq"), axis=0, tiled=True),
        lax.all_gather(ffn_in_master.astype(jnp.bfloat16), ("batch", "seq"), axis=0, tiled=True),
        lax.all_gather(ffn_out_master.astype(jnp.bfloat16), ("batch", "seq"), axis=0, tiled=True),
        lax.all_gather(gains_master.astype(jnp.bfloat16), ("batch", "seq"), axis=0, tiled=True),
    )
    table_local = lax.all_gather(table_master.astype(jnp.bfloat16), "batch", axis=0, tiled=True)
    vocab_block = table_master.shape[0]
    seq_count = lax.axis_size("seq")
    batch_count = lax.axis_size("batch")
    gain_rows = gains.astype(jnp.float32)
    paired_weight_matrix = attention_input_weight[:, MODEL_WIDTH:]
    streams, segment = token_ids.shape
    slots = segment // 3 + 1
    place = lax.axis_index("seq")
    offset = place * segment
    group_tokens, group_mask = (
        lax.all_gather(token_ids, "seq", axis=1, tiled=True),
        lax.all_gather(loss_mask, "seq", axis=1, tiled=True),
    )
    row_length = group_tokens.shape[1]
    book_ends = jnp.cumsum(book_lengths, -1)
    group_pos = jnp.arange(row_length, dtype=jnp.int32)
    group_book = book_number(group_pos, book_ends)
    own_pos = offset + jnp.arange(segment, dtype=jnp.int32)
    own_book = book_number(own_pos, book_ends)
    next_book = book_number(group_pos + 1, book_ends)
    live_all = group_mask.astype(jnp.float32) * (next_book == group_book).astype(jnp.float32)
    member = (group_book[:, :, None] == jnp.arange(NBOOK, dtype=jnp.int32)[None, None, :]).astype(
        jnp.float32
    )
    book_counts = jnp.sum(member * live_all[:, :, None], 1)
    weight_all = live_all * jnp.sum(member / jnp.maximum(book_counts, 1.0)[:, None, :], -1)
    targets_all = jnp.concatenate([group_tokens[:, 1:], group_tokens[:, :1]], 1)
    owner_group, local_group = vocab_place(group_tokens, vocab_block, seq_count)
    table = lax.all_gather(table_local, "seq", axis=0, tiled=True)
    own_rows = lax.dynamic_slice_in_dim(
        owner_group * (batch_count * vocab_block) + local_group, offset, segment, 1
    )
    embedded = table[own_rows].astype(jnp.float32) * MODEL_WIDTH**0.5
    normed_one, unit_one, scale_one = norm_forward(embedded, gain_rows[:, 0])
    attention_input = normed_one.astype(jnp.bfloat16)
    projected = project(attention_input, attention_input_weight).astype(jnp.bfloat16)
    query = projected[..., :MODEL_WIDTH]
    pairs = projected[..., MODEL_WIDTH:]
    memory_pairs, tail_rows = passed_along((pairs, attention_input[:, segment - 2 :]), "seq", 1)
    first_cell = jnp.mod(2 - offset, 3)
    extended = jnp.concatenate(
        [tail_rows, attention_input, jnp.zeros((streams, 4, MODEL_WIDTH), jnp.bfloat16)], 1
    )
    memory_slot_rows = lax.dynamic_slice_in_dim(extended, first_cell, 3 * slots, 1).reshape(
        streams, slots, 3 * MODEL_WIDTH
    )
    compressed_memory = project(memory_slot_rows, w_compress).astype(jnp.bfloat16)
    comp_pairs = project(compressed_memory, paired_weight_matrix).astype(jnp.bfloat16)
    key_parts = [pairs, memory_pairs]
    book_parts = [own_book, book_number(own_pos - segment, book_ends)]
    pos_parts = [own_pos, own_pos - segment]
    for hop in (2, 3, 4):
        key_parts.append(passed_along(comp_pairs, "seq", hop))
        owner = place - hop
        last_pos = (
            owner * segment
            + jnp.mod(2 - owner * segment, 3)
            + 3 * jnp.arange(slots, dtype=jnp.int32)
        )
        last_book = book_number(last_pos, book_ends)
        usable = (owner >= 0) & (last_pos < owner * segment + segment)
        usable = usable[None, :] & (book_number(last_pos - 2, book_ends) == last_book)
        book_parts.append(jnp.where(usable, last_book, -2))
        pos_parts.append(jnp.full((slots,), -1, jnp.int32))
    key_side = jnp.concatenate(key_parts, 1)
    key_book = jnp.concatenate(book_parts, 1)
    key_positions = jnp.concatenate(pos_parts)
    allowed = (key_book[:, None, :] == own_book[:, :, None]) & (
        key_positions[None, None, :] <= own_pos[None, :, None]
    )
    value_heads = split_heads(key_side[..., MODEL_WIDTH:])
    scores = attention_scores(query, key_side, allowed)
    top_score = jnp.max(scores, -1, keepdims=True)
    log_total = top_score + jnp.log(jnp.sum(jnp.exp(scores - top_score), -1, keepdims=True))
    attn_probs = jnp.exp(scores - log_total)
    attention_result = jnp.einsum(
        "shqk,skhd->sqhd",
        attn_probs.astype(jnp.bfloat16),
        value_heads,
        preferred_element_type=jnp.float32,
    )
    attention_result = attention_result.reshape(streams, segment, MODEL_WIDTH).astype(jnp.bfloat16)
    residual = embedded + project(attention_result, attention_output_weight)
    normed_two, unit_two, scale_two = norm_forward(residual, gain_rows[:, 1])
    ffn_input = normed_two.astype(jnp.bfloat16)
    pre_act = project(ffn_input, w_ffn_in)
    activated, gelu_back = jax.vjp(jax.nn.gelu, pre_act)
    activated = activated.astype(jnp.bfloat16)
    output_rows = residual + project(activated, w_ffn_out)
    normed_three, unit_three, scale_three = norm_forward(output_rows, gain_rows[:, 2])
    final_rows = normed_three.astype(jnp.bfloat16)
    keep = segment // 2
    order_all = jnp.argsort(
        1 - group_mask.reshape(streams, seq_count, segment), axis=-1, stable=True
    )[..., :keep]
    order_all = order_all + (segment * jnp.arange(seq_count, dtype=jnp.int32))[None, :, None]
    order = lax.dynamic_index_in_dim(order_all, place, 1, keepdims=False) - offset
    flat_order = order_all.reshape(streams, -1)
    targets_picked = jnp.take_along_axis(targets_all, flat_order, 1)
    scale_picked = jnp.take_along_axis(weight_all, flat_order, 1)
    picked_rows = jnp.take_along_axis(final_rows, order[:, :, None], 1)
    own_targets = lax.dynamic_slice_in_dim(targets_picked, place * keep, keep, 1)
    own_scale = lax.dynamic_slice_in_dim(scale_picked, place * keep, keep, 1)
    target_owner, target_local = vocab_place(own_targets, vocab_block, seq_count)
    own_wanted = target_owner * (batch_count * vocab_block) + target_local
    head_block = 128

    def head_step(carry, inputs):
        grad_table, loss_sum = carry
        rows, wanted, scale_rows = inputs
        logits = jnp.einsum("nd,vd->nv", rows, table, preferred_element_type=jnp.float32)
        top_logit = jnp.max(logits, -1, keepdims=True)
        log_norm = top_logit + jnp.log(jnp.sum(jnp.exp(logits - top_logit), -1, keepdims=True))
        picked = jnp.take_along_axis(logits, wanted[:, None], 1)
        loss_sum = loss_sum + jnp.sum(scale_rows * (log_norm - picked)[:, 0])
        grad_logits = jnp.exp(logits - log_norm).at[jnp.arange(rows.shape[0]), wanted].add(-1.0)
        grad_logits = (scale_rows[:, None] * grad_logits).astype(jnp.bfloat16)
        grad_rows = jnp.einsum("nv,vd->nd", grad_logits, table, preferred_element_type=jnp.float32)
        grad_table = grad_table + jnp.einsum(
            "nv,nd->vd", grad_logits, rows, preferred_element_type=jnp.float32
        )
        return ((grad_table, loss_sum), grad_rows)

    start_carry = (jnp.zeros(table.shape, jnp.float32), jnp.float32(0.0))
    head_inputs = (
        picked_rows.reshape(-1, head_block, MODEL_WIDTH),
        own_wanted.reshape(-1, head_block),
        own_scale.reshape(-1, head_block),
    )
    (grad_table, loss_local), grad_picked = lax.scan(head_step, start_carry, head_inputs)
    grad_picked = grad_picked.reshape(streams, keep, MODEL_WIDTH)
    stream_index = jnp.arange(streams, dtype=jnp.int32)[:, None]
    grad_final = (
        jnp.zeros((streams, segment, MODEL_WIDTH), jnp.float32)
        .at[stream_index, order]
        .set(grad_picked)
    )
    grad_output_rows, grad_gain_three = norm_backward(
        grad_final, unit_three, scale_three, gain_rows[:, 2]
    )
    grad_branch = grad_output_rows.astype(jnp.bfloat16)
    grad_ffn_out = jnp.einsum(
        "snf,snd->fd", activated, grad_branch, preferred_element_type=jnp.float32
    )
    grad_act = jnp.einsum("snd,fd->snf", grad_branch, w_ffn_out, preferred_element_type=jnp.float32)
    grad_pre = gelu_back(grad_act)[0].astype(jnp.bfloat16)
    grad_ffn_in = jnp.einsum("snd,snf->df", ffn_input, grad_pre, preferred_element_type=jnp.float32)
    grad_norm_two = jnp.einsum(
        "snf,df->snd", grad_pre, w_ffn_in, preferred_element_type=jnp.float32
    )
    grad_res_two, grad_gain_two = norm_backward(grad_norm_two, unit_two, scale_two, gain_rows[:, 1])
    grad_residual = grad_output_rows + grad_res_two
    attention_branch_gradient = grad_residual.astype(jnp.bfloat16)
    grad_attn_out = jnp.einsum(
        "uvb,uvr->br",
        attention_result,
        attention_branch_gradient,
        preferred_element_type=jnp.float32,
    )
    grad_attended = jnp.einsum(
        "amj,qj->amq",
        attention_branch_gradient,
        attention_output_weight,
        preferred_element_type=jnp.float32,
    ).astype(jnp.bfloat16)
    scores = attention_scores(query, key_side, allowed)
    attn_probs = jnp.exp(scores - log_total)
    grad_heads = split_heads(grad_attended)
    grad_probs = jnp.einsum(
        "sqhd,skhd->shqk", grad_heads, value_heads, preferred_element_type=jnp.float32
    )
    grad_scores = attn_probs * (grad_probs - jnp.sum(attn_probs * grad_probs, -1, keepdims=True))
    grad_scores = (grad_scores * HEAD ** (-0.5)).astype(jnp.bfloat16)
    grad_query = jnp.einsum(
        "shqk,skhd->sqhd",
        grad_scores,
        split_heads(key_side[..., :MODEL_WIDTH]),
        preferred_element_type=jnp.float32,
    ).reshape(streams, segment, MODEL_WIDTH)
    grad_keys = jnp.einsum(
        "shqk,sqhd->skhd", grad_scores, split_heads(query), preferred_element_type=jnp.float32
    ).reshape(streams, -1, MODEL_WIDTH)
    grad_values = jnp.einsum(
        "shqk,sqhd->skhd",
        attn_probs.astype(jnp.bfloat16),
        grad_heads,
        preferred_element_type=jnp.float32,
    ).reshape(streams, -1, MODEL_WIDTH)
    grad_pairs = jnp.concatenate([grad_keys, grad_values], -1)
    received = jnp.zeros((streams, slots, 2 * MODEL_WIDTH), jnp.float32)
    for hop in (2, 3, 4):
        first_row = 2 * segment + (hop - 2) * slots
        received = received + passed_along(
            grad_pairs[:, first_row : first_row + slots].astype(jnp.bfloat16), "seq", -hop
        ).astype(jnp.float32)
    compressed_pairs_gradient = received.astype(jnp.bfloat16)
    grad_pairs_comp = jnp.einsum(
        "uvb,uvr->br",
        compressed_memory,
        compressed_pairs_gradient,
        preferred_element_type=jnp.float32,
    )
    grad_compressed = jnp.einsum(
        "amj,qj->amq",
        compressed_pairs_gradient,
        paired_weight_matrix,
        preferred_element_type=jnp.float32,
    ).astype(jnp.bfloat16)
    grad_compress = jnp.einsum(
        "snc,snd->cd", memory_slot_rows, grad_compressed, preferred_element_type=jnp.float32
    )
    grad_slots = jnp.einsum(
        "snd,cd->snc", grad_compressed, w_compress, preferred_element_type=jnp.float32
    ).reshape(streams, 3 * slots, MODEL_WIDTH)
    grad_extended = lax.dynamic_update_slice_in_dim(
        jnp.zeros((streams, segment + 6, MODEL_WIDTH), jnp.float32), grad_slots, first_cell, 1
    )
    back_memory, back_tail = (
        passed_along(grad_pairs[:, segment : 2 * segment].astype(jnp.bfloat16), "seq", -1).astype(
            jnp.float32
        ),
        passed_along(grad_extended[:, :2].astype(jnp.bfloat16), "seq", -1).astype(jnp.float32),
    )
    grad_own_pairs = (grad_pairs[:, :segment] + back_memory).astype(jnp.bfloat16)
    projected_gradient = jnp.concatenate([grad_query.astype(jnp.bfloat16), grad_own_pairs], -1)
    grad_attn_in = jnp.einsum(
        "uvb,uvr->br", attention_input, projected_gradient, preferred_element_type=jnp.float32
    )
    grad_attn_in = grad_attn_in + jnp.concatenate(
        [jnp.zeros((MODEL_WIDTH, MODEL_WIDTH), jnp.float32), grad_pairs_comp], 1
    )
    grad_input = (
        jnp.einsum(
            "amj,qj->amq",
            projected_gradient,
            attention_input_weight,
            preferred_element_type=jnp.float32,
        )
        + grad_extended[:, 2 : segment + 2]
    )
    grad_input = grad_input.at[:, segment - 2 :].add(back_tail)
    grad_embed, grad_gain_one = norm_backward(grad_input, unit_one, scale_one, gain_rows[:, 0])
    grad_scaled = (grad_embed + grad_residual) * MODEL_WIDTH**0.5
    grad_gains = jnp.stack([grad_gain_one, grad_gain_two, grad_gain_three], 1)
    grad_table = grad_table.at[own_rows.reshape(-1)].add(grad_scaled.reshape(-1, MODEL_WIDTH))
    grad_table = lax.psum_scatter(
        grad_table.astype(jnp.bfloat16), "seq", scatter_dimension=0, tiled=True
    ).astype(jnp.float32)
    grad_table = lax.psum_scatter(
        grad_table.astype(jnp.bfloat16), "batch", scatter_dimension=0, tiled=True
    ).astype(jnp.float32)
    loss_spread = jnp.full((batch_count * seq_count,), loss_local, jnp.float32)
    summed = (
        lax.psum_scatter(grad_attn_in, ("batch", "seq"), scatter_dimension=0, tiled=True),
        lax.psum_scatter(grad_attn_out, ("batch", "seq"), scatter_dimension=0, tiled=True),
        lax.psum_scatter(grad_compress, ("batch", "seq"), scatter_dimension=0, tiled=True),
        lax.psum_scatter(grad_ffn_in, ("batch", "seq"), scatter_dimension=0, tiled=True),
        lax.psum_scatter(grad_ffn_out, ("batch", "seq"), scatter_dimension=0, tiled=True),
        lax.psum_scatter(grad_gains, ("batch", "seq"), scatter_dimension=0, tiled=True),
        lax.psum_scatter(loss_spread, ("batch", "seq"), scatter_dimension=0, tiled=True),
    )
    grads = (grad_table,) + tuple(summed[:6])
    loss_total = summed[6][0]
    results = []
    for master, first, second, grad, rate in zip(masters, firsts, seconds, grads, STEP_RATES):
        results.extend(adam_update(master, first, second, grad, rate))
    return (loss_total,) + tuple(results)


def solution(mesh):
    placed = (
        P("batch", "seq"),
        P("batch", None),
        P("batch", "seq"),
        P(("batch", "seq"), None),
        P(("batch", "seq"), None),
        P(("batch", "seq"), None),
        P(("batch", "seq"), None),
        P(("batch", "seq"), None),
        P(("batch", "seq"), None),
        P(("batch", "seq"), None),
        P(("batch", "seq"), None),
        P(("batch", "seq"), None),
        P(("batch", "seq"), None),
        P(("batch", "seq"), None),
        P(("batch", "seq"), None),
        P(("batch", "seq"), None),
        P(("batch", "seq"), None),
        P(("batch", "seq"), None),
        P(("batch", "seq"), None),
        P(("batch", "seq"), None),
        P(("batch", "seq"), None),
        P(("batch", "seq"), None),
        P(("batch", "seq"), None),
        P(("batch", "seq"), None),
    )
    return jax.shard_map(
        per_device,
        mesh=mesh,
        in_specs=placed,
        out_specs=(
            P(),
            P(("batch", "seq"), None),
            P(("batch", "seq"), None),
            P(("batch", "seq"), None),
            P(("batch", "seq"), None),
            P(("batch", "seq"), None),
            P(("batch", "seq"), None),
            P(("batch", "seq"), None),
            P(("batch", "seq"), None),
            P(("batch", "seq"), None),
            P(("batch", "seq"), None),
            P(("batch", "seq"), None),
            P(("batch", "seq"), None),
            P(("batch", "seq"), None),
            P(("batch", "seq"), None),
            P(("batch", "seq"), None),
            P(("batch", "seq"), None),
            P(("batch", "seq"), None),
            P(("batch", "seq"), None),
            P(("batch", "seq"), None),
            P(("batch", "seq"), None),
            P(("batch", "seq"), None),
        ),
        check_vma=False,
    )
```

profile of v0, /device:TPU:0, one launch (start us, length us, event | category | flops | bytes accessed | tf_op | source)
XLA Modules:
  0.0 3088.5 jit_solution(2814494199850076136)
XLA Ops:
  23.6 137.5 %all-gather.9.cloned.1.call-done = bf16[4000,1024]{1,0:T(8,128)(2,1)} async-done(((bf16[1000,1024]{1,0:T(8,128)(2,1)}), bf16[4000,1024]{1,0:T(8,128)(2,1)}) %all-gather.9.cloned.1.call-update) | async-done | bytes 8192016 | tf_op jit(solution)/shard_map/all_gather | solution.py:152
  175.6 37.8 %all-gather = bf16[32,32,3]{1,2,0:T(4,128)(2,1)S(1)} all-gather(bf16[1,32,3]{1,2,0:T(4,128)(2,1)S(1)} %convert_bitcast_fusion), channel_id=1, replica_groups=mesh['batch'=4,'seq'=8] {'batch','seq'}, dimensions={0}, use_global_device_ids=true | all-gather | bytes 6336 | tf_op jit(solution)/shard_map/all_gather | solution.py:150
  231.9 226.0 %all-gather.11.cloned.1.call-done = bf16[32000,1024]{1,0:T(8,128)(2,1)} async-done(((bf16[4000,1024]{1,0:T(8,128)(2,1)}), bf16[32000,1024]{1,0:T(8,128)(2,1)}) %all-gather.11.cloned.1.call-update) | async-done | bytes 65536016 | tf_op jit(solution)/shard_map/all_gather | solution.py:181
  462.8 68.4 %all-gather.13.cloned.1.call-done = bf16[1024,3072]{1,0:T(8,128)(2,1)} async-done(((bf16[32,3072]{1,0:T(8,128)(2,1)}), bf16[1024,3072]{1,0:T(8,128)(2,1)}) %all-gather.13.cloned.1.call-update) | async-done | bytes 6291472 | tf_op jit(solution)/shard_map/all_gather | solution.py:145
  561.9 43.2 %all-gather.15.cloned.1.call-done = bf16[3072,1024]{1,0:T(8,128)(2,1)} async-done(((bf16[96,1024]{1,0:T(8,128)(2,1)}), bf16[3072,1024]{1,0:T(8,128)(2,1)}) %all-gather.15.cloned.1.call-update) | async-done | bytes 6291472 | tf_op jit(solution)/shard_map/all_gather | solution.py:147
  787.0 57.8 %all-gather.21.cloned.1.call-done = bf16[4096,1024]{1,0:T(8,128)(2,1)} async-done(((bf16[128,1024]{1,0:T(8,128)(2,1)}), bf16[4096,1024]{1,0:T(8,128)(2,1)}) %all-gather.21.cloned.1.call-update) | async-done | bytes 8388624 | tf_op jit(solution)/shard_map/all_gather | solution.py:149
  858.2 340.1 %while.16 = (s32[]{:T(128)}, f32[32000,1024]{1,0:T(8,128)}, f32[]{:T(128)}, f32[2,128,1024]{2,1,0:T(8,128)}, f32[2,128]{1,0:T(2,128)S(1)}, /*index=5*/bf16[2,128...) while((s32[]{:T(128)}, f32[32000,1024]{1,0:T(8,128)}, ...), condition=%wide.region_27.28_spmd.clone, body=%wide.region_22.27_spmd.clone.sunk | while | flops 25264132096 | bytes 492587680 | solution.py:282
  858.3 33.7 %fusion.215 = (f32[128]{0:T(128)S(1)}, f32[128,32000]{1,0:T(8,128)}) fusion(bf16[32000,1024]{1,0:T(8,128)(2,1)} %get-tuple-element.292, bf16[2,128,1024]{2,1,0:T(8,128)(2,1)S(1)} %get-tuple-element.291, s32[]{:T(128)} %get-tuple-element.275), kind=kOutput, calls=%fused_computation.320.clone.1 | convolution fusion | flops 8392704000 | bytes 82182656 | tf_op jit(solution)/shard_map/while/body/eval_jaxpr/nd,vd->nv/dot_general | solution.py:263
  930.4 48.0 %select_add_fusion.2 = f32[32000,1024]{1,0:T(8,128)} fusion(f32[32000,1024]{1,0:T(8,128)} %get-tuple-element.276, pred[]{:T(512)S(6)} %compare.37, bf16[2,128,1024]{2,1,0:T(8,128)(2,1)S(1)} %get-tuple-element.291, s32[]{:T(128)} %get-tuple-element.275, f32[128,32000]{1,0:T(8,128)} %scatter_fusion, f32[128]{0:T(128)S(1)} %fusion.217), kind=kOutput, calls=%fused_computation.8.clone.3 | convolution fusion | flops 8462336000 | bytes 278790656 | tf_op jit(solution)/shard_map/while/body/eval_jaxpr/nv,nd->vd/dot_general | solution.py:271
  1007.2 33.5 %fusion.215 = (f32[128]{0:T(128)S(1)}, f32[128,32000]{1,0:T(8,128)}) fusion(bf16[32000,1024]{1,0:T(8,128)(2,1)} %get-tuple-element.292, bf16[2,128,1024]{2,1,0:T(8,128)(2,1)S(1)} %get-tuple-element.291, s32[]{:T(128)} %get-tuple-element.275), kind=kOutput, calls=%fused_computation.320.clone.1 | convolution fusion | flops 8392704000 | bytes 82182656 | tf_op jit(solution)/shard_map/while/body/eval_jaxpr/nd,vd->nv/dot_general | solution.py:263
  1079.2 90.5 %select_add_fusion.2 = f32[32000,1024]{1,0:T(8,128)} fusion(f32[32000,1024]{1,0:T(8,128)} %get-tuple-element.276, pred[]{:T(512)S(6)} %compare.37, bf16[2,128,1024]{2,1,0:T(8,128)(2,1)S(1)} %get-tuple-element.291, s32[]{:T(128)} %get-tuple-element.275, f32[128,32000]{1,0:T(8,128)} %scatter_fusion, f32[128]{0:T(128)S(1)} %fusion.217), kind=kOutput, calls=%fused_computation.8.clone.3 | convolution fusion | flops 8462336000 | bytes 278790656 | tf_op jit(solution)/shard_map/while/body/eval_jaxpr/nv,nd->vd/dot_general | solution.py:271
  1266.2 40.4 %fusion.32 = f32[1,1537,8,128]{3,1,2,0:T(8,128)} fusion(f32[8,512,1537]{1,2,0:T(8,128)} %fusion.46, f32[8,512,1537]{1,2,0:T(8,128)} %get-tuple-element.191, f32[8,512]{1,0:T(8,128)S(1)} %copy-done.42, bf16[512,8,128]{2,1,0:T(8,128)(2,1)S(1)} %bitcast.272), kind=kOutput, calls=%fused_computation.67 | convolution fusion | flops 1655735808 | bytes 57724928 | tf_op jit(solution)/shard_map/shqk,sqhd->skhd/dot_general | solution.py:332
  1341.9 41.9 %fusion.88 = bf16[8,128,512]{2,1,0:T(8,128)(2,1)} fusion(f32[8,512,1537]{1,2,0:T(8,128)} %fusion.46, f32[8,512,1537]{1,2,0:T(8,128)} %get-tuple-element.191, f32[8,512]{1,0:T(8,128)S(1)} %copy-done.42, bf16[1537,8,128]{2,1,0:T(8,128)(2,1)} %copy-done.15), kind=kOutput, calls=%fused_computation.134 | convolution fusion | flops 1656260096 | bytes 54577152 | tf_op jit(solution)/shard_map/shqk,skhd->sqhd/dot_general | solution.py:326
  1423.2 74.7 %scatter_fusion.1 = f32[32000,1024]{1,0:T(8,128)} fusion(f32[32000,1024]{1,0:T(8,128)} %get-tuple-element.81, s32[512]{0:T(512)S(1)} %bitcast.299, f32[512,1024]{1,0:T(8,128)} %fusion.75), kind=kCustom, calls=%fused_computation.7 | custom fusion | flops 524288 | bytes 6293504 | tf_op jit(solution)/shard_map/scatter-add | solution.py:397
  1497.9 62.2 %convert_element_type.393 = bf16[32000,1024]{1,0:T(8,128)(2,1)} convert(f32[32000,1024]{1,0:T(8,128)} %scatter_fusion.1) | non-fusion elementwise | flops 32768000 | bytes 196608000 | tf_op jit(solution)/shard_map/convert_element_type | solution.py:399
  1619.3 340.8 %reduce-scatter.11.cloned.1.call-done = bf16[4000,1024]{1,0:T(8,128)(2,1)} async-done(((bf16[32000,1024]{1,0:T(8,128)(2,1)}), bf16[4000,1024]{1,0:T(8,128)(2,1)}) %reduce-scatter.11.cloned.1.call-update) | async-done | bytes 8192016 | tf_op jit(solution)/shard_map/reduce_scatter | solution.py:398
  1960.2 39.7 %all-reduce.2 = f32[32]{0:T(128)S(1)} all-reduce(f32[32]{0:T(128)S(1)} %broadcast_in_dim.169), channel_id=2, replica_groups=mesh['batch'=4,'seq'=8] {'batch','seq'}, use_global_device_ids=true, to_apply=%region_28.29.clone | all-reduce | flops 32 | bytes 256
  2000.5 96.3 %reduce-scatter.25.cloned.1.call-done = f32[32,3]{1,0:T(8,128)} async-done(((f32[1024,3]{1,0:T(8,128)}), f32[32,3]{1,0:T(8,128)}) %reduce-scatter.25.cloned.1.call-update) | async-done | bytes 400
  2098.2 137.6 %reduce-scatter.17.cloned.1.call-done = f32[32,1024]{1,0:T(8,128)} async-done(((f32[1024,1024]{1,0:T(8,128)}), f32[32,1024]{1,0:T(8,128)}) %reduce-scatter.17.cloned.1.call-update) | async-done | bytes 131088 | tf_op jit(solution)/shard_map/reduce_scatter | solution.py:407
  2237.5 156.0 %reduce-scatter.19.cloned.1.call-done = f32[96,1024]{1,0:T(8,128)} async-done(((f32[3072,1024]{1,0:T(8,128)}), f32[96,1024]{1,0:T(8,128)}) %reduce-scatter.19.cloned.1.call-update) | async-done | bytes 393232 | tf_op jit(solution)/shard_map/reduce_scatter | solution.py:408
  2396.0 159.4 %reduce-scatter.15.cloned.1.call-done = f32[32,3072]{1,0:T(8,128)} async-done(((f32[1024,3072]{1,0:T(8,128)}), f32[32,3072]{1,0:T(8,128)}) %reduce-scatter.15.cloned.1.call-update) | async-done | bytes 393232 | tf_op jit(solution)/shard_map/reduce_scatter | solution.py:406
  2557.8 181.7 %reduce-scatter.23.cloned.1.call-done = f32[128,1024]{1,0:T(8,128)} async-done(((f32[4096,1024]{1,0:T(8,128)}), f32[128,1024]{1,0:T(8,128)}) %reduce-scatter.23.cloned.1.call-update) | async-done | bytes 524304 | tf_op jit(solution)/shard_map/reduce_scatter | solution.py:410
  2742.0 184.4 %reduce-scatter.21.cloned.1.call-done = f32[32,4096]{1,0:T(8,128)} async-done(((f32[1024,4096]{1,0:T(8,128)}), f32[32,4096]{1,0:T(8,128)}) %reduce-scatter.21.cloned.1.call-update) | async-done | bytes 524304 | tf_op jit(solution)/shard_map/reduce_scatter | solution.py:409
  2929.0 142.6 %reduce-scatter.13.cloned.1.call-done = bf16[1000,1024]{1,0:T(8,128)(2,1)} async-done(((bf16[4000,1024]{1,0:T(8,128)(2,1)}), bf16[1000,1024]{1,0:T(8,128)(2,1)}) %reduce-scatter.13.cloned.1.call-update) | async-done | bytes 2048016 | tf_op jit(solution)/shard_map/reduce_scatter | solution.py:401
  (405 shorter events, 635.9 us)
Async XLA Ops:
  8.0 153.1 %all-gather.9.cloned.1.call-start = ((), (), s32[]{:S(2)}) async-start(), calls=%async_computation.8 | async-start | bytes 10240000 | tf_op jit(solution)/shard_map/all_gather | solution.py:152
  23.6 434.2 %all-gather.11.cloned.1.call-start = ((), (), s32[]{:S(2)}) async-start(), calls=%async_computation.9 | async-start | bytes 73728000 | tf_op jit(solution)/shard_map/all_gather | solution.py:181
  161.2 370.0 %all-gather.13.cloned.1.call-start = ((), (), s32[]{:S(2)}) async-start(), calls=%async_computation.10 | async-start | bytes 6488064 | tf_op jit(solution)/shard_map/all_gather | solution.py:145
  162.9 442.2 %all-gather.15.cloned.1.call-start = ((), (), s32[]{:S(2)}) async-start(), calls=%async_computation.11 | async-start | bytes 6488064 | tf_op jit(solution)/shard_map/all_gather | solution.py:147
  163.7 567.5 %all-gather.17.cloned.1.call-start = ((), (), s32[]{:S(2)}) async-start(), calls=%async_computation.12 | async-start | bytes 2162688 | tf_op jit(solution)/shard_map/all_gather | solution.py:146
  164.4 600.5 %all-gather.19.cloned.1.call-start = ((), (), s32[]{:S(2)}) async-start(), calls=%async_computation.13 | async-start | bytes 8650752 | tf_op jit(solution)/shard_map/all_gather | solution.py:148
  165.2 679.6 %all-gather.21.cloned.1.call-start = ((), (), s32[]{:S(2)}) async-start(), calls=%async_computation.14 | async-start | bytes 8650752 | tf_op jit(solution)/shard_map/all_gather | solution.py:149
  166.0 1794.0 %reduce-scatter.11.cloned.1.call-start = ((), (), s32[]{:S(2)}) async-start(), calls=%async_computation.15 | async-start | bytes 73728000 | tf_op jit(solution)/shard_map/reduce_scatter | solution.py:398
  538.1 119.5 %collective-permute-start = (bf16[1,512,2048]{2,1,0:T(8,128)(2,1)S(1)}, bf16[1,512,2048]{2,1,0:T(8,128)(2,1)}, u32[]{:S(2)}, u32[]{:S(2)}) collective-permute-start(bf16[1,512,2048]{2,1,0:T(8,128)(2,1)S(1)} %slice.128), channel_id=1, source_target_pairs={{0,1},{1,2},{2,3},{3,4},{4,5},{5,6},{6,7},{8,9},{9,10},{10,11},{11... | collective-permute-start | bytes 6291464 | tf_op jit(solution)/shard_map/ppermute | solution.py:25
  543.1 13.9 collective-permute-start.1
  612.8 19.6 collective-permute-start.2
  617.0 23.1 collective-permute-start.3
  620.0 37.5 %collective-permute-start.4 = (bf16[1,171,2048]{2,1,0:T(8,128)(2,1)S(1)}, bf16[1,171,2048]{2,1,0:T(8,128)(2,1)}, u32[]{:S(2)}, u32[]{:S(2)}) collective-permute-start(bf16[1,171,2048]{2,1,0:T(8,128)(2,1)S(1)} %fusion.54), channel_id=1, source_target_pairs={{0,4},{1,5},{2,6},{3,7},{8,12},{9,13},{10,14},{11,15},{16,20},{17,... | collective-permute-start | bytes 2101256 | tf_op jit(solution)/shard_map/ppermute | solution.py:25
  1333.6 76.4 %collective-permute-start.5 = (bf16[1,512,2048]{2,1,0:T(8,128)(2,1)}, bf16[1,512,2048]{2,1,0:T(8,128)(2,1)}, u32[]{:S(2)}, u32[]{:S(2)}) collective-permute-start(bf16[1,512,2048]{2,1,0:T(8,128)(2,1)} %slice.141), channel_id=1, source_target_pairs={{1,0},{2,1},{3,2},{4,3},{5,4},{6,5},{7,6},{9,8},{10,9},{11,10},{12... | collective-permute-start | bytes 6291464 | tf_op jit(solution)/shard_map/ppermute | solution.py:25
  1338.0 47.2 %collective-permute-start.6 = (bf16[1,171,2048]{2,1,0:T(8,128)(2,1)}, bf16[1,171,2048]{2,1,0:T(8,128)(2,1)}, u32[]{:S(2)}, u32[]{:S(2)}) collective-permute-start(bf16[1,171,2048]{2,1,0:T(8,128)(2,1)} %get-tuple-element.180), channel_id=1, source_target_pairs={{2,0},{3,1},{4,2},{5,3},{6,4},{7,5},{10,8},{11,9},{12,10},{13,11},... | collective-permute-start | bytes 2101256 | tf_op jit(solution)/shard_map/ppermute | solution.py:25
  1339.3 46.0 %collective-permute-start.7 = (bf16[1,171,2048]{2,1,0:T(8,128)(2,1)}, bf16[1,171,2048]{2,1,0:T(8,128)(2,1)}, u32[]{:S(2)}, u32[]{:S(2)}) collective-permute-start(bf16[1,171,2048]{2,1,0:T(8,128)(2,1)} %get-tuple-element.182), channel_id=1, source_target_pairs={{3,0},{4,1},{5,2},{6,3},{7,4},{11,8},{12,9},{13,10},{14,11},{15,12... | collective-permute-start | bytes 2101256 | tf_op jit(solution)/shard_map/ppermute | solution.py:25
  1340.6 44.7 %collective-permute-start.8 = (bf16[1,171,2048]{2,1,0:T(8,128)(2,1)}, bf16[1,171,2048]{2,1,0:T(8,128)(2,1)}, u32[]{:S(2)}, u32[]{:S(2)}) collective-permute-start(bf16[1,171,2048]{2,1,0:T(8,128)(2,1)} %get-tuple-element.181), channel_id=1, source_target_pairs={{4,0},{5,1},{6,2},{7,3},{12,8},{13,9},{14,10},{15,11},{20,16},{21,... | collective-permute-start | bytes 2101256 | tf_op jit(solution)/shard_map/ppermute | solution.py:25
  1560.1 536.7 %reduce-scatter.25.cloned.1.call-start = ((), (), s32[]{:S(2)}) async-start(), calls=%async_computation.22 | async-start | bytes 540672
  1561.9 674.0 %reduce-scatter.17.cloned.1.call-start = ((), (), s32[]{:S(2)}) async-start(), calls=%async_computation.18 | async-start | bytes 4325376 | tf_op jit(solution)/shard_map/reduce_scatter | solution.py:407
  1565.3 828.3 %reduce-scatter.19.cloned.1.call-start = ((), (), s32[]{:S(2)}) async-start(), calls=%async_computation.19 | async-start | bytes 12976128 | tf_op jit(solution)/shard_map/reduce_scatter | solution.py:408
  1572.8 982.6 %reduce-scatter.15.cloned.1.call-start = ((), (), s32[]{:S(2)}) async-start(), calls=%async_computation.17 | async-start | bytes 12976128 | tf_op jit(solution)/shard_map/reduce_scatter | solution.py:406
  1583.5 1156.0 %reduce-scatter.23.cloned.1.call-start = ((), (), s32[]{:S(2)}) async-start(), calls=%async_computation.21 | async-start | bytes 17301504 | tf_op jit(solution)/shard_map/reduce_scatter | solution.py:410
  1603.3 1323.1 %reduce-scatter.21.cloned.1.call-start = ((), (), s32[]{:S(2)}) async-start(), calls=%async_computation.20 | async-start | bytes 17301504 | tf_op jit(solution)/shard_map/reduce_scatter | solution.py:409
  1619.2 1452.4 %reduce-scatter.13.cloned.1.call-start = ((), (), s32[]{:S(2)}) async-start(), calls=%async_computation.16 | async-start | bytes 10240000 | tf_op jit(solution)/shard_map/reduce_scatter | solution.py:401
  (83 other events, 10091.5 us)
Sparse Core Ops, SparseCore 0:
  12.0 149.1 all-gather.8
  163.2 294.5 all-gather.10
  461.7 69.4 all-gather.12
  534.9 70.1 all-gather.14
  608.8 76.0 all-gather.16
  688.5 76.2 all-gather.18
  768.7 76.0 all-gather.20
  1560.2 399.7 reduce-scatter.10
  1963.0 133.7 reduce-scatter.24
  2098.9 136.8 reduce-scatter.16
  2241.9 151.6 reduce-scatter.18
  2400.5 154.8 reduce-scatter.14
  2557.7 181.7 reduce-scatter.22
  2741.7 184.6 reduce-scatter.20
  2928.6 142.9 reduce-scatter.12
Sparse Core Ops, SparseCore 1:
  23.7 5.5 sort.21.cloned.1.call-done
  (1 shorter events, 0.0 us)
where the time goes:
time: 3100 us; the launch traced here: 3090 us
  waiting for transfers between devices  1990 us (64%)
  matrix products  538 us (17%)
  other arithmetic  279 us (9%)
  local copies, waits for them, and re-layouts  139 us (4%)
  blocking collectives  96.7 us (3%)
    reduce_scatter x1, waiting for transfers between devices, per_device(): lax.psum_scatter(grad_table.astype(jnp.bfloat16), 'seq', scatter_dimensio...  341 us
    all_gather x1, waiting for transfers between devices, per_device(): table = lax.all_gather(table_local, 'seq', axis=0, tiled=True)  226 us
    reduce_scatter x1, waiting for transfers between devices, per_device(): lax.psum_scatter(grad_ffn_in, ('batch', 'seq'), scatter_dimension=0, tile...  184 us
    reduce_scatter x1, waiting for transfers between devices, per_device(): lax.psum_scatter(grad_ffn_out, ('batch', 'seq'), scatter_dimension=0, til...  182 us
    reduce_scatter x1, waiting for transfers between devices, per_device(): lax.psum_scatter(grad_attn_in, ('batch', 'seq'), scatter_dimension=0, til...  159 us
    reduce_scatter x1, waiting for transfers between devices, per_device(): lax.psum_scatter(grad_compress, ('batch', 'seq'), scatter_dimension=0, ti...  156 us
    reduce_scatter x1, waiting for transfers between devices, per_device(): lax.psum_scatter(grad_table.astype(jnp.bfloat16), 'batch', scatter_dimens...  143 us
    dot_general x2, matrix products, head_step(): jnp.einsum('nv,nd->vd', grad_logits, rows, preferred_element_type=jnp.flo...  138 us
  transfers between devices with their start and end apart: 25, of which 17 were waited for; matrix products, arithmetic and copies ran while one was open for 10% of the time, Pallas kernels for 0%

commit v1 on v0

v1 whole, which is shorter than its diff:
```python
import jax
import jax.numpy as jnp
from jax import lax
from jax.sharding import Mesh
from jax.sharding import PartitionSpec as P

MODEL_WIDTH = 1024
HEADS = 8
HEAD = 128
NBOOK = 8
STEP = 5

EPSILON = 1e-05
NEGATIVE = -1e30
BETA_ONE = 0.9
BETA_TWO = 0.95
ADAM_EPSILON = 1e-08
WEIGHT_DECAY = 0.1
STEP_RATES = (0.06, 0.03, 0.4, 0.02, 0.03, 0.04, 0.5)

SEQ = ("y", "x", "core")
PLANE = ("y", "x")
SHARE = ("batch", "core")
ALL = ("batch", "y", "x", "core")
BF16 = jnp.bfloat16
F32 = jnp.float32


def passed_along(value, steps):
    count = lax.axis_size(SEQ)
    initial, last = (max(0, -steps), min(count, count - steps))
    return lax.ppermute(value, SEQ, [(source, source + steps) for source in range(initial, last)])


def norm_forward(values, gain):
    center = values - jnp.mean(values, -1, keepdims=True)
    scaler = lax.rsqrt(jnp.mean(center * center, -1, keepdims=True) + EPSILON)
    unit_rows = center * scaler
    return (unit_rows * gain, unit_rows, scaler)


def norm_backward(grad_out, unit_rows, scaler, gain):
    scaled = grad_out * gain
    grad_gain = jnp.sum(grad_out * unit_rows, axis=0)
    grad_in = scaler * (
        scaled
        - jnp.mean(scaled, -1, keepdims=True)
        - unit_rows * jnp.mean(scaled * unit_rows, -1, keepdims=True)
    )
    return (grad_in, grad_gain)


def book_number(positions, book_ends):
    inside = jnp.sum((positions[:, None] >= book_ends[None, :]).astype(jnp.int32), -1)
    return jnp.where(positions < 0, -1, inside)


def matmul(left, right):
    return jnp.dot(left, right, preferred_element_type=F32)


def matmul_nt(left, right):
    return lax.dot_general(left, right, (((1,), (1,)), ((), ())), preferred_element_type=F32)


def matmul_tn(left, right):
    return lax.dot_general(left, right, (((0,), (0,)), ((), ())), preferred_element_type=F32)


def split_heads(rows):
    return rows.reshape(rows.shape[0], HEADS, HEAD)


def attention_scores(query, keys, allowed):
    scores = jnp.einsum(
        "qhd,khd->hqk", split_heads(query), split_heads(keys), preferred_element_type=F32
    ) * HEAD ** (-0.5)
    return jnp.where(allowed[None], scores, NEGATIVE)


def adam_update(master, first, second, grad, rate):
    new_first = BETA_ONE * first + (1.0 - BETA_ONE) * grad
    new_second = BETA_TWO * second + (1.0 - BETA_TWO) * grad * grad
    first_hat = new_first / (1.0 - BETA_ONE**STEP)
    second_hat = new_second / (1.0 - BETA_TWO**STEP)
    new_master = master - rate * (
        first_hat / (jnp.sqrt(second_hat) + ADAM_EPSILON) + WEIGHT_DECAY * master
    )
    return [new_first, new_second, new_master]


def bf16_parts(values):
    high = values.astype(BF16)
    rest = values - high.astype(F32)
    middle = rest.astype(BF16)
    low = (rest - middle.astype(F32)).astype(BF16)
    return high, middle, low


def per_device(token_ids, book_lengths, loss_mask, *state):
    masters, firsts, seconds = state[:7], state[7:14], state[14:]
    table_master, attn_in_m, attn_out_m, compress_m, ffn_in_m, ffn_out_m, gains_m = masters
    vocab_block = table_master.shape[0]
    batch_count = lax.axis_size("batch")
    seq_count = lax.axis_size(SEQ)
    plane_count = seq_count // 2
    share_count = batch_count * 2
    device_count = batch_count * seq_count
    segment = token_ids.shape[1]
    slots = segment // 3 + 1
    keep = segment // 2
    place = lax.axis_index(SEQ)
    offset = place * segment
    share_place = lax.axis_index(SHARE)
    width = MODEL_WIDTH

    own_tokens = token_ids.reshape(segment)
    share_tokens = lax.all_gather(own_tokens, SHARE, axis=0, tiled=True)
    table = lax.all_gather(table_master.astype(BF16), PLANE, axis=0, tiled=True)

    def vocab_place(tokens):
        block = tokens // vocab_block
        seq_index = block % seq_count
        owner = block // seq_count * 2 + seq_index % 2
        return owner, seq_index // 2 * vocab_block + tokens % vocab_block

    share_owner, share_local = vocab_place(share_tokens)
    share_row = jnp.where(share_owner == share_place, share_local, -1)
    looked = jnp.where(
        (share_row >= 0)[:, None], table[jnp.maximum(share_row, 0)], jnp.zeros((), BF16)
    )
    token_rows = lax.psum_scatter(looked, SHARE, scatter_dimension=0, tiled=True)

    rows_in = attn_in_m.size // width
    rows_out = attn_out_m.size // width
    rows_comp = compress_m.size // width
    rows_ffn = ffn_in_m.size // width
    rows_ffn_out = ffn_out_m.size // width
    gain_count = gains_m.size
    gain_block = jnp.zeros((16, width), BF16).at[0, :gain_count].set(
        gains_m.astype(BF16).reshape(-1)
    )
    mixer_block = jnp.concatenate(
        [
            attn_in_m.astype(BF16).reshape(rows_in, width),
            compress_m.astype(BF16),
            attn_out_m.astype(BF16),
            gain_block,
        ],
        0,
    )
    ffn_block = jnp.concatenate(
        [ffn_in_m.astype(BF16).reshape(rows_ffn, width), ffn_out_m.astype(BF16)], 0
    )
    mixer_all = lax.all_gather(mixer_block, ALL, axis=0, tiled=False)
    ffn_all = lax.all_gather(ffn_block, ALL, axis=0, tiled=False)
    at = 0
    w_in = mixer_all[:, at : at + rows_in].reshape(width, 3 * width)
    at += rows_in
    w_compress = mixer_all[:, at : at + rows_comp].reshape(3 * width, width)
    at += rows_comp
    w_out = mixer_all[:, at : at + rows_out].reshape(width, width)
    at += rows_out
    gains = mixer_all[:, at, :gain_count].reshape(width, 3).astype(F32)
    w_ffn_in = ffn_all[:, :rows_ffn].reshape(width, -1)
    w_ffn_out = ffn_all[:, rows_ffn:].reshape(-1, width)
    w_pairs = w_in[:, width:]

    book_ends = jnp.cumsum(book_lengths.reshape(-1))
    own_pos = offset + jnp.arange(segment, dtype=jnp.int32)
    own_book = book_number(own_pos, book_ends)
    next_book = book_number(own_pos + 1, book_ends)
    own_mask = loss_mask.reshape(segment)
    live = own_mask.astype(F32) * (next_book == own_book).astype(F32)
    member = (own_book[:, None] == jnp.arange(NBOOK, dtype=jnp.int32)[None, :]).astype(F32)
    book_counts = lax.psum(jnp.sum(member * live[:, None], 0), SEQ)
    weight = live * jnp.sum(member / jnp.maximum(book_counts, 1.0)[None, :], -1)
    following = passed_along(own_tokens[:1], -1)
    targets = jnp.concatenate([own_tokens[1:], following])
    rank = jnp.cumsum(own_mask) - 1
    chosen = (rank[None, :] == jnp.arange(keep, dtype=jnp.int32)[:, None]) & (
        own_mask[None, :] > 0
    )
    picked_targets = jnp.sum(jnp.where(chosen, targets[None, :], 0), 1)
    picked_weight = jnp.sum(jnp.where(chosen, weight[None, :], 0.0), 1)

    embedded = token_rows.astype(F32) * width**0.5
    normed_one, unit_one, scale_one = norm_forward(embedded, gains[:, 0])
    attention_input = normed_one.astype(BF16)
    projected = matmul(attention_input, w_in).astype(BF16)
    query = projected[:, :width]
    pairs = projected[:, width:]
    memory_pairs = passed_along(pairs, 1)
    tail_rows = passed_along(attention_input[segment - 2 :], 1)
    first_cell = jnp.mod(2 - offset, 3)
    extended = jnp.concatenate([tail_rows, attention_input, jnp.zeros((4, width), BF16)], 0)
    slot_rows = lax.dynamic_slice_in_dim(extended, first_cell, 3 * slots, 0).reshape(
        slots, 3 * width
    )
    compressed = matmul(slot_rows, w_compress).astype(BF16)
    comp_pairs = matmul(compressed, w_pairs).astype(BF16)
    key_parts = [pairs, memory_pairs]
    book_parts = [own_book, book_number(own_pos - segment, book_ends)]
    pos_parts = [own_pos, own_pos - segment]
    for hop in (2, 3, 4):
        key_parts.append(passed_along(comp_pairs, hop))
        owner = place - hop
        last_pos = (
            owner * segment
            + jnp.mod(2 - owner * segment, 3)
            + 3 * jnp.arange(slots, dtype=jnp.int32)
        )
        last_book = book_number(last_pos, book_ends)
        usable = (owner >= 0) & (last_pos < owner * segment + segment)
        usable = usable & (book_number(last_pos - 2, book_ends) == last_book)
        book_parts.append(jnp.where(usable, last_book, -2))
        pos_parts.append(jnp.full((slots,), -1, jnp.int32))
    key_side = jnp.concatenate(key_parts, 0)
    key_book = jnp.concatenate(book_parts)
    key_pos = jnp.concatenate(pos_parts)
    allowed = (key_book[None, :] == own_book[:, None]) & (key_pos[None, :] <= own_pos[:, None])
    value_heads = split_heads(key_side[:, width:])
    scores = attention_scores(query, key_side[:, :width], allowed)
    top_score = jnp.max(scores, -1, keepdims=True)
    log_total = top_score + jnp.log(jnp.sum(jnp.exp(scores - top_score), -1, keepdims=True))
    attn_probs = jnp.exp(scores - log_total)
    attended = jnp.einsum(
        "hqk,khd->qhd", attn_probs.astype(BF16), value_heads, preferred_element_type=F32
    )
    attended = attended.reshape(segment, width).astype(BF16)
    residual = embedded + matmul(attended, w_out)

    normed_two, unit_two, scale_two = norm_forward(residual, gains[:, 1])
    ffn_input = normed_two.astype(BF16)
    pre_act = matmul(ffn_input, w_ffn_in)
    activated, gelu_back = jax.vjp(jax.nn.gelu, pre_act)
    activated = activated.astype(BF16)
    output_rows = residual + matmul(activated, w_ffn_out)
    normed_three, unit_three, scale_three = norm_forward(output_rows, gains[:, 2])
    final_rows = normed_three.astype(BF16)

    chosen_bf16 = chosen.astype(BF16)
    picked_rows = matmul(chosen_bf16, final_rows).astype(BF16)
    high, middle, low = bf16_parts(picked_weight)
    side = jnp.concatenate(
        [
            (picked_targets // 256).astype(BF16),
            (picked_targets % 256).astype(BF16),
            high,
            middle,
            low,
        ]
    )
    side_rows = jnp.zeros((16 * width,), BF16).at[: 5 * keep].set(side).reshape(16, width)
    head_all = lax.all_gather(
        jnp.concatenate([picked_rows, side_rows], 0), SHARE, axis=0, tiled=False
    )
    rows = head_all[:, :keep].reshape(share_count * keep, width)
    side_all = head_all[:, keep:].reshape(share_count, 16 * width)[:, : 5 * keep]
    side_all = side_all.reshape(share_count, 5, keep).astype(F32)
    wanted = (side_all[:, 0] * 256.0 + side_all[:, 1]).astype(jnp.int32).reshape(-1)
    row_weight = (side_all[:, 2] + side_all[:, 3] + side_all[:, 4]).reshape(-1)
    wanted_owner, wanted_local = vocab_place(wanted)
    wanted_row = jnp.where(wanted_owner == share_place, wanted_local, -1)
    logits = matmul_nt(rows, table)
    top_logit = jnp.max(logits, -1)
    total = jnp.sum(jnp.exp(logits - top_logit[:, None]), -1)
    stats = lax.all_gather(jnp.stack([top_logit, total]), SHARE, axis=0, tiled=False)
    top_all = jnp.max(stats[:, 0], 0)
    log_norm = top_all + jnp.log(jnp.sum(stats[:, 1] * jnp.exp(stats[:, 0] - top_all[None]), 0))
    hit = wanted_row[:, None] == jnp.arange(logits.shape[1], dtype=jnp.int32)[None, :]
    target_logit = jnp.sum(jnp.where(hit, logits, 0.0), -1)
    mine = (jnp.arange(share_count * keep) // keep == share_place).astype(F32)
    loss_local = jnp.sum(row_weight * (mine * log_norm - target_logit))
    grad_logits = row_weight[:, None] * (
        jnp.exp(logits - log_norm[:, None]) - hit.astype(F32)
    )
    grad_logits = grad_logits.astype(BF16)
    grad_rows = matmul(grad_logits, table).astype(BF16)
    grad_table = matmul_tn(grad_logits, rows)
    grad_picked = lax.psum_scatter(grad_rows, SHARE, scatter_dimension=0, tiled=True)
    grad_final = matmul_tn(chosen_bf16, grad_picked)

    grad_output_rows, grad_gain_three = norm_backward(
        grad_final, unit_three, scale_three, gains[:, 2]
    )
    grad_branch = grad_output_rows.astype(BF16)
    grad_ffn_out = matmul_tn(activated, grad_branch).astype(BF16)
    grad_act = matmul_nt(grad_branch, w_ffn_out)
    grad_pre = gelu_back(grad_act)[0].astype(BF16)
    grad_ffn_in = matmul_tn(ffn_input, grad_pre).astype(BF16)
    ffn_grads = jnp.concatenate(
        [
            grad_ffn_in.reshape(device_count, rows_ffn, width),
            grad_ffn_out.reshape(device_count, rows_ffn_out, width),
        ],
        1,
    )
    ffn_grads = lax.psum_scatter(ffn_grads, ALL, scatter_dimension=0, tiled=False)
    grad_norm_two = matmul_nt(grad_pre, w_ffn_in)
    grad_res_two, grad_gain_two = norm_backward(grad_norm_two, unit_two, scale_two, gains[:, 1])
    grad_residual = grad_output_rows + grad_res_two

    grad_attn_branch = grad_residual.astype(BF16)
    grad_attn_out = matmul_tn(attended, grad_attn_branch).astype(BF16)
    grad_attended = matmul_nt(grad_attn_branch, w_out).astype(BF16)
    scores = attention_scores(query, key_side[:, :width], allowed)
    attn_probs = jnp.exp(scores - log_total)
    grad_heads = split_heads(grad_attended)
    grad_probs = jnp.einsum("qhd,khd->hqk", grad_heads, value_heads, preferred_element_type=F32)
    grad_scores = attn_probs * (grad_probs - jnp.sum(attn_probs * grad_probs, -1, keepdims=True))
    grad_scores = (grad_scores * HEAD ** (-0.5)).astype(BF16)
    grad_query = jnp.einsum(
        "hqk,khd->qhd",
        grad_scores,
        split_heads(key_side[:, :width]),
        preferred_element_type=F32,
    ).reshape(segment, width)
    grad_keys = jnp.einsum(
        "hqk,qhd->khd", grad_scores, split_heads(query), preferred_element_type=F32
    ).reshape(-1, width)
    grad_values = jnp.einsum(
        "hqk,qhd->khd", attn_probs.astype(BF16), grad_heads, preferred_element_type=F32
    ).reshape(-1, width)
    grad_pairs = jnp.concatenate([grad_keys, grad_values], -1)
    received = jnp.zeros((slots, 2 * width), F32)
    for hop in (2, 3, 4):
        first_row = 2 * segment + (hop - 2) * slots
        received = received + passed_along(
            grad_pairs[first_row : first_row + slots].astype(BF16), -hop
        ).astype(F32)
    grad_comp_pairs = received.astype(BF16)
    grad_pairs_comp = matmul_tn(compressed, grad_comp_pairs)
    grad_compressed = matmul_nt(grad_comp_pairs, w_pairs).astype(BF16)
    grad_compress = matmul_tn(slot_rows, grad_compressed).astype(BF16)
    grad_slots = matmul_nt(grad_compressed, w_compress).reshape(3 * slots, width)
    grad_extended = lax.dynamic_update_slice_in_dim(
        jnp.zeros((segment + 6, width), F32), grad_slots, first_cell, 0
    )
    back_memory = passed_along(grad_pairs[segment : 2 * segment].astype(BF16), -1).astype(F32)
    back_tail = passed_along(grad_extended[:2].astype(BF16), -1).astype(F32)
    grad_own_pairs = (grad_pairs[:segment] + back_memory).astype(BF16)
    projected_gradient = jnp.concatenate([grad_query.astype(BF16), grad_own_pairs], -1)
    grad_attn_in = matmul_tn(attention_input, projected_gradient)
    grad_attn_in = grad_attn_in + jnp.concatenate(
        [jnp.zeros((width, width), F32), grad_pairs_comp], 1
    )
    grad_input = matmul_nt(projected_gradient, w_in) + grad_extended[2 : segment + 2]
    grad_input = grad_input.at[segment - 2 :].add(back_tail)
    grad_embed, grad_gain_one = norm_backward(grad_input, unit_one, scale_one, gains[:, 0])
    grad_scaled = ((grad_embed + grad_residual) * width**0.5).astype(BF16)

    share_grads = lax.all_gather(grad_scaled, SHARE, axis=0, tiled=True)
    spread = (
        jnp.arange(table.shape[0], dtype=jnp.int32)[:, None] == share_row[None, :]
    ).astype(BF16)
    grad_table = (grad_table + matmul(spread, share_grads)).astype(BF16)
    grad_table = lax.psum_scatter(grad_table, PLANE, scatter_dimension=0, tiled=True)

    mixer_grads = jnp.concatenate(
        [
            grad_attn_in.astype(BF16).reshape(device_count, rows_in, width),
            grad_compress.reshape(device_count, rows_comp, width),
            grad_attn_out.reshape(device_count, rows_out, width),
        ],
        1,
    )
    mixer_grads = lax.psum_scatter(mixer_grads, ALL, scatter_dimension=0, tiled=False)
    small = jnp.concatenate(
        [
            jnp.stack([grad_gain_one, grad_gain_two, grad_gain_three], 1).reshape(-1),
            jnp.full((128,), loss_local, F32),
        ]
    )
    small = lax.psum(small, ALL)
    loss_total = small[3 * width]
    device = lax.axis_index(ALL)
    gain_grads = lax.dynamic_slice_in_dim(small, device * gain_count, gain_count, 0)
    grads = (
        grad_table,
        mixer_grads[:rows_in].reshape(attn_in_m.shape),
        mixer_grads[rows_in + rows_comp :].reshape(attn_out_m.shape),
        mixer_grads[rows_in : rows_in + rows_comp].reshape(compress_m.shape),
        ffn_grads[:rows_ffn].reshape(ffn_in_m.shape),
        ffn_grads[rows_ffn:].reshape(ffn_out_m.shape),
        gain_grads.reshape(gains_m.shape),
    )
    results = []
    for master, first, second, grad, rate in zip(masters, firsts, seconds, grads, STEP_RATES):
        results.extend(adam_update(master, first, second, grad.astype(F32), rate))
    return (loss_total,) + tuple(results)


def solution(mesh):
    batch_count, seq_count = mesh.shape["batch"], mesh.shape["seq"]
    devices = mesh.devices.reshape(batch_count, seq_count // 4, 2, 2)
    grid = Mesh(devices, ALL)
    rows = P(ALL, None)
    return jax.shard_map(
        per_device,
        mesh=grid,
        in_specs=(P("batch", SEQ), P("batch", None), P("batch", SEQ)) + (rows,) * 21,
        out_specs=(P(),) + (rows,) * 21,
        check_vma=False,
    )
```

time: 3100 us -> 1540 us (0.50)
  waiting for transfers between devices: 1990 us -> 714 us
  other arithmetic: 279 us -> 108 us
  matrix products: 538 us -> 379 us
  local copies, waits for them, and re-layouts: 139 us -> 203 us
    reduce_scatter x7 -> x4, waiting for transfers between devices: 1300 us -> 313 us  [the longest x1 175 us: per_device(): lax.psum_scatter(ffn_grads, ALL, scatter_dimension=0, tiled=False)]
    all_gather x7 -> x5, waiting for transfers between devices: 563 us -> 321 us  [the longest x1 84.6 us: per_device(): ffn_all = lax.all_gather(ffn_block, ALL, axis=0, tiled=False)]
    dot_general x30, matrix products: 538 us -> 379 us  [the longest x9 111 us: matmul(): return jnp.dot(left, right, preferred_element_type=F32)]
    scatter-add x4 -> x1, other arithmetic: 107 us -> 0.02 us  [per_device(): grad_input = grad_input.at[segment - 2:].add(back_tail)]
    convert_element_type x11 -> x17, other arithmetic: 73.7 us -> 12 us  [the longest x1 3.85 us: per_device(): grad_own_pairs = (grad_pairs[:segment] + back_memory).astype(BF16)]
    psum x0 -> x2, blocking collectives: none -> 57.8 us  [the longest x1 42.4 us: per_device(): small = lax.psum(small, ALL)]
    reshape x1 -> x14, local copies, waits for them, and re-layouts: 2.8 us -> 54.3 us  [the longest x1 14.2 us: per_device(): grad_ffn_in.reshape(device_count, rows_ffn, width)]
    unnamed x1 -> x0, blocking collectives: 39.7 us -> none
  transfers between devices with their start and end apart: 25 -> 21, of which waited for: 17 -> 10; matrix products, arithmetic and copies ran while one was open for 10% -> 22% of each run, Pallas kernels for 0% -> 0%
where the time goes in v1:
time: 1540 us; the launch traced here: 1530 us
  waiting for transfers between devices  714 us (46%)
  matrix products  379 us (25%)
  local copies, waits for them, and re-layouts  203 us (13%)
  other arithmetic  108 us (7%)
  blocking collectives  86.1 us (6%)
  starting transfers between devices  23.3 us (2%)
  between operations  17.6 us (1%)
    reduce_scatter x1, waiting for transfers between devices, per_device(): lax.psum_scatter(ffn_grads, ALL, scatter_dimension=0, tiled=False)  175 us
    dot_general x9, matrix products, matmul(): return jnp.dot(left, right, preferred_element_type=F32)  111 us
    reduce_scatter x1, waiting for transfers between devices, per_device(): lax.psum_scatter(looked, SHARE, scatter_dimension=0, tiled=True)  89.3 us
    all_gather x1, waiting for transfers between devices, per_device(): ffn_all = lax.all_gather(ffn_block, ALL, axis=0, tiled=False)  84.6 us
    unnamed x11, waiting for transfers between devices  78.7 us
    all_gather x1, waiting for transfers between devices, per_device(): table = lax.all_gather(table_master.astype(BF16), PLANE, axis=0, tiled=True)  73.6 us
    all_gather x1, waiting for transfers between devices, per_device(): lax.all_gather(jnp.concatenate([picked_rows, side_rows], 0), SHARE, axis=...  70.3 us
    dot_general x8, matrix products, matmul_tn(): lax.dot_general(left, right, (((0,), (0,)), ((), ())), preferred_element_...  69.7 us
  transfers between devices with their start and end apart: 21, of which 10 were waited for; matrix products, arithmetic and copies ran while one was open for 22% of the time, Pallas kernels for 0%

profile of v1, /device:TPU:0, one launch (start us, length us, event | category | flops | bytes accessed | tf_op | source)
XLA Modules:
  0.0 1531.4 jit_solution(1448289866648498940)
XLA Ops:
  12.0 14.4 all-gather
  27.1 73.6 %all-gather.12.cloned.1.call-done = bf16[4000,1024]{1,0:T(8,128)(2,1)} async-done(((bf16[1000,1024]{1,0:T(8,128)(2,1)}), bf16[4000,1024]{1,0:T(8,128)(2,1)}) %all-gather.12.cloned.1.call-update) | async-done | bytes 8192016 | tf_op jit(solution)/shard_map/all_gather | solution.py:119
  100.7 25.3 %gather_fusion = bf16[4096,1024]{1,0:T(8,128)(2,1)} fusion(bf16[4000,1024]{1,0:T(8,128)(2,1)} %all-gather.12.cloned.1.call-done, s32[4096]{0:T(1024)S(1)} %maximum_clamp_fusion), kind=kCustom, calls=%fused_computation | custom fusion | bytes 16793600 | tf_op jit(solution)/shard_map/gather | solution.py:130
  138.8 15.4 %psum.14 = f32[8]{0:T(128)S(1)} all-reduce(f32[8]{0:T(128)S(1)} %select_reduce_fusion.3), channel_id=1, replica_groups=mesh['batch'=4,'y'=2,'x'=2,'core'=2] {'y','x','core'}, use_global_device_ids=true, to_apply=%region_23.24 | all-reduce | flops 8 | bytes 64 | tf_op jit(solution)/shard_map/psum | solution.py:176
  160.1 89.3 %reduce-scatter.8.cloned.1.call-done = bf16[512,1024]{1,0:T(8,128)(2,1)} async-done(((bf16[4096,1024]{1,0:T(8,128)(2,1)}), bf16[512,1024]{1,0:T(8,128)(2,1)}) %reduce-scatter.8.cloned.1.call-update) | async-done | bytes 1048592 | tf_op jit(solution)/shard_map/reduce_scatter | solution.py:132
  252.6 54.4 %all-gather.16.cloned.1.call-done = bf16[7680,1024]{1,0:T(8,128)(2,1)} async-done(((bf16[240,1024]{1,0:T(8,128)(2,1)}), bf16[7680,1024]{1,0:T(8,128)(2,1)}) %all-gather.16.cloned.1.call-update) | async-done | bytes 15728656 | tf_op jit(solution)/shard_map/all_gather | solution.py:155
  367.7 84.6 %all-gather.18.cloned.1.call-done = bf16[8192,1024]{1,0:T(8,128)(2,1)} async-done(((bf16[256,1024]{1,0:T(8,128)(2,1)}), bf16[8192,1024]{1,0:T(8,128)(2,1)}) %all-gather.18.cloned.1.call-update) | async-done | bytes 16777232 | tf_op jit(solution)/shard_map/all_gather | solution.py:156
  478.3 27.9 %concatenate.56 = bf16[1537,2048]{1,0:T(8,128)(2,1)} concatenate(bf16[512,2048]{1,0:T(8,128)(2,1)S(1)} %slice.245, bf16[512,2048]{1,0:T(8,128)(2,1)} %collective-permute-done, bf16[171,2048]{1,0:T(8,128)(2,1)} %collective-permute-done.2, bf16[171,2048]{1,0:T(8,128)(2,1)S(1)} %collective-permute-done.3, bf16[171,2048]{1,0:T(8,128)(2,1)S(1)} %collective-permute-done.4), dimensions={0} | concatenate | bytes 12591104 | tf_op jit(solution)/shard_map/concatenate | solution.py:218
  569.1 70.3 %all-gather.20.cloned.1.call-done = bf16[2176,1024]{1,0:T(8,128)(2,1)} async-done(((bf16[272,1024]{1,0:T(8,128)(2,1)}), bf16[2176,1024]{1,0:T(8,128)(2,1)}) %all-gather.20.cloned.1.call-update) | async-done | bytes 4456464 | tf_op jit(solution)/shard_map/all_gather | solution.py:255
  645.3 25.0 %fusion.172 = (f32[2048]{0:T(1024)S(1)}, f32[2048,4000]{0,1:T(8,128)}) fusion(bf16[2048,1024]{1,0:T(8,128)(2,1)} %bitcast.193, bf16[4000,1024]{1,0:T(8,128)(2,1)} %all-gather.12.cloned.1.call-done), kind=kOutput, calls=%fused_computation.349 | convolution fusion | flops 16785405952 | bytes 45162496 | tf_op jit(solution)/shard_map/dot_general | solution.py:63
  670.3 14.8 select_reduce_fusion
  700.0 25.1 %convolution_convert_fusion.4 = bf16[2048,1024]{1,0:T(8,128)(2,1)} fusion(bf16[4000,1024]{1,0:T(8,128)(2,1)} %all-gather.12.cloned.1.call-done, f32[2048,4000]{0,1:T(8,128)} %get-tuple-element.221, s32[2048]{0:T(1024)S(1)} %fusion.118, f32[2048]{0:T(1024)S(1)} %log_add_fusion.1, f32[2048]{0:T(1024)S(1)} %bitcast.212), kind=kOutput, calls=%fused_computation.47 | convolution fusion | flops 16828465152 | bytes 45178880 | tf_op jit(solution)/shard_map/dot_general | solution.py:59
  725.4 48.7 %reduce-scatter.10.cloned.1.call-done = bf16[256,1024]{1,0:T(8,128)(2,1)} async-done(((bf16[2048,1024]{1,0:T(8,128)(2,1)}), bf16[256,1024]{1,0:T(8,128)(2,1)}) %reduce-scatter.10.cloned.1.call-update) | async-done | bytes 524304 | tf_op jit(solution)/shard_map/reduce_scatter | solution.py:281
  778.2 16.0 %fusion.14 = bf16[512,4096]{1,0:T(8,128)(2,1)} fusion(f32[512,4096]{1,0:T(8,128)} %copy-done.85, bf16[4096,1024]{1,0:T(8,128)(2,1)} %bitcast.184, f32[512,1024]{1,0:T(8,128)S(1)} %subtract_multiply_fusion), kind=kOutput, calls=%fused_computation.29 | convolution fusion | flops 4337434624 | bytes 23068672 | tf_op jit(solution)/shard_map/dot_general | solution.py:63
  807.0 14.8 convolution_bitcast_fusion
  844.2 41.7 %fusion.21 = f32[1537,8,128]{2,0,1:T(8,128)} fusion(f32[8,512,1537]{1,2,0:T(8,128)} %fusion.36, f32[8,512,1537]{1,2,0:T(8,128)} %get-tuple-element.215, f32[8,512]{1,0:T(8,128)S(1)} %copy-done.52, bf16[512,3072]{1,0:T(8,128)(2,1)} %copy-done.32), kind=kOutput, calls=%fused_computation.41 | convolution fusion | flops 1655735808 | bytes 108564480 | tf_op jit(solution)/shard_map/hqk,qhd->khd/dot_general | solution.py:319
  916.9 42.1 %fusion.53 = bf16[8,128,512]{2,1,0:T(8,128)(2,1)S(1)} fusion(f32[8,512,1537]{1,2,0:T(8,128)} %fusion.36, f32[8,512,1537]{1,2,0:T(8,128)} %get-tuple-element.215, f32[8,512]{1,0:T(8,128)S(1)} %copy-done.52, bf16[1537,8,128]{2,1,0:T(8,128)(2,1)} %copy-done.19), kind=kOutput, calls=%fused_computation.92 | convolution fusion | flops 1656260096 | bytes 54577152 | tf_op jit(solution)/shard_map/hqk,khd->qhd/dot_general | solution.py:313
  1035.4 27.0 %fusion.151 = f32[4000,1024]{1,0:T(8,128)} fusion(bf16[2048,1024]{1,0:T(8,128)(2,1)} %bitcast.194, f32[2048,4000]{0,1:T(8,128)} %get-tuple-element.221, s32[2048]{0:T(1024)S(1)} %copy-done.62, f32[2048]{0:T(1024)S(1)} %copy-done.64, f32[2048]{0:T(1024)S(1)} %bitcast.213), kind=kOutput, calls=%fused_computation.340 | convolution fusion | flops 16826368000 | bytes 53370880 | tf_op jit(solution)/shard_map/dot_general | solution.py:67
  1062.4 38.6 %all-gather.14.cloned.1.call-done = bf16[4096,1024]{1,0:T(8,128)(2,1)} async-done(((bf16[512,1024]{1,0:T(8,128)(2,1)}), bf16[4096,1024]{1,0:T(8,128)(2,1)}) %all-gather.14.cloned.1.call-update) | async-done | bytes 8388624 | tf_op jit(solution)/shard_map/all_gather | solution.py:353
  1101.1 53.1 %add_convert_fusion = bf16[4000,1024]{1,0:T(8,128)(2,1)} fusion(f32[4000,1024]{1,0:T(8,128)} %fusion.151, bf16[4096,1024]{1,0:T(8,128)(2,1)} %all-gather.14.cloned.1.call-done, s32[4096]{0:T(1024)S(1)} %copy-done.56), kind=kOutput, calls=%fused_computation.17 | convolution fusion | flops 33579008000 | bytes 32980992 | tf_op jit(solution)/shard_map/dot_general | solution.py:59
  1165.2 14.2 reshape.758
  1204.7 42.4 %psum.15 = f32[3200]{0:T(1024)S(1)} all-reduce(f32[3200]{0:T(1024)S(1)} %concatenate.66), channel_id=1, replica_groups=mesh['batch'=4,'y'=2,'x'=2,'core'=2] {'batch','y','x','core'}, use_global_device_ids=true, to_apply=%region_41.42 | all-reduce | flops 3200 | bytes 25600 | tf_op jit(solution)/shard_map/psum | solution.py:375
  1254.7 78.6 %reduce-scatter.16.cloned.1.call-done = bf16[1000,1024]{1,0:T(8,128)(2,1)} async-done(((bf16[4000,1024]{1,0:T(8,128)(2,1)}), bf16[1000,1024]{1,0:T(8,128)(2,1)}) %reduce-scatter.16.cloned.1.call-update) | async-done | bytes 2048016
  1342.9 175.4 %reduce-scatter.14.cloned.1.call-done = bf16[1,256,1024]{2,1,0:T(8,128)(2,1)} async-done(((bf16[32,256,1024]{2,1,0:T(8,128)(2,1)}), bf16[1,256,1024]{2,1,0:T(8,128)(2,1)}) %reduce-scatter.14.cloned.1.call-update) | async-done | bytes 524304 | tf_op jit(solution)/shard_map/reduce_scatter | solution.py:299
  (426 shorter events, 401.3 us)
Async XLA Ops:
  8.0 92.7 %all-gather.12.cloned.1.call-start = ((), (), s32[]{:S(2)}) async-start(), calls=%async_computation.5 | async-start | bytes 10240000 | tf_op jit(solution)/shard_map/all_gather | solution.py:119
  11.9 237.5 %reduce-scatter.8.cloned.1.call-start = ((), (), s32[]{:S(2)}) async-start(), calls=%async_computation.6 | async-start | bytes 9437184 | tf_op jit(solution)/shard_map/reduce_scatter | solution.py:132
  133.3 173.7 %all-gather.16.cloned.1.call-start = ((), (), s32[]{:S(2)}) async-start(), calls=%async_computation.11 | async-start | bytes 16220160 | tf_op jit(solution)/shard_map/all_gather | solution.py:155
  135.3 317.0 %all-gather.18.cloned.1.call-start = ((), (), s32[]{:S(2)}) async-start(), calls=%async_computation.12 | async-start | bytes 17301504 | tf_op jit(solution)/shard_map/all_gather | solution.py:156
  136.5 502.9 %all-gather.20.cloned.1.call-start = ((), (), s32[]{:S(2)}) async-start(), calls=%async_computation.13 | async-start | bytes 5013504 | tf_op jit(solution)/shard_map/all_gather | solution.py:255
  137.5 20.1 %collective-permute-start.5 = (s32[1]{0:T(128)}, s32[1]{0:T(128)}, u32[]{:S(2)}, u32[]{:S(2)}) collective-permute-start(s32[1]{0:T(128)} %bitcast.14), channel_id=1, source_target_pairs={{1,0},{2,1},{3,2},{4,3},{5,4},{6,5},{7,6},{9,8},{10,9},{11,10},{12... | collective-permute-start | bytes 20 | tf_op jit(solution)/shard_map/ppermute | solution.py:32
  330.9 471.8 %copy-start.70 = (f32[1024]{0:T(1024)}, f32[1024]{0:T(1024)S(1)}, u32[]{:S(2)}) copy-start(f32[1024]{0:T(1024)S(1)} %get-tuple-element.158) | copy-start | bytes 12292
  331.5 17.9 %collective-permute-start.1 = (bf16[2,1024]{1,0:T(2,128)(2,1)S(1)}, bf16[2,1024]{1,0:T(2,128)(2,1)S(1)}, u32[]{:S(2)}, u32[]{:S(2)}) collective-permute-start(bf16[2,1024]{1,0:T(2,128)(2,1)S(1)} %slice.246), channel_id=1, source_target_pairs={{0,1},{1,2},{2,3},{3,4},{4,5},{5,6},{6,7},{8,9},{9,10},{10,11},{11... | collective-permute-start | bytes 12296 | tf_op jit(solution)/shard_map/ppermute | solution.py:32
  344.7 133.6 %collective-permute-start = (bf16[512,2048]{1,0:T(8,128)(2,1)S(1)}, bf16[512,2048]{1,0:T(8,128)(2,1)}, u32[]{:S(2)}, u32[]{:S(2)}) collective-permute-start(bf16[512,2048]{1,0:T(8,128)(2,1)S(1)} %slice.245), channel_id=1, source_target_pairs={{0,1},{1,2},{2,3},{3,4},{4,5},{5,6},{6,7},{8,9},{9,10},{10,11},{11... | collective-permute-start | bytes 6291464 | tf_op jit(solution)/shard_map/ppermute | solution.py:32
  361.0 117.3 %collective-permute-start.4 = (bf16[171,2048]{1,0:T(8,128)(2,1)}, bf16[171,2048]{1,0:T(8,128)(2,1)S(1)}, u32[]{:S(2)}, u32[]{:S(2)}) collective-permute-start(bf16[171,2048]{1,0:T(8,128)(2,1)} %fusion.39), channel_id=1, source_target_pairs={{0,4},{1,5},{2,6},{3,7},{8,12},{9,13},{10,14},{11,15},{16,20},{17,... | collective-permute-start | bytes 2101256 | tf_op jit(solution)/shard_map/ppermute | solution.py:32
  362.3 115.9 %collective-permute-start.3 = (bf16[171,2048]{1,0:T(8,128)(2,1)}, bf16[171,2048]{1,0:T(8,128)(2,1)S(1)}, u32[]{:S(2)}, u32[]{:S(2)}) collective-permute-start(bf16[171,2048]{1,0:T(8,128)(2,1)} %fusion.39), channel_id=1, source_target_pairs={{0,3},{1,4},{2,5},{3,6},{4,7},{8,11},{9,12},{10,13},{11,14},{12,15... | collective-permute-start | bytes 2101256 | tf_op jit(solution)/shard_map/ppermute | solution.py:32
  364.4 113.9 %collective-permute-start.2 = (bf16[171,2048]{1,0:T(8,128)(2,1)}, bf16[171,2048]{1,0:T(8,128)(2,1)}, u32[]{:S(2)}, u32[]{:S(2)}) collective-permute-start(bf16[171,2048]{1,0:T(8,128)(2,1)} %fusion.39), channel_id=1, source_target_pairs={{0,2},{1,3},{2,4},{3,5},{4,6},{5,7},{8,10},{9,11},{10,12},{11,13},... | collective-permute-start | bytes 2101256 | tf_op jit(solution)/shard_map/ppermute | solution.py:32
  569.1 205.0 %reduce-scatter.10.cloned.1.call-start = ((), (), s32[]{:S(2)}) async-start(), calls=%async_computation.7 | async-start | bytes 4718592 | tf_op jit(solution)/shard_map/reduce_scatter | solution.py:281
  725.2 375.9 %all-gather.14.cloned.1.call-start = ((), (), s32[]{:S(2)}) async-start(), calls=%async_computation.8 | async-start | bytes 9437184 | tf_op jit(solution)/shard_map/all_gather | solution.py:353
  910.2 73.6 %collective-permute-start.6 = (bf16[512,2048]{1,0:T(8,128)(2,1)}, bf16[512,2048]{1,0:T(8,128)(2,1)}, u32[]{:S(2)}, u32[]{:S(2)}) collective-permute-start(bf16[512,2048]{1,0:T(8,128)(2,1)} %slice.268), channel_id=1, source_target_pairs={{1,0},{2,1},{3,2},{4,3},{5,4},{6,5},{7,6},{9,8},{10,9},{11,10},{12... | collective-permute-start | bytes 6291464 | tf_op jit(solution)/shard_map/ppermute | solution.py:32
  913.0 47.9 %collective-permute-start.7 = (bf16[171,2048]{1,0:T(8,128)(2,1)}, bf16[171,2048]{1,0:T(8,128)(2,1)S(1)}, u32[]{:S(2)}, u32[]{:S(2)}) collective-permute-start(bf16[171,2048]{1,0:T(8,128)(2,1)} %get-tuple-element.196), channel_id=1, source_target_pairs={{2,0},{3,1},{4,2},{5,3},{6,4},{7,5},{10,8},{11,9},{12,10},{13,11},... | collective-permute-start | bytes 2101256 | tf_op jit(solution)/shard_map/ppermute | solution.py:32
  914.3 46.6 %collective-permute-start.9 = (bf16[171,2048]{1,0:T(8,128)(2,1)}, bf16[171,2048]{1,0:T(8,128)(2,1)S(1)}, u32[]{:S(2)}, u32[]{:S(2)}) collective-permute-start(bf16[171,2048]{1,0:T(8,128)(2,1)} %get-tuple-element.197), channel_id=1, source_target_pairs={{4,0},{5,1},{6,2},{7,3},{12,8},{13,9},{14,10},{15,11},{20,16},{21,... | collective-permute-start | bytes 2101256 | tf_op jit(solution)/shard_map/ppermute | solution.py:32
  915.6 45.3 %collective-permute-start.8 = (bf16[171,2048]{1,0:T(8,128)(2,1)}, bf16[171,2048]{1,0:T(8,128)(2,1)}, u32[]{:S(2)}, u32[]{:S(2)}) collective-permute-start(bf16[171,2048]{1,0:T(8,128)(2,1)} %get-tuple-element.198), channel_id=1, source_target_pairs={{3,0},{4,1},{5,2},{6,3},{7,4},{11,8},{12,9},{13,10},{14,11},{15,12... | collective-permute-start | bytes 2101256 | tf_op jit(solution)/shard_map/ppermute | solution.py:32
  981.9 9.3 collective-permute-start.10
  994.6 253.8 %reduce-scatter.12.cloned.1.call-start = ((), (), s32[]{:S(2)}) async-start(), calls=%async_computation.9 | async-start | bytes 15138816 | tf_op jit(solution)/shard_map/reduce_scatter | solution.py:368
  1034.7 298.5 %reduce-scatter.16.cloned.1.call-start = ((), (), s32[]{:S(2)}) async-start(), calls=%async_computation.14 | async-start | bytes 10240000
  1154.2 364.1 %reduce-scatter.14.cloned.1.call-start = ((), (), s32[]{:S(2)}) async-start(), calls=%async_computation.10 | async-start | bytes 17301504 | tf_op jit(solution)/shard_map/reduce_scatter | solution.py:299
  1254.7 264.9 %copy-start.43 = (f32[32,4096]{1,0:T(8,128)S(1)}, f32[32,4096]{1,0:T(8,128)}, u32[]{:S(2)}) copy-start(f32[32,4096]{1,0:T(8,128)} %param.51) | copy-start | bytes 1572868
  1254.7 264.9 %copy-start.44 = (f32[32,4096]{1,0:T(8,128)S(1)}, f32[32,4096]{1,0:T(8,128)}, u32[]{:S(2)}) copy-start(f32[32,4096]{1,0:T(8,128)} %param.44) | copy-start | bytes 1572868
  (91 other events, 2419.6 us)
Sparse Core Ops, SparseCore 0:
  12.0 88.6 all-gather.11
  133.4 115.9 reduce-scatter.7
  569.2 70.1 all-gather.19
  725.3 48.7 reduce-scatter.9
  994.7 106.2 all-gather.13
Sparse Core Ops, SparseCore 1:
  137.3 169.7 all-gather.15
  310.3 142.0 all-gather.17
  1034.8 208.8 reduce-scatter.11
  1246.9 86.3 reduce-scatter.15
  1335.6 182.7 reduce-scatter.13

commit v2 on v1

v2 whole, which is shorter than its diff:
```python
import jax
import jax.numpy as jnp
from jax import lax
from jax.experimental import pallas as pl
from jax.experimental.pallas import tpu as pltpu
from jax.sharding import Mesh
from jax.sharding import PartitionSpec as P

MODEL_WIDTH = 1024
HEADS = 8
HEAD = 128
NBOOK = 8
STEP = 5

EPSILON = 1e-05
NEGATIVE = -1e30
BETA_ONE = 0.9
BETA_TWO = 0.95
ADAM_EPSILON = 1e-08
WEIGHT_DECAY = 0.1
STEP_RATES = (0.06, 0.03, 0.4, 0.02, 0.03, 0.04, 0.5)

SEQ = ("far", "y", "x", "core")
PLANE = ("far", "y", "x")
SHARE = ("batch", "core")
LINE = ("batch", "far")
ALL = ("batch", "far", "y", "x", "core")
PIECE = 512
BLOCK = 128
GROUPS = 32
BF16 = jnp.bfloat16
F32 = jnp.float32


def passed_along(value, steps):
    count = lax.axis_size(SEQ)
    initial, last = (max(0, -steps), min(count, count - steps))
    return lax.ppermute(value, SEQ, [(source, source + steps) for source in range(initial, last)])


def norm_forward(values, gain):
    center = values - jnp.mean(values, -1, keepdims=True)
    scaler = lax.rsqrt(jnp.mean(center * center, -1, keepdims=True) + EPSILON)
    unit_rows = center * scaler
    return (unit_rows * gain, unit_rows, scaler)


def norm_backward(grad_out, unit_rows, scaler, gain):
    scaled = grad_out * gain
    grad_gain = jnp.sum(grad_out * unit_rows, axis=0)
    grad_in = scaler * (
        scaled
        - jnp.mean(scaled, -1, keepdims=True)
        - unit_rows * jnp.mean(scaled * unit_rows, -1, keepdims=True)
    )
    return (grad_in, grad_gain)


def book_number(positions, book_ends):
    inside = jnp.sum((positions[:, None] >= book_ends[None, :]).astype(jnp.int32), -1)
    return jnp.where(positions < 0, -1, inside)


def matmul(left, right):
    return jnp.dot(left, right, preferred_element_type=F32)


def matmul_nt(left, right):
    return lax.dot_general(left, right, (((1,), (1,)), ((), ())), preferred_element_type=F32)


def matmul_tn(left, right):
    return lax.dot_general(left, right, (((0,), (0,)), ((), ())), preferred_element_type=F32)


def fill_bias(bias, key_book, key_pos, query_book, query_pos):
    allowed = (key_book[...] == query_book[...]) & (key_pos[...] <= query_pos[...])
    bias[...] = jnp.where(allowed, 0.0, NEGATIVE)


def attention_forward_body(*refs):
    query, own_k, own_v, mem_k, mem_v = refs[:5]
    marks, (out, log_total, bias) = refs[5:9], refs[9:]

    @pl.when(pl.program_id(0) == 0)
    def _():
        fill_bias(bias, *marks)

    keys = jnp.concatenate([own_k[...], mem_k[...]], 0)
    values = jnp.concatenate([own_v[...], mem_v[...]], 0)
    scores = matmul_nt(keys, query[...]) * HEAD ** (-0.5) + bias[...]
    top = jnp.max(scores, 0, keepdims=True)
    probs = jnp.exp(scores - top)
    total = jnp.sum(probs, 0, keepdims=True)
    log_total[0] = top + jnp.log(total)
    probs = (probs * (1.0 / total)).astype(BF16)
    out[...] = matmul_tn(values, probs).T.astype(BF16)


def attention_backward_body(*refs):
    query, own_k, own_v, mem_k, mem_v = refs[:5]
    marks = refs[5:9]
    log_total, grad_out, grad_query, grad_own, grad_mem, g2, g3, g4, bias = refs[9:]

    @pl.when(pl.program_id(0) == 0)
    def _():
        fill_bias(bias, *marks)

    keys = jnp.concatenate([own_k[...], mem_k[...]], 0)
    values = jnp.concatenate([own_v[...], mem_v[...]], 0)
    scores = matmul_nt(keys, query[...]) * HEAD ** (-0.5) + bias[...]
    probs = jnp.exp(scores - log_total[0])
    grad_probs = matmul_nt(values, grad_out[...])
    inner = jnp.sum(probs * grad_probs, 0, keepdims=True)
    grad_scores = (probs * (grad_probs - inner) * HEAD ** (-0.5)).astype(BF16)
    grad_query[...] = matmul_tn(keys, grad_scores).T.astype(BF16)
    pair = (matmul(grad_scores, query[...]), matmul(probs.astype(BF16), grad_out[...]))
    at = 0
    for part in (grad_own, grad_mem, g2, g3, g4):
        count = part.shape[1]
        for side in (0, 1):
            part[side] = pair[side][at : at + count].astype(part.dtype)
        at += count


def attention_specs(segment, others):
    def column(rows, shift):
        return pl.BlockSpec((rows, HEAD), lambda h: (0, h + shift * HEADS))

    mark_k = pl.BlockSpec((segment + others, 1), lambda h: (0, 0))
    mark_q = pl.BlockSpec((1, segment), lambda h: (0, 0))
    specs = [column(segment, 0), column(segment, 1), column(segment, 2)]
    specs += [column(others, 0), column(others, 1)]
    return specs + [mark_k, mark_k, mark_q, mark_q]


def attention_forward(projected, memory, marks):
    segment, others = projected.shape[0], memory.shape[0]
    keys = segment + others
    return pl.pallas_call(
        attention_forward_body,
        grid=(HEADS,),
        in_specs=attention_specs(segment, others),
        out_specs=[
            pl.BlockSpec((segment, HEAD), lambda h: (0, h)),
            pl.BlockSpec((1, 1, segment), lambda h: (h, 0, 0)),
        ],
        out_shape=[
            jax.ShapeDtypeStruct((segment, HEADS * HEAD), BF16),
            jax.ShapeDtypeStruct((HEADS, 1, segment), F32),
        ],
        scratch_shapes=[pltpu.VMEM((keys, segment), F32)],
        compiler_params=pltpu.CompilerParams(vmem_limit_bytes=48 << 20),
        cost_estimate=pl.CostEstimate(
            flops=4 * HEADS * keys * segment * HEAD,
            bytes_accessed=12 << 20,
            transcendentals=HEADS * keys * segment,
        ),
        name="attention_forward",
    )(projected, projected, projected, memory, memory, *marks)


def attention_backward(projected, memory, marks, log_total, grad_out):
    segment, others = projected.shape[0], memory.shape[0]
    keys, slots = segment + others, (others - segment) // 3
    width = HEADS * HEAD

    def pair_spec(rows):
        return pl.BlockSpec((2, rows, HEAD), lambda h: (0, 0, h))

    return pl.pallas_call(
        attention_backward_body,
        grid=(HEADS,),
        in_specs=attention_specs(segment, others)
        + [
            pl.BlockSpec((1, 1, segment), lambda h: (h, 0, 0)),
            pl.BlockSpec((segment, HEAD), lambda h: (0, h)),
        ],
        out_specs=[pl.BlockSpec((segment, HEAD), lambda h: (0, h))]
        + [pair_spec(segment)] * 2
        + [pair_spec(slots)] * 3,
        out_shape=[
            jax.ShapeDtypeStruct((segment, width), BF16),
            jax.ShapeDtypeStruct((2, segment, width), F32),
            jax.ShapeDtypeStruct((2, segment, width), BF16),
        ]
        + [jax.ShapeDtypeStruct((2, slots, width), BF16)] * 3,
        scratch_shapes=[pltpu.VMEM((keys, segment), F32)],
        compiler_params=pltpu.CompilerParams(vmem_limit_bytes=48 << 20),
        cost_estimate=pl.CostEstimate(
            flops=10 * HEADS * keys * segment * HEAD,
            bytes_accessed=24 << 20,
            transcendentals=HEADS * keys * segment,
        ),
        name="attention_backward",
    )(projected, projected, projected, memory, memory, *marks, log_total, grad_out)


def adam_update(master, first, second, grad, rate):
    new_first = BETA_ONE * first + (1.0 - BETA_ONE) * grad
    new_second = BETA_TWO * second + (1.0 - BETA_TWO) * grad * grad
    first_hat = new_first / (1.0 - BETA_ONE**STEP)
    second_hat = new_second / (1.0 - BETA_TWO**STEP)
    new_master = master - rate * (
        first_hat / (jnp.sqrt(second_hat) + ADAM_EPSILON) + WEIGHT_DECAY * master
    )
    return [new_first, new_second, new_master]


def swapped(value, axis):
    return lax.ppermute(value, axis, [(0, 1), (1, 0)])


def grouped(buffer, sections):
    if buffer.shape[0] == GROUPS:
        return buffer
    parts, at = [], 0
    for count in sections:
        parts.append(buffer[:, at : at + count].reshape(GROUPS, -1, buffer.shape[2]))
        at += count
    return jnp.concatenate(parts, 1)


def matmul_packed(value, buffer, rows, first, count):
    size, depth = value.shape

    def body(value_ref, weight_ref, out):
        weight = weight_ref[...].reshape(depth, PIECE)
        out[...] = matmul(value_ref[...], weight).astype(BF16)

    return pl.pallas_call(
        body,
        grid=(count, 2),
        in_specs=[
            pl.BlockSpec((size, depth), lambda j, h: (0, 0)),
            pl.BlockSpec((GROUPS, rows, PIECE), lambda j, h: (0, first + j, h)),
        ],
        out_specs=pl.BlockSpec((size, PIECE), lambda j, h: (0, 2 * j + h)),
        out_shape=jax.ShapeDtypeStruct((size, count * 2 * PIECE), BF16),
        compiler_params=pltpu.CompilerParams(vmem_limit_bytes=48 << 20),
        cost_estimate=pl.CostEstimate(
            flops=4 * size * depth * count * PIECE,
            bytes_accessed=2 * depth * count * 1024,
            transcendentals=0,
        ),
        name="matmul_packed",
    )(value, buffer)


def matmul_packed_back(grads, buffer, rows, first, start=None):
    count, size, width = grads.shape
    depth = GROUPS * rows
    extra = [] if start is None else [start]

    def body(grad_ref, weight_ref, *rest):
        out = rest[-1]

        @pl.when(pl.program_id(0) == 0)
        def _():
            out[...] = jnp.zeros(out.shape, F32) if start is None else rest[0][...]

        out[...] += matmul_nt(grad_ref[0], weight_ref[...].reshape(depth, width))

    return pl.pallas_call(
        body,
        grid=(count,),
        in_specs=[
            pl.BlockSpec((1, size, width), lambda j: (j, 0, 0)),
            pl.BlockSpec((GROUPS, rows, width), lambda j: (0, first + j, 0)),
        ]
        + [pl.BlockSpec((size, depth), lambda j: (0, 0)) for _ in extra],
        out_specs=pl.BlockSpec((size, depth), lambda j: (0, 0)),
        out_shape=jax.ShapeDtypeStruct((size, depth), F32),
        compiler_params=pltpu.CompilerParams(vmem_limit_bytes=48 << 20),
        cost_estimate=pl.CostEstimate(
            flops=2 * size * depth * count * width,
            bytes_accessed=2 * depth * count * width,
            transcendentals=0,
        ),
        name="matmul_packed_back",
    )(grads, buffer, *extra)


GELU_SCALE = 0.7978845608028654
GELU_CUBE = 0.044715


def feed_forward(value, buffer, residual, chunk):
    size, width = value.shape
    blocks = (buffer.shape[1] - BLOCK) * GROUPS // width
    lines = width // (8 * chunk)

    def body(value_ref, first_ref, second_ref, residual_ref, out, pre, turned):
        hidden = matmul(value_ref[...], first_ref[...].reshape(width, width))
        pre[...] = hidden
        inner = jnp.tanh(GELU_SCALE * (hidden + GELU_CUBE * hidden * hidden * hidden))
        active = (0.5 * hidden * (1.0 + inner)).astype(BF16)

        @pl.when(pl.program_id(0) == 0)
        def _():
            out[...] = residual_ref[...]

        out[...] += matmul(active, second_ref[...].reshape(width, width))
        columns = active.T
        for line in range(lines):
            for place in range(8):
                target = place % 2 * 4 + place // 2
                at = (line * 8 + place) * chunk
                turned[target, line * chunk : (line + 1) * chunk] = columns[at : at + chunk]

    return pl.pallas_call(
        body,
        grid=(blocks,),
        in_specs=[
            pl.BlockSpec((size, width), lambda j: (0, 0)),
            pl.BlockSpec((GROUPS, width // GROUPS, width), lambda j: (0, j, 0)),
            pl.BlockSpec((width // BLOCK, BLOCK, width), lambda j: (j, 1, 0)),
            pl.BlockSpec((size, width), lambda j: (0, 0)),
        ],
        out_specs=[
            pl.BlockSpec((size, width), lambda j: (0, 0)),
            pl.BlockSpec((size, width), lambda j: (0, j)),
            pl.BlockSpec((8, width // 8, size), lambda j: (0, j, 0)),
        ],
        out_shape=[
            jax.ShapeDtypeStruct((size, width), F32),
            jax.ShapeDtypeStruct((size, blocks * width), F32),
            jax.ShapeDtypeStruct((8, blocks * width // 8, size), BF16),
        ],
        compiler_params=pltpu.CompilerParams(vmem_limit_bytes=56 << 20),
        cost_estimate=pl.CostEstimate(
            flops=4 * size * width * width * blocks,
            bytes_accessed=32 << 20,
            transcendentals=size * width * blocks,
        ),
        name="feed_forward",
    )(value, buffer, buffer, residual)


def feed_forward_back(grad, pre, buffer):
    size, width = grad.shape
    blocks = pre.shape[1] // width

    def body(grad_ref, pre_ref, first_ref, second_ref, grad_pre, out):
        grad_active = matmul_nt(grad_ref[...], second_ref[...].reshape(width, width))
        hidden = pre_ref[...]
        square = hidden * hidden
        inner = jnp.tanh(GELU_SCALE * hidden * (1.0 + GELU_CUBE * square))
        slope = 0.5 * (1.0 + inner) + 0.5 * hidden * (1.0 - inner * inner) * GELU_SCALE * (
            1.0 + 3.0 * GELU_CUBE * square
        )
        back = (grad_active * slope).astype(BF16)
        grad_pre[...] = back

        @pl.when(pl.program_id(0) == 0)
        def _():
            out[...] = jnp.zeros(out.shape, F32)

        out[...] += matmul_nt(back, first_ref[...].reshape(width, width))

    return pl.pallas_call(
        body,
        grid=(blocks,),
        in_specs=[
            pl.BlockSpec((size, width), lambda j: (0, 0)),
            pl.BlockSpec((size, width), lambda j: (0, j)),
            pl.BlockSpec((GROUPS, width // GROUPS, width), lambda j: (0, j, 0)),
            pl.BlockSpec((width // BLOCK, BLOCK, width), lambda j: (j, 1, 0)),
        ],
        out_specs=[
            pl.BlockSpec((size, width), lambda j: (0, j)),
            pl.BlockSpec((size, width), lambda j: (0, 0)),
        ],
        out_shape=[
            jax.ShapeDtypeStruct((size, blocks * width), BF16),
            jax.ShapeDtypeStruct((size, width), F32),
        ],
        compiler_params=pltpu.CompilerParams(vmem_limit_bytes=56 << 20),
        cost_estimate=pl.CostEstimate(
            flops=4 * size * width * width * blocks,
            bytes_accessed=32 << 20,
            transcendentals=size * width * blocks,
        ),
        name="feed_forward_back",
    )(grad, pre, buffer, buffer)


def grouped_transpose(rows):
    tokens, columns = rows.shape
    line = lax.axis_size(LINE)
    split = rows.reshape(tokens, line, 2, 2, 2, columns // (line * 8))
    return split.transpose(4, 2, 3, 1, 5, 0).reshape(8, columns // 8, tokens)


def core_halves(grouped):
    core = lax.axis_index("core")
    mine = lax.dynamic_slice_in_dim(grouped, 4 * core, 4, 0)
    other = lax.dynamic_slice_in_dim(grouped, 4 * (1 - core), 4, 0)
    return mine, swapped(other, "core")


def gradient_piece(weights, place, half, axis, moved, dtype):
    operands, specs, plan = [], [], []
    first = 0
    for products, blocks, wide in weights:
        for own, other, rhs_own, rhs_other, lead in products:
            tokens = own.shape[2]

            def inner(step, first=first, blocks=blocks):
                return jnp.clip(step - first, 0, blocks - 1)

            for side in (own, other):
                for free in (0, 1):
                    flip = 2 * free + moved if axis == "x" else 2 * moved + free

                    def lhs_map(step, me, flip=flip, inner=inner, wide=wide):
                        return (me[0] ^ flip, 0 if wide else inner(step), 0)

                    operands.append(side)
                    specs.append(pl.BlockSpec((1, BLOCK, tokens), lhs_map))
            for side in (rhs_own, rhs_other):

                def rhs_map(step, me, inner=inner, wide=wide, lead=lead):
                    return (lead, 0, 2 * inner(step) + half if wide else half)

                operands.append(side)
                specs.append(pl.BlockSpec((1, tokens, PIECE), rhs_map))
        plan.append((first, blocks, len(products)))
        first += blocks

    def body(me, *refs):
        out = refs[-1]
        step = pl.program_id(0)
        at = 0
        for start, blocks, count in plan:
            group = refs[at : at + 6 * count]

            @pl.when((step >= start) & (step < start + blocks))
            def _():
                total = jnp.zeros((2 * BLOCK, PIECE), F32)
                for k in range(0, 6 * count, 6):
                    near = jnp.concatenate([group[k][0], group[k + 1][0]], 0)
                    far = jnp.concatenate([group[k + 2][0], group[k + 3][0]], 0)
                    total += matmul(near, group[k + 4][0]) + matmul(far, group[k + 5][0])
                out[0] = total.astype(out.dtype)

            at += 6 * count

    return pl.pallas_call(
        body,
        grid_spec=pltpu.PrefetchScalarGridSpec(
            num_scalar_prefetch=1,
            grid=(first,),
            in_specs=specs,
            out_specs=pl.BlockSpec((1, 2 * BLOCK, PIECE), lambda step, me: (step, 0, 0)),
        ),
        out_shape=jax.ShapeDtypeStruct((first, 2 * BLOCK, PIECE), dtype),
        compiler_params=pltpu.CompilerParams(vmem_limit_bytes=40 << 20),
        cost_estimate=pl.CostEstimate(
            flops=first * 2 * 2 * BLOCK * PIECE * 1024,
            bytes_accessed=first * (3 << 20),
            transcendentals=0,
        ),
        name="gradient_piece",
    )(place, *operands)


def line_scatter(value):
    count = lax.axis_size(LINE)
    index = lax.axis_index(LINE)
    total = lax.dynamic_index_in_dim(value, index, 0, False)
    upward = downward = jnp.zeros(total.shape, F32)
    for steps in range(count - 1, 0, -1):
        above = lax.dynamic_index_in_dim(value, jnp.minimum(index + steps, count - 1), 0, False)
        below = lax.dynamic_index_in_dim(value, jnp.maximum(index - steps, 0), 0, False)
        up = [(i, i + 1) for i in range(count - steps)]
        down = [(i, i - 1) for i in range(steps, count)]
        upward = lax.ppermute((above + upward).astype(BF16), LINE, up).astype(F32)
        downward = lax.ppermute((below + downward).astype(BF16), LINE, down).astype(F32)
    return total + upward + downward


def chip_place():
    place = lax.axis_index("y") * 2 + lax.axis_index("x")
    return jnp.reshape(place, (1,)).astype(jnp.int32)


def gradient_sends(weights):
    return [
        gradient_piece(weights, chip_place(), 0, "x", 1, BF16),
        gradient_piece(weights, chip_place(), 1, "y", 1, BF16),
    ]


def gradient_keeps(weights):
    return [
        gradient_piece(weights, chip_place(), 0, "x", 0, F32),
        gradient_piece(weights, chip_place(), 1, "y", 0, F32),
    ]


def plane_sums(sends, keeps):
    result = []
    for arrived, keep in zip(sends, keeps):
        count = keep.shape[1] // 2
        other = (keep[:, count:] + arrived[:, count:].astype(F32)).astype(BF16)
        result.append((keep[:, :count] + arrived[:, :count].astype(F32), other))
    return result


def line_parts(weights, sums):
    line = lax.axis_size(LINE)
    joined = [
        mine + swapped(other, axis).astype(F32) for (mine, other), axis in zip(sums, ("y", "x"))
    ]
    first, chunks = 0, []
    for weight in weights:
        blocks, wide = weight[1:]
        for part in range(blocks if wide else 1):
            count = 1 if wide else blocks
            pair = [
                half[first : first + count].reshape(line, count * BLOCK // line, PIECE)
                for half in joined
            ]
            chunks.append(jnp.concatenate(pair, -1))
            first += count
    return jnp.concatenate(chunks, 1)


def small_sum(value):
    for axis in ("core", "x", "y"):
        value = value + swapped(value, axis)
    count = lax.axis_size(LINE)
    step = 1
    while step < count:
        pairs = [(i, i ^ step) for i in range(count)]
        value = value + lax.ppermute(value, LINE, pairs)
        step *= 2
    return value


def spread_body(row_of, token_row, grads, table_grad, *refs):
    outs, total = refs[:2], refs[2]
    task, step = pl.program_id(0), pl.program_id(1)
    rows, tokens = total.shape[0], grads.shape[0]
    first = row_of(task) * rows

    @pl.when(step == 0)
    def _():
        total[...] = table_grad[0]

    wanted = token_row[...] - first
    hit = lax.broadcasted_iota(jnp.int32, (rows, tokens), 0) == wanted
    total[...] += matmul(jnp.where(hit, 1.0, 0.0).astype(BF16), grads[...])

    for side in (0, 1):

        @pl.when((step == pl.num_programs(1) - 1) & (task // 2 == side))
        def _():
            outs[side][0] = total[...].astype(outs[side].dtype)


def spread_piece(token_row, grads, table_grad, row_of, dtype):
    blocks, rows, width = table_grad.shape
    tokens = 1024

    def body(*refs):
        spread_body(row_of, *refs)

    return pl.pallas_call(
        body,
        grid=(4, grads.shape[0] // tokens),
        in_specs=[
            pl.BlockSpec((1, tokens), lambda task, step: (0, step)),
            pl.BlockSpec((tokens, PIECE), lambda task, step: (step, task // 2)),
            pl.BlockSpec((1, rows, PIECE), lambda task, step: (row_of(task), 0, task // 2)),
        ],
        out_specs=[
            pl.BlockSpec((1, rows, PIECE), lambda task, step: (jnp.minimum(task, 1), 0, 0)),
            pl.BlockSpec((1, rows, PIECE), lambda task, step: (jnp.maximum(task - 2, 0), 0, 0)),
        ],
        out_shape=[jax.ShapeDtypeStruct((2, rows, PIECE), dtype)] * 2,
        scratch_shapes=[pltpu.VMEM((rows, PIECE), F32)],
        compiler_params=pltpu.CompilerParams(vmem_limit_bytes=48 << 20),
        cost_estimate=pl.CostEstimate(
            flops=4 * 2 * rows * PIECE * grads.shape[0],
            bytes_accessed=24 << 20,
            transcendentals=0,
        ),
        name="spread_piece",
    )(token_row, grads, table_grad)


def column_blocks(rows):
    return jnp.concatenate(jnp.split(rows, rows.shape[1] // MODEL_WIDTH, 1), 0)


def bf16_parts(values):
    high = values.astype(BF16)
    rest = values - high.astype(F32)
    middle = rest.astype(BF16)
    low = (rest - middle.astype(F32)).astype(BF16)
    return high, middle, low


def per_device(token_ids, book_lengths, loss_mask, *state):
    masters, firsts, seconds = state[:7], state[7:14], state[14:]
    table_master, attn_in_m, attn_out_m, compress_m, ffn_in_m, ffn_out_m, gains_m = masters
    vocab_block = table_master.shape[0]
    batch_count = lax.axis_size("batch")
    seq_count = lax.axis_size(SEQ)
    plane_count = seq_count // 2
    share_count = batch_count * 2
    device_count = batch_count * seq_count
    segment = token_ids.shape[1]
    slots = -(-(segment // 3 + 1) // 16) * 16
    keep = segment // 2
    place = lax.axis_index(SEQ)
    offset = place * segment
    share_place = lax.axis_index(SHARE)
    width = MODEL_WIDTH

    own_tokens = token_ids.reshape(segment)
    share_tokens = lax.all_gather(own_tokens, SHARE, axis=0, tiled=True)
    own_table = lax.all_gather(table_master.astype(BF16), "far", axis=0, tiled=True)
    table_x, table_y = swapped(own_table, "x"), swapped(own_table, "y")
    part_rows = own_table.shape[0]
    table = jnp.zeros((4 * part_rows, width), BF16)
    for value, row, column in (
        (own_table, 0, 0),
        (table_x, 1, 0),
        (table_y, 2, 0),
        (swapped(table_x[:, :PIECE], "y"), 3, 0),
        (swapped(table_y[:, PIECE:], "x"), 3, PIECE),
    ):
        table = lax.dynamic_update_slice(table, value, (row * part_rows, column))

    def vocab_place(tokens):
        block = tokens // vocab_block
        seq_index = block % seq_count
        owner = block // seq_count * 2 + seq_index % 2
        chip = seq_index // 2 % 4
        part = chip ^ (lax.axis_index("y") * 2 + lax.axis_index("x"))
        inside = seq_index // 8 * vocab_block + tokens % vocab_block
        return owner, part * part_rows + inside

    share_owner, share_local = vocab_place(share_tokens)
    share_row = jnp.where(share_owner == share_place, share_local, -1)
    looked = jnp.where(
        (share_row >= 0)[:, None], table[jnp.maximum(share_row, 0)], jnp.zeros((), BF16)
    )

    rows_in = attn_in_m.size // width
    rows_out = attn_out_m.size // width
    rows_comp = compress_m.size // width
    rows_ffn = ffn_in_m.size // width
    rows_ffn_out = ffn_out_m.size // width
    gain_count = gains_m.size
    gain_block = jnp.zeros((16, width), BF16).at[0, :gain_count].set(
        gains_m.astype(BF16).reshape(-1)
    )
    mixer_block = jnp.concatenate(
        [
            column_blocks(attn_in_m.astype(BF16)),
            compress_m.astype(BF16),
            attn_out_m.astype(BF16),
            gain_block,
        ],
        0,
    )
    ffn_block = jnp.concatenate(
        [column_blocks(ffn_in_m.astype(BF16)), ffn_out_m.astype(BF16)], 0
    )
    mixer_all = lax.all_gather(mixer_block, ALL, axis=0, tiled=False)
    ffn_all = lax.all_gather(ffn_block, ALL, axis=0, tiled=False)
    token_rows = lax.psum_scatter(looked, SHARE, scatter_dimension=0, tiled=True)
    gains = mixer_all[:, rows_in + rows_comp + rows_out, :gain_count]
    gains = gains.reshape(width, 3).astype(F32)
    part = attn_in_m.shape[0]
    mixer_all = grouped(mixer_all, (part, part, part, rows_comp, rows_out, 16))
    ffn_all = grouped(ffn_all, (part,) * (rows_ffn // part) + (rows_ffn_out,))
    thin = width // GROUPS

    book_ends = jnp.cumsum(book_lengths.reshape(-1))
    own_pos = offset + jnp.arange(segment, dtype=jnp.int32)
    own_book = book_number(own_pos, book_ends)
    next_book = book_number(own_pos + 1, book_ends)
    own_mask = loss_mask.reshape(segment)
    numbers = jnp.arange(NBOOK, dtype=jnp.int32)
    live = own_mask.astype(F32) * (next_book == own_book).astype(F32)
    member = (own_book[:, None] == numbers[None, :]).astype(F32)
    book_counts = jnp.sum(member * live[:, None], 0)
    for axis in ("core", "x", "y"):
        book_counts = book_counts + swapped(book_counts, axis)
    book_counts = lax.psum(book_counts, "far")
    weight = live * jnp.sum(member / jnp.maximum(book_counts, 1.0)[None, :], -1)
    following = passed_along(own_tokens[:1], -1)
    targets = jnp.concatenate([own_tokens[1:], following])
    rank = jnp.cumsum(own_mask) - 1
    chosen = (rank[None, :] == jnp.arange(keep, dtype=jnp.int32)[:, None]) & (
        own_mask[None, :] > 0
    )
    picked_targets = jnp.sum(jnp.where(chosen, targets[None, :], 0), 1)
    picked_weight = jnp.sum(jnp.where(chosen, weight[None, :], 0.0), 1)

    embedded = token_rows.astype(F32) * width**0.5
    normed_one, unit_one, scale_one = norm_forward(embedded, gains[:, 0])
    attention_input = normed_one.astype(BF16)
    projected = matmul_packed(attention_input, mixer_all, thin, 0, 3)
    memory_rows = passed_along(attention_input, 1)
    tail_rows = passed_along(attention_input[segment - 2 :], 1)
    first_cell = jnp.mod(2 - offset, 3)
    padding = 3 * slots - segment + 2
    extended = jnp.concatenate([tail_rows, attention_input, jnp.zeros((padding, width), BF16)], 0)
    slot_rows = lax.dynamic_slice_in_dim(extended, first_cell, 3 * slots, 0).reshape(
        slots, 3 * width
    )
    compressed = matmul_packed(slot_rows, mixer_all, 3 * thin, 1, 1)
    other_rows = [memory_rows]
    book_parts = [own_book, book_number(own_pos - segment, book_ends)]
    pos_parts = [own_pos, own_pos - segment]
    for hop in (2, 3, 4):
        other_rows.append(passed_along(compressed, hop))
        owner = place - hop
        last_pos = (
            owner * segment
            + jnp.mod(2 - owner * segment, 3)
            + 3 * jnp.arange(slots, dtype=jnp.int32)
        )
        last_book = book_number(last_pos, book_ends)
        usable = (owner >= 0) & (last_pos < owner * segment + segment)
        usable = usable & (book_number(last_pos - 2, book_ends) == last_book)
        book_parts.append(jnp.where(usable, last_book, -2))
        pos_parts.append(jnp.full((slots,), -1, jnp.int32))
    marks = (
        jnp.concatenate(book_parts)[:, None],
        jnp.concatenate(pos_parts)[:, None],
        own_book[None, :],
        own_pos[None, :],
    )
    memory_pairs = matmul_packed(jnp.concatenate(other_rows, 0), mixer_all, thin, 1, 2)
    attended, log_total = attention_forward(projected, memory_pairs, marks)
    w_out = mixer_all[:, 6 * thin : 7 * thin].reshape(width, width)
    residual = embedded + matmul(attended, w_out)

    normed_two, unit_two, scale_two = norm_forward(residual, gains[:, 1])
    ffn_input = normed_two.astype(BF16)
    output_rows, pre_act, activated_turned = feed_forward(
        ffn_input, ffn_all, residual, rows_ffn_out
    )
    normed_three, unit_three, scale_three = norm_forward(output_rows, gains[:, 2])
    final_rows = normed_three.astype(BF16)

    chosen_bf16 = chosen.astype(BF16)
    picked_rows = matmul(chosen_bf16, final_rows).astype(BF16)
    high, middle, low = bf16_parts(picked_weight)
    side = jnp.concatenate(
        [
            (picked_targets // 256).astype(BF16),
            (picked_targets % 256).astype(BF16),
            high,
            middle,
            low,
        ]
    )
    side_rows = jnp.zeros((16 * width,), BF16).at[: 5 * keep].set(side).reshape(16, width)
    head_all = lax.all_gather(
        jnp.concatenate([picked_rows, side_rows], 0), SHARE, axis=0, tiled=False
    )
    spare = -slots % BLOCK
    comp_tall = jnp.concatenate([compressed, jnp.zeros((spare, width), BF16)], 0)
    slot_tall = jnp.concatenate([slot_rows, jnp.zeros((spare, 3 * width), BF16)], 0)
    halves = [
        core_halves(value)
        for value in (
            grouped_transpose(ffn_input),
            activated_turned,
            grouped_transpose(attention_input),
            grouped_transpose(comp_tall),
            grouped_transpose(slot_tall),
            grouped_transpose(attended),
        )
    ]
    rows = head_all[:, :keep].reshape(share_count * keep, width)
    rows, halves = lax.optimization_barrier((rows, halves))
    side_all = head_all[:, keep:].reshape(share_count, 16 * width)[:, : 5 * keep]
    side_all = side_all.reshape(share_count, 5, keep).astype(F32)
    wanted = (side_all[:, 0] * 256.0 + side_all[:, 1]).astype(jnp.int32).reshape(-1)
    row_weight = (side_all[:, 2] + side_all[:, 3] + side_all[:, 4]).reshape(-1)
    wanted_owner, wanted_local = vocab_place(wanted)
    wanted_row = jnp.where(wanted_owner == share_place, wanted_local, -1)
    logits = matmul_nt(rows, table)
    top_logit = jnp.max(logits, -1)
    total = jnp.sum(jnp.exp(logits - top_logit[:, None]), -1)
    stats = lax.all_gather(jnp.stack([top_logit, total]), SHARE, axis=0, tiled=False)
    top_all = jnp.max(stats[:, 0], 0)
    log_norm = top_all + jnp.log(jnp.sum(stats[:, 1] * jnp.exp(stats[:, 0] - top_all[None]), 0))
    hit = wanted_row[:, None] == jnp.arange(logits.shape[1], dtype=jnp.int32)[None, :]
    target_logit = jnp.sum(jnp.where(hit, logits, 0.0), -1)
    mine = (jnp.arange(share_count * keep) // keep == share_place).astype(F32)
    loss_local = jnp.sum(row_weight * (mine * log_norm - target_logit))
    grad_logits = row_weight[:, None] * (
        jnp.exp(logits - log_norm[:, None]) - hit.astype(F32)
    )
    grad_logits = grad_logits.astype(BF16)
    grad_rows = matmul(grad_logits, table).astype(BF16)
    grad_table = matmul_tn(grad_logits, rows)
    grad_picked = lax.psum_scatter(grad_rows, SHARE, scatter_dimension=0, tiled=True)
    grad_picked, grad_table = lax.optimization_barrier((grad_picked, grad_table))
    grad_final = matmul_tn(chosen_bf16, grad_picked)

    grad_output_rows, grad_gain_three = norm_backward(
        grad_final, unit_three, scale_three, gains[:, 2]
    )
    grad_branch = grad_output_rows.astype(BF16)
    grad_pre, grad_norm_two = feed_forward_back(grad_branch, pre_act, ffn_all)

    def product(pair, grad, lead=0):
        return pair + (grad[0], grad[1], lead)

    def with_other(grad):
        grad = grad if grad.ndim == 3 else grad[None]
        return grad, swapped(grad, "core")

    ffn_weights = [
        ([product(halves[0], with_other(grad_pre))], ffn_in_m.shape[1] // width, True),
        (
            [product(halves[1], with_other(grad_branch))],
            rows_ffn_out * device_count // width,
            False,
        ),
    ]
    grad_res_two, grad_gain_two = norm_backward(grad_norm_two, unit_two, scale_two, gains[:, 1])
    grad_residual = grad_output_rows + grad_res_two

    grad_attn_branch = grad_residual.astype(BF16)
    grad_attended = matmul_nt(grad_attn_branch, w_out).astype(BF16)
    ffn_sends = gradient_sends(ffn_weights)
    *ffn_sends, grad_attended = lax.optimization_barrier((*ffn_sends, grad_attended))
    ffn_arrived = [swapped(send, axis) for send, axis in zip(ffn_sends, ("x", "y"))]
    grad_query, grad_own, grad_memory, *grad_comps = attention_backward(
        projected, memory_pairs, marks, log_total, grad_attended
    )
    back_memory = passed_along(grad_memory, -1)
    ffn_keeps = gradient_keeps(ffn_weights)
    received = jnp.zeros((2, slots, width), F32)
    for hop, grad_comp in zip((2, 3, 4), grad_comps):
        received = received + passed_along(grad_comp, -hop).astype(F32)
    received = received.astype(BF16)
    ffn_sums = plane_sums(ffn_arrived, ffn_keeps)
    ffn_sums, grad_comp_pairs = lax.optimization_barrier((ffn_sums, received))
    ffn_parts = line_parts(ffn_weights, ffn_sums)
    grad_compressed = matmul_packed_back(grad_comp_pairs, mixer_all, thin, 1).astype(BF16)
    grad_slots = matmul_packed_back(grad_compressed[None], mixer_all, 3 * thin, 1)
    grad_slots = grad_slots.reshape(3 * slots, width)
    grad_first = jnp.concatenate([jnp.zeros((2, width), F32), grad_slots[:2]], 0)
    grad_first = lax.dynamic_slice_in_dim(grad_first, 2 - first_cell, 2, 0)
    back_tail = passed_along(grad_first.astype(BF16), -1).astype(F32)
    grad_own_pairs = (grad_own + back_memory.astype(F32)).astype(BF16)
    grad_input = matmul_packed_back(grad_query[None], mixer_all, thin, 0)
    grad_input = matmul_packed_back(grad_own_pairs, mixer_all, thin, 1, grad_input)
    grad_input = grad_input + lax.dynamic_slice_in_dim(grad_slots, 2 - first_cell, segment, 0)
    grad_input = grad_input.at[segment - 2 :].add(back_tail)
    grad_embed, grad_gain_one = norm_backward(grad_input, unit_one, scale_one, gains[:, 0])
    grad_scaled = ((grad_embed + grad_residual) * width**0.5).astype(BF16)

    share_grads = lax.all_gather(grad_scaled, SHARE, axis=0, tiled=True)
    query_pair, own_pair = with_other(grad_query), with_other(grad_own_pairs)
    comp_pair = with_other(jnp.pad(grad_comp_pairs, ((0, 0), (0, spare), (0, 0))))
    slot_pair = with_other(jnp.pad(grad_compressed, ((0, spare), (0, 0))))
    mixer_weights = [
        ([product(halves[2], query_pair)], 1, True),
        ([product(halves[2], own_pair, 0), product(halves[3], comp_pair, 0)], 1, True),
        ([product(halves[2], own_pair, 1), product(halves[3], comp_pair, 1)], 1, True),
        ([product(halves[4], slot_pair)], 3, False),
        ([product(halves[5], with_other(grad_attn_branch))], 1, True),
    ]
    mixer_sends = gradient_sends(mixer_weights)
    mixer_arrived = [swapped(send, axis) for send, axis in zip(mixer_sends, ("x", "y"))]
    mixer_keeps = gradient_keeps(mixer_weights)
    ffn_grads = line_scatter(ffn_parts)
    table_parts = grad_table.reshape(4, part_rows, width)
    token_row, mixer_keeps, ffn_grads = lax.optimization_barrier(
        (share_row[None, :], mixer_keeps, ffn_grads)
    )
    table_sends = spread_piece(
        token_row, share_grads, table_parts, lambda t: jnp.where(t < 2, 2 * t + 1, t), BF16
    )
    table_sends, mixer_keeps = lax.optimization_barrier((table_sends, mixer_keeps))
    table_arrived = [swapped(send, axis) for send, axis in zip(table_sends, ("x", "y"))]
    table_keeps = spread_piece(
        token_row, share_grads, table_parts, lambda t: jnp.where(t < 2, 2 * t, t - 2), F32
    )
    mixer_sums = plane_sums(mixer_arrived, mixer_keeps)
    mixer_grads = line_scatter(line_parts(mixer_weights, mixer_sums))
    halves_new = []
    for arrived, keep_part, axis in zip(table_arrived, table_keeps, ("y", "x")):
        other = (keep_part[1] + arrived[1].astype(F32)).astype(BF16)
        mine = keep_part[0] + arrived[0].astype(F32)
        halves_new.append(mine + swapped(other, axis).astype(F32))
    grad_table = jnp.concatenate(halves_new, 1)
    if lax.axis_size("far") > 1:
        grad_table = lax.psum_scatter(
            grad_table.astype(BF16), "far", scatter_dimension=0, tiled=True
        )

    small = jnp.concatenate(
        [
            jnp.stack([grad_gain_one, grad_gain_two, grad_gain_three], 1).reshape(-1),
            jnp.full((128,), loss_local, F32),
        ]
    )
    small = small_sum(small)
    loss_total = small[3 * width]
    device = lax.axis_index(ALL)
    gain_grads = lax.dynamic_slice_in_dim(small, device * gain_count, gain_count, 0)

    def side_by_side(rows, count):
        return jnp.concatenate(jnp.split(rows, count, 0), 1)

    low, high = rows_in, rows_in + rows_comp
    grads = (
        grad_table,
        side_by_side(mixer_grads[:low], 3),
        mixer_grads[high:],
        mixer_grads[low:high],
        side_by_side(ffn_grads[:rows_ffn], rows_ffn // attn_in_m.shape[0]),
        ffn_grads[rows_ffn:],
        gain_grads.reshape(gains_m.shape),
    )
    results = []
    for master, first, second, grad, rate in zip(masters, firsts, seconds, grads, STEP_RATES):
        results.extend(adam_update(master, first, second, grad.astype(F32), rate))
    return (loss_total,) + tuple(results)


def solution(mesh):
    batch_count, seq_count = mesh.shape["batch"], mesh.shape["seq"]
    devices = mesh.devices.reshape(batch_count, seq_count // 8, 2, 2, 2)
    grid = Mesh(devices, ALL)
    rows = P(ALL, None)
    return jax.shard_map(
        per_device,
        mesh=grid,
        in_specs=(P("batch", SEQ), P("batch", None), P("batch", SEQ)) + (rows,) * 21,
        out_specs=(P(),) + (rows,) * 21,
        check_vma=False,
    )
```

time: 1540 us -> 1160 us (0.75)
  matrix products: 379 us -> 84.3 us
  waiting for transfers between devices: 714 us -> 444 us
  Pallas kernels: 0 us -> 226 us
  starting transfers between devices: 23.3 us -> 134 us
  local copies, waits for them, and re-layouts: 203 us -> 109 us
  blocking collectives: 86.1 us -> 27.1 us
    pallas_call x0 -> x21, Pallas kernels: none -> 226 us  [the longest x8 60.7 us: gradient_piece(): pl.pallas_call(body, grid_spec=pltpu.PrefetchScalarGridSpec(num_scalar_pr...]
    reduce_scatter x2 -> x0, waiting for transfers between devices: 175 us -> none  [the longest x1 175 us: per_device(): lax.psum_scatter(ffn_grads, ALL, scatter_dimension=0, tiled=False)]
    ppermute x0 -> x49, waiting for transfers between devices: none -> 163 us  [the longest x35 112 us: swapped(): return lax.ppermute(value, axis, [(0, 1), (1, 0)])]
    dot_general x6 -> x0, matrix products: 134 us -> none  [the longest x1 42.1 us: per_device(): jnp.einsum('hqk,khd->qhd', grad_scores, split_heads(key_side[:, :width]),...]
    ppermute x0 -> x49, starting transfers between devices: none -> 98.4 us  [the longest x35 59.4 us: swapped(): return lax.ppermute(value, axis, [(0, 1), (1, 0)])]
    dot_general x9 -> x3, matrix products: 111 us -> 27.2 us  [matmul(): return jnp.dot(left, right, preferred_element_type=F32)]
    unnamed x11 -> x6, waiting for transfers between devices: 78.7 us -> 0.1 us
    all_gather x1 -> x0, waiting for transfers between devices: 73.6 us -> none  [per_device(): table = lax.all_gather(table_master.astype(BF16), PLANE, axis=0, tiled=True)]
  transfers between devices with their start and end apart: 21 -> 66, of which waited for: 10 -> 31; matrix products, arithmetic and copies ran while one was open for 22% -> 13% of each run, Pallas kernels for 0% -> 15%
where the time goes in v2:
time: 1160 us; the launch traced here: 1150 us
  waiting for transfers between devices  444 us (38%)
  Pallas kernels  226 us (19%)
  starting transfers between devices  134 us (12%)
  local copies, waits for them, and re-layouts  109 us (9%)
  other arithmetic  104 us (9%)
  matrix products  84.3 us (7%)
  blocking collectives  27.1 us (2%)
  between operations  18.2 us (2%)
    ppermute x35, waiting for transfers between devices, swapped(): return lax.ppermute(value, axis, [(0, 1), (1, 0)])  112 us
    reduce_scatter x1, waiting for transfers between devices, per_device(): lax.psum_scatter(looked, SHARE, scatter_dimension=0, tiled=True)  98.2 us
    pallas_call x8, Pallas kernels, gradient_piece(): pl.pallas_call(body, grid_spec=pltpu.PrefetchScalarGridSpec(num_scalar_pr...  60.7 us
    ppermute x35, starting transfers between devices, swapped(): return lax.ppermute(value, axis, [(0, 1), (1, 0)])  59.4 us
    all_gather x1, waiting for transfers between devices, per_device(): mixer_all = lax.all_gather(mixer_block, ALL, axis=0, tiled=False)  54.3 us
    pallas_call x2, Pallas kernels, spread_piece(): pl.pallas_call(body, grid=(4, grads.shape[0] // tokens), in_specs=[pl.Blo...  51.5 us
    ppermute x6, waiting for transfers between devices, line_scatter(): upward = lax.ppermute((above + upward).astype(BF16), LINE, up).astype(F32)  46.6 us
    ppermute x11, waiting for transfers between devices, passed_along(): lax.ppermute(value, SEQ, [(source, source + steps) for source in range(in...  43.6 us
  transfers between devices with their start and end apart: 66, of which 31 were waited for; matrix products, arithmetic and copies ran while one was open for 13% of the time, Pallas kernels for 15%

profile of v2, /device:TPU:0, one launch (start us, length us, event | category | flops | bytes accessed | tf_op | source)
XLA Modules:
  0.0 1146.5 jit_solution(1376874127684449883)
XLA Ops:
  28.0 30.1 %collective-permute-done = bf16[1000,1024]{1,0:T(8,128)(2,1)S(1)} collective-permute-done((bf16[1000,1024]{1,0:T(8,128)(2,1)S(1)}, bf16[1000,1024]{1,0:T(8,128)(2,1)S(1)}, u32[]{:S(2)}, u32[]{:S(2)}) %collective-permute-start) | collective-permute-done | bytes 2048032 | tf_op jit(solution)/shard_map/ppermute | solution.py:211
  92.6 25.2 %gather_fusion = bf16[4096,1024]{1,0:T(8,128)(2,1)} fusion(bf16[4000,1024]{1,0:T(8,128)(2,1)} %constant_dynamic-update-slice_fusion.6, s32[4096]{0:T(1024)S(1)} %maximum_clamp_fusion), kind=kCustom, calls=%fused_computation | custom fusion | bytes 16793600 | tf_op jit(solution)/shard_map/gather | solution.py:650
  143.3 98.2 %reduce-scatter.3.cloned.1.call-done = bf16[512,1024]{1,0:T(8,128)(2,1)} async-done(((bf16[4096,1024]{1,0:T(8,128)(2,1)}), bf16[512,1024]{1,0:T(8,128)(2,1)}) %reduce-scatter.3.cloned.1.call-update) | async-done | bytes 1048592 | tf_op jit(solution)/shard_map/reduce_scatter | solution.py:676
  244.8 54.3 %all-gather.13.cloned.1.call-done = bf16[7680,1024]{1,0:T(8,128)(2,1)} async-done(((bf16[240,1024]{1,0:T(8,128)(2,1)}), bf16[7680,1024]{1,0:T(8,128)(2,1)}) %all-gather.13.cloned.1.call-update) | async-done | bytes 15728656 | tf_op jit(solution)/shard_map/all_gather | solution.py:674
  315.0 18.8 %collective-permute-start.8 = (bf16[176,1024]{1,0:T(8,128)(2,1)S(1)}, bf16[176,1024]{1,0:T(8,128)(2,1)}, u32[]{:S(2)}, u32[]{:S(2)}) collective-permute-start(bf16[176,1024]{1,0:T(8,128)(2,1)S(1)} %matmul_packed.4), channel_id=1, source_target_pairs={{0,4},{1,5},{2,6},{3,7},{8,12},{9,13},{10,14},{11,15},{16,20},{17,... | collective-permute-start | bytes 1081352 | tf_op jit(solution)/shard_map/ppermute | solution.py:38
  366.7 16.5 %attention_forward.1 = (bf16[512,1024]{1,0:T(8,128)(2,1)S(1)}, f32[8,1,512]{2,1,0:T(1,128)S(1)}) custom-call(bf16[512,3072]{1,0:T(8,128)(2,1)S(1)} %matmul_packed.3.refs_0_.refs_1_.refs_2_, bf16[512,3072]{1,0:T(8,128)(2,1)S(1)} %matmul_packed.3.refs_0_.refs_1_.refs_2_, bf16[512,3072]{1,0:T(8,128)(2,1)S(1)} %matmul_packed.3.refs_0_.refs_1_.refs_2_, ...), custom_call_target="tpu_custom_call" | custom-call | flops 3254779904 | bytes 12582912 | tf_op jit(solution)/shard_map/attention_forward/pallas_call | solution.py:140
  386.3 40.8 %all-gather.15.cloned.1.call-done = bf16[8192,1024]{1,0:T(8,128)(2,1)} async-done(((bf16[256,1024]{1,0:T(8,128)(2,1)}), bf16[8192,1024]{1,0:T(8,128)(2,1)}) %all-gather.15.cloned.1.call-update) | async-done | bytes 16777232 | tf_op jit(solution)/shard_map/all_gather | solution.py:675
  427.0 16.7 %feed_forward.1 = (f32[512,1024]{1,0:T(8,128)}, f32[512,4096]{1,0:T(8,128)}, bf16[8,512,512]{2,1,0:T(8,128)(2,1)}) custom-call(bf16[512,1024]{1,0:T(8,128)(2,1)} %multiply_convert_fusion.3.value_ref, bf16[32,256,1024]{2,1,0:T(8,128)(2,1)} %bitcast.193, bf16[32,256,1024]{2,1,0:T(8,128)(2,1)} %bitcast.194, f32[512,1024]{1,0:T(8,128)} %copy-done.38), custom_call_target="tpu_custom_call" | custom-call | flops 8589934592 | bytes 33554432 | tf_op jit(solution)/shard_map/feed_forward/pallas_call | solution.py:311
  473.7 22.0 %all-gather.17.cloned.1.call-done = bf16[2176,1024]{1,0:T(8,128)(2,1)} async-done(((bf16[272,1024]{1,0:T(8,128)(2,1)}), bf16[2176,1024]{1,0:T(8,128)(2,1)}) %all-gather.17.cloned.1.call-update) | async-done | bytes 4456464 | tf_op jit(solution)/shard_map/all_gather | solution.py:767
  499.7 25.1 %fusion.114 = (f32[2048]{0:T(1024)S(1)}, f32[2048,4000]{0,1:T(8,128)}) fusion(bf16[2048,1024]{1,0:T(8,128)(2,1)S(1)} %bitcast.203, bf16[4000,1024]{1,0:T(8,128)(2,1)} %constant_dynamic-update-slice_fusion.6), kind=kOutput, calls=%fused_computation.369 | convolution fusion | flops 16785405952 | bytes 45162496 | tf_op jit(solution)/shard_map/dot_general | solution.py:69
  524.9 14.8 %select_reduce_fusion = (f32[2048]{0:T(1024)S(1)}, f32[2048]{0:T(1024)S(1)}) fusion(f32[2048,4000]{0,1:T(8,128)} %get-tuple-element.355, s32[2048]{0:T(1024)S(1)} %fusion.69, f32[2048]{0:T(1024)S(1)} %get-tuple-element.354), kind=kLoop, calls=%fused_computation.1 | loop fusion | flops 40955904 | bytes 32800768 | tf_op jit(solution)/shard_map/reduce_sum | solution.py:799
  554.8 25.2 %convolution_convert_fusion = bf16[2048,1024]{1,0:T(8,128)(2,1)} fusion(bf16[4000,1024]{1,0:T(8,128)(2,1)} %constant_dynamic-update-slice_fusion.6, f32[2048,4000]{0,1:T(8,128)} %get-tuple-element.355, s32[2048]{0:T(1024)S(1)} %fusion.69, f32[2048]{0:T(1024)S(1)} %log_add_fusion, f32[2048]{0:T(1024)S(1)} %bitcast.246), kind=kOutput, calls=%fused_computation.12 | convolution fusion | flops 16828465152 | bytes 45178880 | tf_op jit(solution)/shard_map/dot_general | solution.py:65
  580.1 27.2 %fusion.97 = f32[4000,1024]{1,0:T(8,128)} fusion(bf16[2048,1024]{1,0:T(8,128)(2,1)} %bitcast.204, f32[2048,4000]{0,1:T(8,128)} %get-tuple-element.355, s32[2048]{0:T(1024)S(1)} %fusion.69, f32[2048]{0:T(1024)S(1)} %log_add_fusion, f32[2048]{0:T(1024)S(1)} %bitcast.247), kind=kOutput, calls=%fused_computation.360 | convolution fusion | flops 16826368000 | bytes 53370880 | tf_op jit(solution)/shard_map/dot_general | solution.py:73
  607.4 21.6 %reduce-scatter.5.cloned.1.call-done = bf16[256,1024]{1,0:T(8,128)(2,1)} async-done(((bf16[2048,1024]{1,0:T(8,128)(2,1)}), bf16[256,1024]{1,0:T(8,128)(2,1)}) %reduce-scatter.5.cloned.1.call-update) | async-done | bytes 524304 | tf_op jit(solution)/shard_map/reduce_scatter | solution.py:808
  634.8 19.1 %feed_forward_back.1 = (bf16[512,4096]{1,0:T(8,128)(2,1)}, f32[512,1024]{1,0:T(8,128)}) custom-call(bf16[512,1024]{1,0:T(8,128)(2,1)} %get-tuple-element.288.grad_ref, f32[512,4096]{1,0:T(8,128)} %get-tuple-element.114.pre_ref, bf16[32,256,1024]{2,1,0:T(8,128)(2,1)} %bitcast.195, bf16[32,256,1024]{2,1,0:T(8,128)(2,1)} %bitcast.196), custom_call_target="tpu_custom_call" | custom-call | flops 8589934592 | bytes 33554432 | tf_op jit(solution)/shard_map/feed_forward_back/pallas_call | solution.py:361
  683.4 24.9 %attention_backward.1 = (bf16[512,1024]{1,0:T(8,128)(2,1)}, f32[2,512,1024]{2,1,0:T(8,128)}, bf16[2,512,1024]{2,1,0:T(8,128)(2,1)}, bf16[2,176,1024]{2,1,0:T(8,1...) custom-call(bf16[512,3072]{1,0:T(8,128)(2,1)} %copy-done.5, bf16[512,3072]{1,0:T(8,128)(2,1)} %copy-done.5, ...), custom_call_target="tpu_custom_call" | custom-call | flops 8136949760 | bytes 25165824 | tf_op jit(solution)/shard_map/attention_backward/pallas_call | solution.py:171
  712.3 32.9 %collective-permute-done.26 = bf16[2,176,1024]{2,1,0:T(8,128)(2,1)} collective-permute-done((bf16[2,176,1024]{2,1,0:T(8,128)(2,1)}, bf16[2,176,1024]{2,1,0:T(8,128)(2,1)}, u32[]{:S(2)}, u32[]{:S(2)}) %collective-permute-start.26) | collective-permute-done | bytes 720928 | tf_op jit(solution)/shard_map/ppermute | solution.py:38
  802.2 25.0 %collective-permute-start.39 = (bf16[8,128,512]{2,1,0:T(8,128)(2,1)}, bf16[8,128,512]{2,1,0:T(8,128)(2,1)}, u32[]{:S(2)}, u32[]{:S(2)}) collective-permute-start(bf16[8,128,512]{2,1,0:T(8,128)(2,1)} %get-tuple-element.140), channel_id=1, source_target_pairs={{0,2},{2,0},{1,3},{3,1},{4,6},{6,4},{5,7},{7,5},{8,10},{10,8},{9,1... | collective-permute-start | bytes 3145736 | tf_op jit(solution)/shard_map/ppermute | solution.py:211
  845.4 15.9 %collective-permute-done.38 = bf16[8,128,512]{2,1,0:T(8,128)(2,1)} collective-permute-done((bf16[8,128,512]{2,1,0:T(8,128)(2,1)}, bf16[8,128,512]{2,1,0:T(8,128)(2,1)}, u32[]{:S(2)}, u32[]{:S(2)}) %collective-permute-start.38) | collective-permute-done | bytes 1048608 | tf_op jit(solution)/shard_map/ppermute | solution.py:211
  873.1 21.1 %collective-permute-done.40 = bf16[256,1024]{1,0:T(8,128)(2,1)} collective-permute-done((bf16[256,1024]{1,0:T(8,128)(2,1)}, bf16[256,1024]{1,0:T(8,128)(2,1)}, u32[]{:S(2)}, u32[]{:S(2)}) %collective-permute-start.40) | collective-permute-done | bytes 524320 | tf_op jit(solution)/shard_map/ppermute | solution.py:478
  905.6 18.5 %collective-permute-done.41 = bf16[256,1024]{1,0:T(8,128)(2,1)} collective-permute-done((bf16[256,1024]{1,0:T(8,128)(2,1)}, bf16[256,1024]{1,0:T(8,128)(2,1)}, u32[]{:S(2)}, u32[]{:S(2)}) %collective-permute-start.41) | collective-permute-done | bytes 524320 | tf_op jit(solution)/shard_map/ppermute | solution.py:478
  974.9 25.0 %spread_piece.3 = (bf16[2,1000,512]{2,1,0:T(8,128)(2,1)S(1)}, bf16[2,1000,512]{2,1,0:T(8,128)(2,1)S(1)}) custom-call(s32[1,4096]{1,0:T(1,128)S(1)} %bitcast.182, bf16[4096,1024]{1,0:T(8,128)(2,1)} %all-gather.11.cloned.1.call-done.refs_1_, f32[4,1000,1024]{2,1,0:T(8,128)} %bitcast.255), custom_call_target="tpu_custom_call" | custom-call | flops 16777216000 | bytes 25165824 | tf_op jit(solution)/shard_map/spread_piece/pallas_call | solution.py:570
  1009.3 15.4 %collective-permute-done.29 = f32[3200]{0:T(1024)S(1)} collective-permute-done((f32[3200]{0:T(1024)S(1)}, f32[3200]{0:T(1024)S(1)}, u32[]{:S(2)}, u32[]{:S(2)}) %collective-permute-start.29) | collective-permute-done | bytes 12832 | tf_op jit(solution)/shard_map/ppermute | solution.py:211
  1068.7 26.5 %spread_piece.2 = (f32[2,1000,512]{2,1,0:T(8,128)S(1)}, f32[2,1000,512]{2,1,0:T(8,128)}) custom-call(s32[1,4096]{1,0:T(1,128)S(1)} %bitcast.183, bf16[4096,1024]{1,0:T(8,128)(2,1)} %all-gather.11.cloned.1.call-done.refs_1_, f32[4,1000,1024]{2,1,0:T(8,128)} %bitcast.256), custom_call_target="tpu_custom_call" | custom-call | flops 16777216000 | bytes 25165824 | tf_op jit(solution)/shard_map/spread_piece/pallas_call | solution.py:570
  (621 shorter events, 467.3 us)
Async XLA Ops:
  8.0 233.5 %reduce-scatter.3.cloned.1.call-start = ((), (), s32[]{:S(2)}) async-start(), calls=%async_computation.2 | async-start | bytes 9437184 | tf_op jit(solution)/shard_map/reduce_scatter | solution.py:676
  10.6 47.6 %collective-permute-start = (bf16[1000,1024]{1,0:T(8,128)(2,1)S(1)}, bf16[1000,1024]{1,0:T(8,128)(2,1)S(1)}, u32[]{:S(2)}, u32[]{:S(2)}) collective-permute-start(bf16[1000,1024]{1,0:T(8,128)(2,1)S(1)} %convert_element_type.340), channel_id=1, source_target_pairs={{0,2},{2,0},{1,3},{3,1},{4,6},{6,4},{5,7},{7,5},{8,10},{10,8},{9,1... | collective-permute-start | bytes 6144008 | tf_op jit(solution)/shard_map/ppermute | solution.py:211
  13.6 53.1 %collective-permute-start.1 = (bf16[1000,1024]{1,0:T(8,128)(2,1)S(1)}, bf16[1000,1024]{1,0:T(8,128)(2,1)}, u32[]{:S(2)}, u32[]{:S(2)}) collective-permute-start(bf16[1000,1024]{1,0:T(8,128)(2,1)S(1)} %convert_element_type.340), channel_id=1, source_target_pairs={{0,4},{4,0},{1,5},{5,1},{2,6},{6,2},{3,7},{7,3},{8,12},{12,8},{9,1... | collective-permute-start | bytes 6144008 | tf_op jit(solution)/shard_map/ppermute | solution.py:211
  125.1 174.1 %all-gather.13.cloned.1.call-start = ((), (), s32[]{:S(2)}) async-start(), calls=%async_computation.5 | async-start | bytes 16220160 | tf_op jit(solution)/shard_map/all_gather | solution.py:674
  127.2 299.8 %all-gather.15.cloned.1.call-start = ((), (), s32[]{:S(2)}) async-start(), calls=%async_computation.6 | async-start | bytes 17301504 | tf_op jit(solution)/shard_map/all_gather | solution.py:675
  128.2 367.5 %all-gather.17.cloned.1.call-start = ((), (), s32[]{:S(2)}) async-start(), calls=%async_computation.7 | async-start | bytes 5013504 | tf_op jit(solution)/shard_map/all_gather | solution.py:767
  301.8 55.4 %collective-permute-start.4 = (bf16[512,1024]{1,0:T(8,128)(2,1)S(1)}, bf16[512,1024]{1,0:T(8,128)(2,1)}, u32[]{:S(2)}, u32[]{:S(2)}) collective-permute-start(bf16[512,1024]{1,0:T(8,128)(2,1)S(1)} %multiply_convert_fusion.4.value_ref), channel_id=1, source_target_pairs={{0,1},{1,2},{2,3},{3,4},{4,5},{5,6},{6,7},{8,9},{9,10},{10,11},{11... | collective-permute-start | bytes 3145736 | tf_op jit(solution)/shard_map/ppermute | solution.py:38
  315.0 41.6 %collective-permute-start.8 = (bf16[176,1024]{1,0:T(8,128)(2,1)S(1)}, bf16[176,1024]{1,0:T(8,128)(2,1)}, u32[]{:S(2)}, u32[]{:S(2)}) collective-permute-start(bf16[176,1024]{1,0:T(8,128)(2,1)S(1)} %matmul_packed.4), channel_id=1, source_target_pairs={{0,4},{1,5},{2,6},{3,7},{8,12},{9,13},{10,14},{11,15},{16,20},{17,... | collective-permute-start | bytes 1081352 | tf_op jit(solution)/shard_map/ppermute | solution.py:38
  447.9 181.0 %reduce-scatter.5.cloned.1.call-start = ((), (), s32[]{:S(2)}) async-start(), calls=%async_computation.3 | async-start | bytes 4718592 | tf_op jit(solution)/shard_map/reduce_scatter | solution.py:808
  452.1 47.6 %collective-permute-start.14 = (bf16[4,512,512]{2,1,0:T(8,128)(2,1)}, bf16[4,512,512]{2,1,0:T(8,128)(2,1)}, u32[]{:S(2)}, u32[]{:S(2)}) collective-permute-start(bf16[4,512,512]{2,1,0:T(8,128)(2,1)} %get-tuple-element.300), channel_id=1, source_target_pairs={{0,1},{1,0},{2,3},{3,2},{4,5},{5,4},{6,7},{7,6},{8,9},{9,8},{10,11... | collective-permute-start | bytes 6291464 | tf_op jit(solution)/shard_map/ppermute | solution.py:211
  455.9 43.7 %collective-permute-start.15 = (bf16[4,128,512]{2,1,0:T(8,128)(2,1)}, bf16[4,128,512]{2,1,0:T(8,128)(2,1)S(1)}, u32[]{:S(2)}, u32[]{:S(2)}) collective-permute-start(bf16[4,128,512]{2,1,0:T(8,128)(2,1)} %get-tuple-element.330), channel_id=1, source_target_pairs={{0,1},{1,0},{2,3},{3,2},{4,5},{5,4},{6,7},{7,6},{8,9},{9,8},{10,11... | collective-permute-start | bytes 1572872 | tf_op jit(solution)/shard_map/ppermute | solution.py:211
  580.1 394.4 %all-gather.11.cloned.1.call-start = ((), (), s32[]{:S(2)}) async-start(), calls=%async_computation.4 | async-start | bytes 9437184 | tf_op jit(solution)/shard_map/all_gather | solution.py:867
  680.5 87.0 %collective-permute-start.22 = (bf16[8,256,512]{2,1,0:T(8,128)(2,1)}, bf16[8,256,512]{2,1,0:T(8,128)(2,1)}, u32[]{:S(2)}, u32[]{:S(2)}) collective-permute-start(bf16[8,256,512]{2,1,0:T(8,128)(2,1)} %gradient_piece.8), channel_id=1, source_target_pairs={{0,2},{2,0},{1,3},{3,1},{4,6},{6,4},{5,7},{7,5},{8,10},{10,8},{9,1... | collective-permute-start | bytes 6291464 | tf_op jit(solution)/shard_map/ppermute | solution.py:211
  682.0 89.6 %collective-permute-start.23 = (bf16[8,256,512]{2,1,0:T(8,128)(2,1)}, bf16[8,256,512]{2,1,0:T(8,128)(2,1)}, u32[]{:S(2)}, u32[]{:S(2)}) collective-permute-start(bf16[8,256,512]{2,1,0:T(8,128)(2,1)} %gradient_piece.9), channel_id=1, source_target_pairs={{0,4},{4,0},{1,5},{5,1},{2,6},{6,2},{3,7},{7,3},{8,12},{12,8},{9,1... | collective-permute-start | bytes 6291464 | tf_op jit(solution)/shard_map/ppermute | solution.py:211
  709.6 55.8 %collective-permute-start.25 = (bf16[2,176,1024]{2,1,0:T(8,128)(2,1)}, bf16[2,176,1024]{2,1,0:T(8,128)(2,1)}, u32[]{:S(2)}, u32[]{:S(2)}) collective-permute-start(bf16[2,176,1024]{2,1,0:T(8,128)(2,1)} %get-tuple-element.126), channel_id=1, source_target_pairs={{3,0},{4,1},{5,2},{6,3},{7,4},{11,8},{12,9},{13,10},{14,11},{15,12... | collective-permute-start | bytes 2162696 | tf_op jit(solution)/shard_map/ppermute | solution.py:38
  710.9 54.5 %collective-permute-start.24 = (bf16[2,176,1024]{2,1,0:T(8,128)(2,1)}, bf16[2,176,1024]{2,1,0:T(8,128)(2,1)}, u32[]{:S(2)}, u32[]{:S(2)}) collective-permute-start(bf16[2,176,1024]{2,1,0:T(8,128)(2,1)} %get-tuple-element.125), channel_id=1, source_target_pairs={{2,0},{3,1},{4,2},{5,3},{6,4},{7,5},{10,8},{11,9},{12,10},{13,11},... | collective-permute-start | bytes 2162696 | tf_op jit(solution)/shard_map/ppermute | solution.py:38
  745.1 43.3 %collective-permute-start.21 = (bf16[2,512,1024]{2,1,0:T(8,128)(2,1)}, bf16[2,512,1024]{2,1,0:T(8,128)(2,1)}, u32[]{:S(2)}, u32[]{:S(2)}) collective-permute-start(bf16[2,512,1024]{2,1,0:T(8,128)(2,1)} %get-tuple-element.121), channel_id=1, source_target_pairs={{1,0},{2,1},{3,2},{4,3},{5,4},{6,5},{7,6},{9,8},{10,9},{11,10},{12... | collective-permute-start | bytes 6291464 | tf_op jit(solution)/shard_map/ppermute | solution.py:38
  802.2 40.9 %collective-permute-start.39 = (bf16[8,128,512]{2,1,0:T(8,128)(2,1)}, bf16[8,128,512]{2,1,0:T(8,128)(2,1)}, u32[]{:S(2)}, u32[]{:S(2)}) collective-permute-start(bf16[8,128,512]{2,1,0:T(8,128)(2,1)} %get-tuple-element.140), channel_id=1, source_target_pairs={{0,2},{2,0},{1,3},{3,1},{4,6},{6,4},{5,7},{7,5},{8,10},{10,8},{9,1... | collective-permute-start | bytes 3145736 | tf_op jit(solution)/shard_map/ppermute | solution.py:211
  837.4 95.6 %collective-permute-start.34 = (bf16[2,512,1024]{2,1,0:T(8,128)(2,1)S(1)}, bf16[2,512,1024]{2,1,0:T(8,128)(2,1)}, u32[]{:S(2)}, u32[]{:S(2)}) collective-permute-start(bf16[2,512,1024]{2,1,0:T(8,128)(2,1)S(1)} %add_convert_fusion.grad_ref.refs_10_.refs_22_), channel_id=1, source_target_pairs={{0,1},{1,0},{2,3},{3,2},{4,5},{5,4},{6,7},{7,6},{8,9},{9,8},{10,11... | collective-permute-start | bytes 6291464 | tf_op jit(solution)/shard_map/ppermute | solution.py:211
  873.1 54.2 %collective-permute-start.37 = (bf16[1,512,1024]{2,1,0:T(8,128)(2,1)}, bf16[1,512,1024]{2,1,0:T(8,128)(2,1)}, u32[]{:S(2)}, u32[]{:S(2)}) collective-permute-start(bf16[1,512,1024]{2,1,0:T(8,128)(2,1)} %get-tuple-element.286.refs_40_), channel_id=1, source_target_pairs={{0,1},{1,0},{2,3},{3,2},{4,5},{5,4},{6,7},{7,6},{8,9},{9,8},{10,11... | collective-permute-start | bytes 3145736 | tf_op jit(solution)/shard_map/ppermute | solution.py:211
  928.8 45.4 %collective-permute-start.42 = (bf16[256,1024]{1,0:T(8,128)(2,1)}, bf16[256,1024]{1,0:T(8,128)(2,1)S(1)}, u32[]{:S(2)}, u32[]{:S(2)}) collective-permute-start(bf16[256,1024]{1,0:T(8,128)(2,1)} %get-tuple-element.296), channel_id=1, source_target_pairs={{0,8},{8,16},{16,24},{1,9},{9,17},{17,25},{2,10},{10,18},{18,26},{... | collective-permute-start | bytes 1572872 | tf_op jit(solution)/shard_map/ppermute | solution.py:478
  943.5 56.4 %collective-permute-start.52 = (bf16[7,256,512]{2,1,0:T(8,128)(2,1)S(1)}, bf16[7,256,512]{2,1,0:T(8,128)(2,1)}, u32[]{:S(2)}, u32[]{:S(2)}) collective-permute-start(bf16[7,256,512]{2,1,0:T(8,128)(2,1)S(1)} %gradient_piece.15), channel_id=1, source_target_pairs={{0,4},{4,0},{1,5},{5,1},{2,6},{6,2},{3,7},{7,3},{8,12},{12,8},{9,1... | collective-permute-start | bytes 5505032 | tf_op jit(solution)/shard_map/ppermute | solution.py:211
  956.2 46.2 %collective-permute-start.50 = (bf16[7,256,512]{2,1,0:T(8,128)(2,1)}, bf16[7,256,512]{2,1,0:T(8,128)(2,1)}, u32[]{:S(2)}, u32[]{:S(2)}) collective-permute-start(bf16[7,256,512]{2,1,0:T(8,128)(2,1)} %gradient_piece.14), channel_id=1, source_target_pairs={{0,2},{2,0},{1,3},{3,1},{4,6},{6,4},{5,7},{7,5},{8,10},{10,8},{9,1... | collective-permute-start | bytes 5505032 | tf_op jit(solution)/shard_map/ppermute | solution.py:211
  1065.5 43.3 %collective-permute-start.46 = (bf16[2,1000,512]{2,1,0:T(8,128)(2,1)S(1)}, bf16[2,1000,512]{2,1,0:T(8,128)(2,1)S(1)}, u32[]{:S(2)}, u32[]{:S(2)}) collective-permute-start(bf16[2,1000,512]{2,1,0:T(8,128)(2,1)S(1)} %copy-done.34), channel_id=1, source_target_pairs={{0,2},{2,0},{1,3},{3,1},{4,6},{6,4},{5,7},{7,5},{8,10},{10,8},{9,1... | collective-permute-start | bytes 6144008 | tf_op jit(solution)/shard_map/ppermute | solution.py:211
  (169 other events, 3581.2 us)
Sparse Core Ops, SparseCore 0:
  125.2 116.3 reduce-scatter.2
  448.0 47.6 all-gather.16
  580.1 48.7 reduce-scatter.4
  802.3 130.0 all-gather.10
Sparse Core Ops, SparseCore 1:
  129.0 170.0 all-gather.12
  302.4 124.5 all-gather.14

commit v3 on v2

--- a/solution.py
+++ b/solution.py
@@ -28,6 +28,7 @@
 PIECE = 512
 BLOCK = 128
 GROUPS = 32
+CHUNK = 256
 BF16 = jnp.bfloat16
 F32 = jnp.float32
 
@@ -100,7 +101,7 @@
 def attention_backward_body(*refs):
     query, own_k, own_v, mem_k, mem_v = refs[:5]
     marks = refs[5:9]
-    log_total, grad_out, grad_query, grad_own, grad_mem, g2, g3, g4, bias = refs[9:]
+    log_total, grad_out, grad_query, grad_own, grad_mem, bias = refs[9:]
 
     @pl.when(pl.program_id(0) == 0)
     def _():
@@ -116,7 +117,7 @@
     grad_query[...] = matmul_tn(keys, grad_scores).T.astype(BF16)
     pair = (matmul(grad_scores, query[...]), matmul(probs.astype(BF16), grad_out[...]))
     at = 0
-    for part in (grad_own, grad_mem, g2, g3, g4):
+    for part in (grad_own, grad_mem):
         count = part.shape[1]
         for side in (0, 1):
             part[side] = pair[side][at : at + count].astype(part.dtype)
@@ -162,7 +163,7 @@
 
 def attention_backward(projected, memory, marks, log_total, grad_out):
     segment, others = projected.shape[0], memory.shape[0]
-    keys, slots = segment + others, (others - segment) // 3
+    keys = segment + others
     width = HEADS * HEAD
 
     def pair_spec(rows):
@@ -177,14 +178,12 @@
             pl.BlockSpec((segment, HEAD), lambda h: (0, h)),
         ],
         out_specs=[pl.BlockSpec((segment, HEAD), lambda h: (0, h))]
-        + [pair_spec(segment)] * 2
-        + [pair_spec(slots)] * 3,
+        + [pair_spec(segment), pair_spec(others)],
         out_shape=[
             jax.ShapeDtypeStruct((segment, width), BF16),
-            jax.ShapeDtypeStruct((2, segment, width), F32),
             jax.ShapeDtypeStruct((2, segment, width), BF16),
-        ]
-        + [jax.ShapeDtypeStruct((2, slots, width), BF16)] * 3,
+            jax.ShapeDtypeStruct((2, others, width), BF16),
+        ],
         scratch_shapes=[pltpu.VMEM((keys, segment), F32)],
         compiler_params=pltpu.CompilerParams(vmem_limit_bytes=48 << 20),
         cost_estimate=pl.CostEstimate(
@@ -465,19 +464,36 @@
     )(place, *operands)
 
 
-def line_scatter(value):
+def line_open(value):
+    shape = value.shape[1:]
     count = lax.axis_size(LINE)
-    index = lax.axis_index(LINE)
-    total = lax.dynamic_index_in_dim(value, index, 0, False)
-    upward = downward = jnp.zeros(total.shape, F32)
-    for steps in range(count - 1, 0, -1):
-        above = lax.dynamic_index_in_dim(value, jnp.minimum(index + steps, count - 1), 0, False)
-        below = lax.dynamic_index_in_dim(value, jnp.maximum(index - steps, 0), 0, False)
-        up = [(i, i + 1) for i in range(count - steps)]
-        down = [(i, i - 1) for i in range(steps, count)]
-        upward = lax.ppermute((above + upward).astype(BF16), LINE, up).astype(F32)
-        downward = lax.ppermute((below + downward).astype(BF16), LINE, down).astype(F32)
-    return total + upward + downward
+    return value, jnp.zeros(shape, BF16), jnp.zeros(shape, BF16), count - 1
+
+
+def line_sends(state):
+    value, upward, downward, steps = state
+    count, index = lax.axis_size(LINE), lax.axis_index(LINE)
+    above = lax.dynamic_index_in_dim(value, jnp.minimum(index + steps, count - 1), 0, False)
+    below = lax.dynamic_index_in_dim(value, jnp.maximum(index - steps, 0), 0, False)
+    return (above + upward.astype(F32)).astype(BF16), (below + downward.astype(F32)).astype(BF16)
+
+
+def line_move(state, sends):
+    steps = state[3]
+    count = lax.axis_size(LINE)
+    up = [(i, i + 1) for i in range(count - steps)]
+    down = [(i, i - 1) for i in range(steps, count)]
+    upward = lax.ppermute(sends[0], LINE, up)
+    downward = lax.ppermute(sends[1], LINE, down)
+    return state[0], upward, downward, steps - 1
+
+
+def line_close(state):
+    while state[3] > 0:
+        state = line_move(state, line_sends(state))
+    value, upward, downward, _ = state
+    total = lax.dynamic_index_in_dim(value, lax.axis_index(LINE), 0, False)
+    return total + upward.astype(F32) + downward.astype(F32)
 
 
 def chip_place():
@@ -485,17 +501,17 @@
     return jnp.reshape(place, (1,)).astype(jnp.int32)
 
 
-def gradient_sends(weights):
+def gradient_sends(weights, place):
     return [
-        gradient_piece(weights, chip_place(), 0, "x", 1, BF16),
-        gradient_piece(weights, chip_place(), 1, "y", 1, BF16),
+        gradient_piece(weights, place, 0, "x", 1, BF16),
+        gradient_piece(weights, place, 1, "y", 1, BF16),
     ]
 
 
-def gradient_keeps(weights):
+def gradient_keeps(weights, place):
     return [
-        gradient_piece(weights, chip_place(), 0, "x", 0, F32),
-        gradient_piece(weights, chip_place(), 1, "y", 0, F32),
+        gradient_piece(weights, place, 0, "x", 0, F32),
+        gradient_piece(weights, place, 1, "y", 0, F32),
     ]
 
 
@@ -508,11 +524,13 @@
     return result
 
 
-def line_parts(weights, sums):
+def plane_others(sums):
+    return [swapped(other, axis) for (_, other), axis in zip(sums, ("y", "x"))]
+
+
+def line_parts(weights, sums, others):
     line = lax.axis_size(LINE)
-    joined = [
-        mine + swapped(other, axis).astype(F32) for (mine, other), axis in zip(sums, ("y", "x"))
-    ]
+    joined = [mine + other.astype(F32) for (mine, _), other in zip(sums, others)]
     first, chunks = 0, []
     for weight in weights:
         blocks, wide = weight[1:]
@@ -527,16 +545,222 @@
     return jnp.concatenate(chunks, 1)
 
 
-def small_sum(value):
-    for axis in ("core", "x", "y"):
-        value = value + swapped(value, axis)
-    count = lax.axis_size(LINE)
+class SmallSum:
+    def __init__(self, value):
+        count = lax.axis_size(LINE)
+        self.value = value
+        self.steps = [("core", 1), ("x", 1), ("y", 1)]
+        step = 1
+        while step < count:
+            self.steps.append((LINE, step))
+            step *= 2
+
+    def exchange(self):
+        axis, step = self.steps.pop(0)
+        size = lax.axis_size(axis)
+        return lax.ppermute(self.value, axis, [(i, i ^ step) for i in range(size)])
+
+    def total(self):
+        while self.steps:
+            self.value = self.value + self.exchange()
+        return self.value
+
+
+def line_gather(block):
+    return lax.all_gather(block, LINE, axis=0, tiled=False)
+
+
+def plane_swaps(value):
+    return swapped(value, "x"), swapped(value, "y")
+
+
+def plane_corners(swaps):
+    return swapped(swaps[0][..., :PIECE], "y"), swapped(swaps[1][..., PIECE:], "x")
+
+
+def plane_gather(value, swaps, corners):
+    line, rows, width = value.shape
+    along_x, along_y = swaps
+    pieces = (
+        (value, 0, 0, 0),
+        (along_x, 0, 1, 0),
+        (along_y, 1, 0, 0),
+        (corners[0], 1, 1, 0),
+        (corners[1], 1, 1, PIECE),
+    )
+    y, x, core = (lax.axis_index(axis) for axis in ("y", "x", "core"))
+    result = jnp.zeros((line, 2, 2, 2, rows, width), BF16)
+    for piece, flip_y, flip_x, column in pieces:
+        for flip in (0, 1):
+            part = swapped(piece, "core") if flip else piece
+            start = (0, y ^ flip_y, x ^ flip_x, core ^ flip, 0, column)
+            result = lax.dynamic_update_slice(result, part[:, None, None, None], start)
+    return result.reshape(8 * line, rows, width)
+
+
+def share_combine(top, total):
+    def merged(top, total, axis, pairs):
+        pair = lax.ppermute(jnp.concatenate([top, total], 0), axis, pairs)
+        best = jnp.maximum(top, pair[:1])
+        return best, total * jnp.exp(top - best) + pair[1:] * jnp.exp(pair[:1] - best)
+
+    top, total = merged(top, total, "core", [(0, 1), (1, 0)])
+    count = lax.axis_size("batch")
     step = 1
     while step < count:
-        pairs = [(i, i ^ step) for i in range(count)]
-        value = value + lax.ppermute(value, LINE, pairs)
+        top, total = merged(top, total, "batch", [(i, i ^ step) for i in range(count)])
         step *= 2
-    return value
+    return top + jnp.log(total)
+
+
+def head_logits(rows, table, wanted):
+    parts, part_rows, width = table.shape
+    count = rows.shape[0]
+
+    def body(rows_ref, table_ref, wanted_ref, logits, top, total, target):
+        part = pl.program_id(0)
+
+        @pl.when(part == 0)
+        def _():
+            top[...] = jnp.full(top.shape, NEGATIVE, F32)
+            total[...] = jnp.zeros(total.shape, F32)
+            target[...] = jnp.zeros(target.shape, F32)
+
+        for at in range(0, count, CHUNK):
+            span = slice(at, at + CHUNK)
+            scores = matmul_nt(table_ref[0], rows_ref[span])
+            logits[0, :, span] = scores
+            best = jnp.maximum(top[:, span], jnp.max(scores, 0, keepdims=True))
+            total[:, span] = total[:, span] * jnp.exp(top[:, span] - best) + jnp.sum(
+                jnp.exp(scores - best), 0, keepdims=True
+            )
+            top[:, span] = best
+            place = lax.broadcasted_iota(jnp.int32, scores.shape, 0)
+            hit = place == wanted_ref[:, span] - part * part_rows
+            target[:, span] += jnp.sum(jnp.where(hit, scores, 0.0), 0, keepdims=True)
+
+    row = pl.BlockSpec((1, count), lambda p: (0, 0))
+    return pl.pallas_call(
+        body,
+        grid=(parts,),
+        in_specs=[
+            pl.BlockSpec((count, width), lambda p: (0, 0)),
+            pl.BlockSpec((1, part_rows, width), lambda p: (p, 0, 0)),
+            row,
+        ],
+        out_specs=[pl.BlockSpec((1, part_rows, count), lambda p: (p, 0, 0)), row, row, row],
+        out_shape=[jax.ShapeDtypeStruct((parts, part_rows, count), F32)]
+        + [jax.ShapeDtypeStruct((1, count), F32)] * 3,
+        compiler_params=pltpu.CompilerParams(vmem_limit_bytes=56 << 20),
+        cost_estimate=pl.CostEstimate(
+            flops=2 * parts * part_rows * count * width,
+            bytes_accessed=4 * parts * part_rows * (count + width // 2),
+            transcendentals=parts * part_rows * count,
+        ),
+        name="head_logits",
+    )(rows, table, wanted)
+
+
+def head_grad(logits, log_norm, weight, wanted, first):
+    place = lax.broadcasted_iota(jnp.int32, logits.shape, 0)
+    probs = jnp.exp(logits - log_norm)
+    return (weight * jnp.where(place == wanted - first, probs - 1.0, probs)).astype(BF16)
+
+
+def head_row_grads(logits, log_norm, weight, wanted, turned):
+    parts, part_rows, count = logits.shape
+    width, deep = turned.shape[1:]
+
+    def body(logits_ref, log_norm_ref, weight_ref, wanted_ref, turned_ref, out, total):
+        part = pl.program_id(0)
+        @pl.when(part == 0)
+        def _():
+            total[...] = jnp.zeros(total.shape, F32)
+
+        for at in range(0, count, CHUNK):
+            span = slice(at, at + CHUNK)
+            grad = head_grad(
+                logits_ref[0, :, span],
+                log_norm_ref[:, span],
+                weight_ref[:, span],
+                wanted_ref[:, span],
+                part * part_rows,
+            )
+            if deep > part_rows:
+                grad = jnp.concatenate([grad, jnp.zeros((deep - part_rows, CHUNK), BF16)], 0)
+            total[:, span] += matmul(turned_ref[0], grad)
+
+        @pl.when(part == parts - 1)
+        def _():
+            out[...] = total[...].T.astype(BF16)
+
+    row = pl.BlockSpec((1, count), lambda p: (0, 0))
+    return pl.pallas_call(
+        body,
+        grid=(parts,),
+        in_specs=[
+            pl.BlockSpec((1, part_rows, count), lambda p: (p, 0, 0)),
+            row,
+            row,
+            row,
+            pl.BlockSpec((1, width, deep), lambda p: (p, 0, 0)),
+        ],
+        out_specs=pl.BlockSpec((count, width), lambda p: (0, 0)),
+        out_shape=jax.ShapeDtypeStruct((count, width), BF16),
+        scratch_shapes=[pltpu.VMEM((width, count), F32)],
+        compiler_params=pltpu.CompilerParams(vmem_limit_bytes=56 << 20),
+        cost_estimate=pl.CostEstimate(
+            flops=2 * parts * part_rows * count * width,
+            bytes_accessed=4 * parts * part_rows * (count + width // 2),
+            transcendentals=parts * part_rows * count,
+        ),
+        name="head_row_grads",
+    )(logits, log_norm, weight, wanted, turned)
+
+
+def head_table_grads(groups):
+    parts, part_rows, count = groups[0][0].shape
+    width = groups[0][4].shape[1]
+
+    def body(*refs):
+        out = refs[-1]
+        total = jnp.zeros((part_rows, width), F32)
+        for at in range(0, 5 * len(groups), 5):
+            logits, log_norm, weight, wanted, rows = refs[at : at + 5]
+            for start in range(0, count, CHUNK):
+                span = slice(start, start + CHUNK)
+                grad = head_grad(
+                    logits[0, :, span],
+                    log_norm[:, span],
+                    weight[:, span],
+                    wanted[:, span],
+                    pl.program_id(0) * part_rows,
+                )
+                total += matmul(grad, rows[span])
+        out[0] = total
+
+    row = pl.BlockSpec((1, count), lambda p: (0, 0))
+    specs = [
+        pl.BlockSpec((1, part_rows, count), lambda p: (p, 0, 0)),
+        row,
+        row,
+        row,
+        pl.BlockSpec((count, width), lambda p: (0, 0)),
+    ]
+    return pl.pallas_call(
+        body,
+        grid=(parts,),
+        in_specs=specs * len(groups),
+        out_specs=pl.BlockSpec((1, part_rows, width), lambda p: (p, 0, 0)),
+        out_shape=jax.ShapeDtypeStruct((parts, part_rows, width), F32),
+        compiler_params=pltpu.CompilerParams(vmem_limit_bytes=58 << 20),
+        cost_estimate=pl.CostEstimate(
+            flops=2 * parts * part_rows * count * width * len(groups),
+            bytes_accessed=4 * parts * part_rows * (count * len(groups) + width),
+            transcendentals=parts * part_rows * count * len(groups),
+        ),
+        name="head_table_grads",
+    )(*[value for group in groups for value in group])
 
 
 def spread_body(row_of, token_row, grads, table_grad, *refs):
@@ -622,8 +846,34 @@
 
     own_tokens = token_ids.reshape(segment)
     share_tokens = lax.all_gather(own_tokens, SHARE, axis=0, tiled=True)
+    rows_in = attn_in_m.size // width
+    rows_out = attn_out_m.size // width
+    rows_comp = compress_m.size // width
+    rows_ffn = ffn_in_m.size // width
+    rows_ffn_out = ffn_out_m.size // width
+    gain_count = gains_m.size
+    gain_block = jnp.zeros((16, width), BF16).at[0, :gain_count].set(
+        gains_m.astype(BF16).reshape(-1)
+    )
+    mixer_block = jnp.concatenate(
+        [
+            column_blocks(attn_in_m.astype(BF16)),
+            compress_m.astype(BF16),
+            attn_out_m.astype(BF16),
+            gain_block,
+        ],
+        0,
+    )
+    ffn_block = jnp.concatenate(
+        [column_blocks(ffn_in_m.astype(BF16)), ffn_out_m.astype(BF16)], 0
+    )
     own_table = lax.all_gather(table_master.astype(BF16), "far", axis=0, tiled=True)
-    table_x, table_y = swapped(own_table, "x"), swapped(own_table, "y")
+    table_x, table_y = plane_swaps(own_table)
+    mixer_line_all, ffn_line_all = line_gather(mixer_block), line_gather(ffn_block)
+    table_x, table_y, mixer_line_all = lax.optimization_barrier(
+        (table_x, table_y, mixer_line_all)
+    )
+    mixer_swaps = plane_swaps(mixer_line_all)
     part_rows = own_table.shape[0]
     table = jnp.zeros((4 * part_rows, width), BF16)
     for value, row, column in (
@@ -650,35 +900,23 @@
         (share_row >= 0)[:, None], table[jnp.maximum(share_row, 0)], jnp.zeros((), BF16)
     )
 
-    rows_in = attn_in_m.size // width
-    rows_out = attn_out_m.size // width
-    rows_comp = compress_m.size // width
-    rows_ffn = ffn_in_m.size // width
-    rows_ffn_out = ffn_out_m.size // width
-    gain_count = gains_m.size
-    gain_block = jnp.zeros((16, width), BF16).at[0, :gain_count].set(
-        gains_m.astype(BF16).reshape(-1)
-    )
-    mixer_block = jnp.concatenate(
-        [
-            column_blocks(attn_in_m.astype(BF16)),
-            compress_m.astype(BF16),
-            attn_out_m.astype(BF16),
-            gain_block,
-        ],
-        0,
-    )
-    ffn_block = jnp.concatenate(
-        [column_blocks(ffn_in_m.astype(BF16)), ffn_out_m.astype(BF16)], 0
-    )
-    mixer_all = lax.all_gather(mixer_block, ALL, axis=0, tiled=False)
-    ffn_all = lax.all_gather(ffn_block, ALL, axis=0, tiled=False)
+    looked, mixer_swaps, ffn_line_all = lax.optimization_barrier(
+        (looked, mixer_swaps, ffn_line_all)
+    )
+    mixer_corners = plane_corners(mixer_swaps)
+    table_again, mixer_corners, ffn_line_all = lax.optimization_barrier(
+        (table, mixer_corners, ffn_line_all)
+    )
+    ffn_swaps = plane_swaps(ffn_line_all)
+    mixer_all = plane_gather(mixer_line_all, mixer_swaps, mixer_corners)
+    gains = mixer_all[:, rows_in + rows_comp + rows_out, :gain_count]
     token_rows = lax.psum_scatter(looked, SHARE, scatter_dimension=0, tiled=True)
-    gains = mixer_all[:, rows_in + rows_comp + rows_out, :gain_count]
     gains = gains.reshape(width, 3).astype(F32)
+    table = table_again.reshape(4, part_rows, width)
+    turned = jnp.pad(table, ((0, 0), (0, -part_rows % 128), (0, 0))).transpose(0, 2, 1)
+    token_rows, turned, ffn_swaps = lax.optimization_barrier((token_rows, turned, ffn_swaps))
     part = attn_in_m.shape[0]
     mixer_all = grouped(mixer_all, (part, part, part, rows_comp, rows_out, 16))
-    ffn_all = grouped(ffn_all, (part,) * (rows_ffn // part) + (rows_ffn_out,))
     thin = width // GROUPS
 
     book_ends = jnp.cumsum(book_lengths.reshape(-1))
@@ -706,6 +944,9 @@
     embedded = token_rows.astype(F32) * width**0.5
     normed_one, unit_one, scale_one = norm_forward(embedded, gains[:, 0])
     attention_input = normed_one.astype(BF16)
+    attention_input, ffn_swaps = lax.optimization_barrier((attention_input, ffn_swaps))
+    ffn_all = plane_gather(ffn_line_all, ffn_swaps, plane_corners(ffn_swaps))
+    ffn_all = grouped(ffn_all, (part,) * (rows_ffn // part) + (rows_ffn_out,))
     projected = matmul_packed(attention_input, mixer_all, thin, 0, 3)
     memory_rows = passed_along(attention_input, 1)
     tail_rows = passed_along(attention_input[segment - 2 :], 1)
@@ -717,6 +958,7 @@
     )
     compressed = matmul_packed(slot_rows, mixer_all, 3 * thin, 1, 1)
     other_rows = [memory_rows]
+    spare = -(segment + 3 * slots) % BLOCK
     book_parts = [own_book, book_number(own_pos - segment, book_ends)]
     pos_parts = [own_pos, own_pos - segment]
     for hop in (2, 3, 4):
@@ -732,13 +974,17 @@
         usable = usable & (book_number(last_pos - 2, book_ends) == last_book)
         book_parts.append(jnp.where(usable, last_book, -2))
         pos_parts.append(jnp.full((slots,), -1, jnp.int32))
+    book_parts.append(jnp.full((spare,), -2, jnp.int32))
+    pos_parts.append(jnp.full((spare,), -1, jnp.int32))
+    other_rows.append(jnp.zeros((spare, width), BF16))
     marks = (
         jnp.concatenate(book_parts)[:, None],
         jnp.concatenate(pos_parts)[:, None],
         own_book[None, :],
         own_pos[None, :],
     )
-    memory_pairs = matmul_packed(jnp.concatenate(other_rows, 0), mixer_all, thin, 1, 2)
+    other_rows = jnp.concatenate(other_rows, 0)
+    memory_pairs = matmul_packed(other_rows, mixer_all, thin, 1, 2)
     attended, log_total = attention_forward(projected, memory_pairs, marks)
     w_out = mixer_all[:, 6 * thin : 7 * thin].reshape(width, width)
     residual = embedded + matmul(attended, w_out)
@@ -764,48 +1010,54 @@
         ]
     )
     side_rows = jnp.zeros((16 * width,), BF16).at[: 5 * keep].set(side).reshape(16, width)
+    half = keep // 2
     head_all = lax.all_gather(
         jnp.concatenate([picked_rows, side_rows], 0), SHARE, axis=0, tiled=False
     )
-    spare = -slots % BLOCK
-    comp_tall = jnp.concatenate([compressed, jnp.zeros((spare, width), BF16)], 0)
-    slot_tall = jnp.concatenate([slot_rows, jnp.zeros((spare, 3 * width), BF16)], 0)
+    slot_spare = -slots % BLOCK
+    slot_tall = jnp.concatenate([slot_rows, jnp.zeros((slot_spare, 3 * width), BF16)], 0)
     halves = [
         core_halves(value)
         for value in (
             grouped_transpose(ffn_input),
             activated_turned,
             grouped_transpose(attention_input),
-            grouped_transpose(comp_tall),
+            grouped_transpose(other_rows),
             grouped_transpose(slot_tall),
             grouped_transpose(attended),
         )
     ]
-    rows = head_all[:, :keep].reshape(share_count * keep, width)
-    rows, halves = lax.optimization_barrier((rows, halves))
+    rows_one = head_all[:, :half].reshape(share_count * half, width)
+    rows_two = head_all[:, half:keep].reshape(share_count * half, width)
     side_all = head_all[:, keep:].reshape(share_count, 16 * width)[:, : 5 * keep]
-    side_all = side_all.reshape(share_count, 5, keep).astype(F32)
-    wanted = (side_all[:, 0] * 256.0 + side_all[:, 1]).astype(jnp.int32).reshape(-1)
-    row_weight = (side_all[:, 2] + side_all[:, 3] + side_all[:, 4]).reshape(-1)
-    wanted_owner, wanted_local = vocab_place(wanted)
-    wanted_row = jnp.where(wanted_owner == share_place, wanted_local, -1)
-    logits = matmul_nt(rows, table)
-    top_logit = jnp.max(logits, -1)
-    total = jnp.sum(jnp.exp(logits - top_logit[:, None]), -1)
-    stats = lax.all_gather(jnp.stack([top_logit, total]), SHARE, axis=0, tiled=False)
-    top_all = jnp.max(stats[:, 0], 0)
-    log_norm = top_all + jnp.log(jnp.sum(stats[:, 1] * jnp.exp(stats[:, 0] - top_all[None]), 0))
-    hit = wanted_row[:, None] == jnp.arange(logits.shape[1], dtype=jnp.int32)[None, :]
-    target_logit = jnp.sum(jnp.where(hit, logits, 0.0), -1)
-    mine = (jnp.arange(share_count * keep) // keep == share_place).astype(F32)
-    loss_local = jnp.sum(row_weight * (mine * log_norm - target_logit))
-    grad_logits = row_weight[:, None] * (
-        jnp.exp(logits - log_norm[:, None]) - hit.astype(F32)
-    )
-    grad_logits = grad_logits.astype(BF16)
-    grad_rows = matmul(grad_logits, table).astype(BF16)
-    grad_table = matmul_tn(grad_logits, rows)
-    grad_picked = lax.psum_scatter(grad_rows, SHARE, scatter_dimension=0, tiled=True)
+    rows_one, rows_two, halves = lax.optimization_barrier((rows_one, rows_two, halves))
+    side_all = side_all.reshape(share_count, 5, 2, half).astype(F32)
+    side_all = side_all.transpose(1, 2, 0, 3).reshape(5, 2, share_count * half)
+    wanted_all = (side_all[0] * 256.0 + side_all[1]).astype(jnp.int32)
+    weight_all = side_all[2] + side_all[3] + side_all[4]
+    wanted_owner, wanted_local = vocab_place(wanted_all)
+    wanted_all = jnp.where(wanted_owner == share_place, wanted_local, -1)
+    mine = (jnp.arange(share_count * half) // half == share_place).astype(F32)
+    loss_local = jnp.zeros((), F32)
+    groups, stats = [], []
+    for index, rows in enumerate((rows_one, rows_two)):
+        wanted, row_weight = wanted_all[index][None], weight_all[index][None]
+        logits, top, total, target_logit = head_logits(rows, table, wanted)
+        loss_local -= jnp.sum(row_weight * target_logit)
+        stats.append((top, total))
+        groups.append([logits, row_weight, wanted, rows])
+    log_norms = [share_combine(*stats[0]), None]
+    stats[1], log_norms[0] = lax.optimization_barrier((stats[1], log_norms[0]))
+    log_norms[1] = share_combine(*stats[1])
+    for index, (logits, row_weight, wanted, rows) in enumerate(groups):
+        loss_local += jnp.sum(row_weight * mine[None] * log_norms[index])
+        groups[index] = (logits, log_norms[index], row_weight, wanted, rows)
+    grad_picked = []
+    for group in groups:
+        grad_rows = head_row_grads(*group[:4], turned)
+        grad_picked.append(lax.psum_scatter(grad_rows, SHARE, scatter_dimension=0, tiled=True))
+    grad_picked = jnp.concatenate(grad_picked, 0)
+    grad_table = head_table_grads(groups)
     grad_picked, grad_table = lax.optimization_barrier((grad_picked, grad_table))
     grad_final = matmul_tn(chosen_bf16, grad_picked)
 
@@ -830,69 +1082,100 @@
             False,
         ),
     ]
+    ffn_rows = rows_ffn + rows_ffn_out
     grad_res_two, grad_gain_two = norm_backward(grad_norm_two, unit_two, scale_two, gains[:, 1])
     grad_residual = grad_output_rows + grad_res_two
 
     grad_attn_branch = grad_residual.astype(BF16)
     grad_attended = matmul_nt(grad_attn_branch, w_out).astype(BF16)
-    ffn_sends = gradient_sends(ffn_weights)
-    *ffn_sends, grad_attended = lax.optimization_barrier((*ffn_sends, grad_attended))
+    ffn_weights.append(([product(halves[5], with_other(grad_attn_branch))], 1, True))
+    grad_query, grad_own, grad_other = attention_backward(
+        projected, memory_pairs, marks, log_total, grad_attended
+    )
+    grad_other_rows = matmul_packed_back(grad_other, mixer_all, thin, 1).astype(BF16)
+    back_memory = passed_along(grad_other_rows[:segment], -1)
+    returned = []
+    for hop in (2, 3, 4):
+        first_row = segment + (hop - 2) * slots
+        returned.append(passed_along(grad_other_rows[first_row : first_row + slots], -hop))
+    place, grad_query = lax.optimization_barrier((chip_place(), grad_query))
+    ffn_sends = gradient_sends(ffn_weights, place)
+    grad_input = matmul_packed_back(grad_query[None], mixer_all, thin, 0)
+    grad_input = matmul_packed_back(grad_own, mixer_all, thin, 1, grad_input)
+    returned, ffn_sends, grad_input = lax.optimization_barrier(
+        (returned, ffn_sends, grad_input)
+    )
     ffn_arrived = [swapped(send, axis) for send, axis in zip(ffn_sends, ("x", "y"))]
-    grad_query, grad_own, grad_memory, *grad_comps = attention_backward(
-        projected, memory_pairs, marks, log_total, grad_attended
-    )
-    back_memory = passed_along(grad_memory, -1)
-    ffn_keeps = gradient_keeps(ffn_weights)
-    received = jnp.zeros((2, slots, width), F32)
-    for hop, grad_comp in zip((2, 3, 4), grad_comps):
-        received = received + passed_along(grad_comp, -hop).astype(F32)
-    received = received.astype(BF16)
-    ffn_sums = plane_sums(ffn_arrived, ffn_keeps)
-    ffn_sums, grad_comp_pairs = lax.optimization_barrier((ffn_sums, received))
-    ffn_parts = line_parts(ffn_weights, ffn_sums)
-    grad_compressed = matmul_packed_back(grad_comp_pairs, mixer_all, thin, 1).astype(BF16)
+    grad_compressed = sum(part.astype(F32) for part in returned).astype(BF16)
     grad_slots = matmul_packed_back(grad_compressed[None], mixer_all, 3 * thin, 1)
     grad_slots = grad_slots.reshape(3 * slots, width)
     grad_first = jnp.concatenate([jnp.zeros((2, width), F32), grad_slots[:2]], 0)
     grad_first = lax.dynamic_slice_in_dim(grad_first, 2 - first_cell, 2, 0)
     back_tail = passed_along(grad_first.astype(BF16), -1).astype(F32)
-    grad_own_pairs = (grad_own + back_memory.astype(F32)).astype(BF16)
-    grad_input = matmul_packed_back(grad_query[None], mixer_all, thin, 0)
-    grad_input = matmul_packed_back(grad_own_pairs, mixer_all, thin, 1, grad_input)
     grad_input = grad_input + lax.dynamic_slice_in_dim(grad_slots, 2 - first_cell, segment, 0)
+    grad_input = grad_input + back_memory.astype(F32)
     grad_input = grad_input.at[segment - 2 :].add(back_tail)
     grad_embed, grad_gain_one = norm_backward(grad_input, unit_one, scale_one, gains[:, 0])
     grad_scaled = ((grad_embed + grad_residual) * width**0.5).astype(BF16)
 
-    share_grads = lax.all_gather(grad_scaled, SHARE, axis=0, tiled=True)
-    query_pair, own_pair = with_other(grad_query), with_other(grad_own_pairs)
-    comp_pair = with_other(jnp.pad(grad_comp_pairs, ((0, 0), (0, spare), (0, 0))))
-    slot_pair = with_other(jnp.pad(grad_compressed, ((0, spare), (0, 0))))
+    query_pair, own_pair = with_other(grad_query), with_other(grad_own)
+    other_pair = with_other(grad_other)
+    slot_pair = with_other(jnp.pad(grad_compressed, ((0, slot_spare), (0, 0))))
     mixer_weights = [
         ([product(halves[2], query_pair)], 1, True),
-        ([product(halves[2], own_pair, 0), product(halves[3], comp_pair, 0)], 1, True),
-        ([product(halves[2], own_pair, 1), product(halves[3], comp_pair, 1)], 1, True),
+        ([product(halves[2], own_pair, 0), product(halves[3], other_pair, 0)], 1, True),
+        ([product(halves[2], own_pair, 1), product(halves[3], other_pair, 1)], 1, True),
         ([product(halves[4], slot_pair)], 3, False),
-        ([product(halves[5], with_other(grad_attn_branch))], 1, True),
     ]
-    mixer_sends = gradient_sends(mixer_weights)
+    small = jnp.concatenate(
+        [
+            jnp.stack([grad_gain_one, grad_gain_two, grad_gain_three], 1).reshape(-1),
+            jnp.full((128,), loss_local, F32),
+        ]
+    )
+    grad_scaled, place = lax.optimization_barrier((grad_scaled, place))
+    small = SmallSum(small)
+    share_grads = lax.all_gather(grad_scaled, SHARE, axis=0, tiled=True)
+    mixer_sends = gradient_sends(mixer_weights, place)
+    mixer_sends, place, arrived = lax.optimization_barrier(
+        (mixer_sends, place, small.exchange())
+    )
+    small.value += arrived
     mixer_arrived = [swapped(send, axis) for send, axis in zip(mixer_sends, ("x", "y"))]
-    mixer_keeps = gradient_keeps(mixer_weights)
-    ffn_grads = line_scatter(ffn_parts)
-    table_parts = grad_table.reshape(4, part_rows, width)
-    token_row, mixer_keeps, ffn_grads = lax.optimization_barrier(
-        (share_row[None, :], mixer_keeps, ffn_grads)
-    )
+    ffn_sums = plane_sums(ffn_arrived, gradient_keeps(ffn_weights, place))
+    ffn_sums, place, arrived = lax.optimization_barrier((ffn_sums, place, small.exchange()))
+    small.value += arrived
+    mixer_keeps = gradient_keeps(mixer_weights, place)
+    mixer_sums = plane_sums(mixer_arrived, mixer_keeps)
+    token_row, mixer_sums, arrived = lax.optimization_barrier(
+        (share_row[None, :], mixer_sums, small.exchange())
+    )
+    small.value += arrived
     table_sends = spread_piece(
-        token_row, share_grads, table_parts, lambda t: jnp.where(t < 2, 2 * t + 1, t), BF16
-    )
-    table_sends, mixer_keeps = lax.optimization_barrier((table_sends, mixer_keeps))
+        token_row, share_grads, grad_table, lambda t: jnp.where(t < 2, 2 * t + 1, t), BF16
+    )
+    ffn_others, mixer_others = plane_others(ffn_sums), plane_others(mixer_sums)
+    table_sends, token_row, ffn_others, mixer_others, arrived = lax.optimization_barrier(
+        (table_sends, token_row, ffn_others, mixer_others, small.exchange())
+    )
+    small.value += arrived
     table_arrived = [swapped(send, axis) for send, axis in zip(table_sends, ("x", "y"))]
+    lines = [
+        line_open(line_parts(ffn_weights, ffn_sums, ffn_others)),
+        line_open(line_parts(mixer_weights, mixer_sums, mixer_others)),
+    ]
+    lines = [line_move(line, line_sends(line)) for line in lines]
     table_keeps = spread_piece(
-        token_row, share_grads, table_parts, lambda t: jnp.where(t < 2, 2 * t, t - 2), F32
-    )
-    mixer_sums = plane_sums(mixer_arrived, mixer_keeps)
-    mixer_grads = line_scatter(line_parts(mixer_weights, mixer_sums))
+        token_row, share_grads, grad_table, lambda t: jnp.where(t < 2, 2 * t, t - 2), F32
+    )
+    table_keeps, table_arrived, moved, arrived = lax.optimization_barrier(
+        (table_keeps, table_arrived, [line[1:3] for line in lines], small.exchange())
+    )
+    small.value += arrived
+    lines = [(line[0], *pair, line[3]) for line, pair in zip(lines, moved)]
+    lines = [line_move(line, line_sends(line)) for line in lines]
+    summed, mixer_grads = [line_close(line) for line in lines]
+    ffn_grads, attn_out_grad = summed[:ffn_rows], summed[ffn_rows : ffn_rows + rows_out]
     halves_new = []
     for arrived, keep_part, axis in zip(table_arrived, table_keeps, ("y", "x")):
         other = (keep_part[1] + arrived[1].astype(F32)).astype(BF16)
@@ -904,13 +1187,7 @@
             grad_table.astype(BF16), "far", scatter_dimension=0, tiled=True
         )
 
-    small = jnp.concatenate(
-        [
-            jnp.stack([grad_gain_one, grad_gain_two, grad_gain_three], 1).reshape(-1),
-            jnp.full((128,), loss_local, F32),
-        ]
-    )
-    small = small_sum(small)
+    small = small.total()
     loss_total = small[3 * width]
     device = lax.axis_index(ALL)
     gain_grads = lax.dynamic_slice_in_dim(small, device * gain_count, gain_count, 0)
@@ -922,7 +1199,7 @@
     grads = (
         grad_table,
         side_by_side(mixer_grads[:low], 3),
-        mixer_grads[high:],
+        attn_out_grad,
         mixer_grads[low:high],
         side_by_side(ffn_grads[:rows_ffn], rows_ffn // attn_in_m.shape[0]),
         ffn_grads[rows_ffn:],

time: 1160 us -> 965 us (0.83)
  waiting for transfers between devices: 444 us -> 167 us
  Pallas kernels: 226 us -> 331 us
  local copies, waits for them, and re-layouts: 109 us -> 209 us
  matrix products: 84.3 us -> 6.05 us
  starting transfers between devices: 134 us -> 103 us
  blocking collectives: 27.1 us -> 13.2 us
    reduce_scatter x1, waiting for transfers between devices: 98.2 us -> 0.01 us  [per_device(): lax.psum_scatter(looked, SHARE, scatter_dimension=0, tiled=True)]
    all_gather x2, waiting for transfers between devices: 95.1 us -> 0.01 us  [line_gather(): return lax.all_gather(block, LINE, axis=0, tiled=False)]
    pallas_call x0 -> x5, Pallas kernels: none -> 91.3 us  [the longest x2 33.3 us: head_logits(): pl.pallas_call(body, grid=(parts,), in_specs=[pl.BlockSpec((count, width)...]
    ppermute x35 -> x50, waiting for transfers between devices: 112 us -> 66.5 us  [swapped(): return lax.ppermute(value, axis, [(0, 1), (1, 0)])]
    dynamic_update_slice x0 -> x20, local copies, waits for them, and re-layouts: none -> 41.5 us  [plane_gather(): result = lax.dynamic_update_slice(result, part[:, None, None, None], start)]
    ppermute x11, waiting for transfers between devices: 43.6 us -> 6.96 us  [passed_along(): lax.ppermute(value, SEQ, [(source, source + steps) for source in range(in...]
    dot_general x2 -> x1, matrix products: 30.7 us -> 2.74 us  [matmul_tn(): lax.dot_general(left, right, (((0,), (0,)), ((), ())), preferred_element_...]
    dot_general x3 -> x2, matrix products: 27.2 us -> 2.02 us  [matmul(): return jnp.dot(left, right, preferred_element_type=F32)]
  transfers between devices with their start and end apart: 66 -> 91, of which waited for: 31 -> 22; matrix products, arithmetic and copies ran while one was open for 13% -> 27% of each run, Pallas kernels for 15% -> 28%
where the time goes in v3:
time: 965 us; the launch traced here: 956 us
  Pallas kernels  331 us (34%)
  local copies, waits for them, and re-layouts  209 us (22%)
  waiting for transfers between devices  167 us (17%)
  other arithmetic  106 us (11%)
  starting transfers between devices  103 us (11%)
  between operations  19.8 us (2%)
  blocking collectives  13.2 us (1%)
    pallas_call x8, Pallas kernels, gradient_piece(): pl.pallas_call(body, grid_spec=pltpu.PrefetchScalarGridSpec(num_scalar_pr...  67 us
    ppermute x50, waiting for transfers between devices, swapped(): return lax.ppermute(value, axis, [(0, 1), (1, 0)])  66.5 us
    pallas_call x2, Pallas kernels, spread_piece(): pl.pallas_call(body, grid=(4, grads.shape[0] // tokens), in_specs=[pl.Blo...  51.3 us
    ppermute x50, starting transfers between devices, swapped(): return lax.ppermute(value, axis, [(0, 1), (1, 0)])  43.8 us
    dynamic_update_slice x20, local copies, waits for them, and re-layouts, plane_gather(): result = lax.dynamic_update_slice(result, part[:, None, None, None], start)  41.5 us
    pallas_call x2, Pallas kernels, head_logits(): pl.pallas_call(body, grid=(parts,), in_specs=[pl.BlockSpec((count, width)...  33.3 us
    unnamed x272, local copies, waits for them, and re-layouts  32.9 us
    pallas_call x2, Pallas kernels, head_row_grads(): pl.pallas_call(body, grid=(parts,), in_specs=[pl.BlockSpec((1, part_rows,...  31.1 us
  transfers between devices with their start and end apart: 91, of which 22 were waited for; matrix products, arithmetic and copies ran while one was open for 27% of the time, Pallas kernels for 28%

profile of v3, /device:TPU:0, one launch (start us, length us, event | category | flops | bytes accessed | tf_op | source)
XLA Modules:
  0.0 955.9 jit_solution(17045458155046040757)
XLA Ops:
  20.2 13.2 %all-gather = s32[1,4096]{1,0:T(1,128)S(1)} all-gather(s32[1,512]{1,0:T(1,128)S(1)} %copy-done.118), channel_id=2, replica_groups=mesh['batch'=4,'far'=1,'y'=2,'x'=2,'core'=2] {'batch','core'}, dimensions={1}, use_global_device_ids=true | all-gather | bytes 18432 | tf_op jit(solution)/shard_map/all_gather | solution.py:848
  33.3 28.9 %collective-permute-done = bf16[1000,1024]{1,0:T(8,128)(2,1)} collective-permute-done((bf16[1000,1024]{1,0:T(8,128)(2,1)S(1)}, bf16[1000,1024]{1,0:T(8,128)(2,1)}, u32[]{:S(2)}, u32[]{:S(2)}) %collective-permute-start) | collective-permute-done | bytes 2048032 | tf_op jit(solution)/shard_map/ppermute | solution.py:210
  82.2 9.6 collective-permute-done.2
  95.7 25.2 %gather_fusion = bf16[4096,1024]{1,0:T(8,128)(2,1)} fusion(bf16[4000,1024]{1,0:T(8,128)(2,1)} %constant_dynamic-update-slice_fusion.10, s32[4096]{0:T(1024)S(1)} %maximum_clamp_fusion), kind=kCustom, calls=%fused_computation | custom fusion | bytes 16793600 | tf_op jit(solution)/shard_map/gather | solution.py:900
  183.0 11.4 %copy.173 = bf16[4,1000,1024]{1,2,0:T(8,128)(2,1)} copy(bf16[4,1000,1024]{2,1,0:T(8,128)(2,1)} %bitcast.4.table_ref) | data formatting | bytes 16384000 | tf_op jit(solution)/shard_map/reshape | solution.py:915
  299.2 17.3 %attention_forward.1 = (bf16[512,1024]{1,0:T(8,128)(2,1)S(1)}, f32[8,1,512]{2,1,0:T(1,128)S(1)}) custom-call(bf16[512,3072]{1,0:T(8,128)(2,1)S(1)} %matmul_packed.3.refs_0_.refs_1_.refs_2_, bf16[512,3072]{1,0:T(8,128)(2,1)S(1)} %matmul_packed.3.refs_0_.refs_1_.refs_2_, bf16[512,3072]{1,0:T(8,128)(2,1)S(1)} %matmul_packed.3.refs_0_.refs_1_.refs_2_, ...), custom_call_target="tpu_custom_call" | custom-call | flops 3489660928 | bytes 12582912 | tf_op jit(solution)/shard_map/attention_forward/pallas_call | solution.py:141
  330.5 16.7 %feed_forward.1 = (f32[512,1024]{1,0:T(8,128)}, f32[512,4096]{1,0:T(8,128)}, bf16[8,512,512]{2,1,0:T(8,128)(2,1)}) custom-call(bf16[512,1024]{1,0:T(8,128)(2,1)} %multiply_convert_fusion.2.value_ref, bf16[32,256,1024]{2,1,0:T(8,128)(2,1)} %bitcast.49.first_ref.second_ref, bf16[32,256,1024]{2,1,0:T(8,128)(2,1)} %bitcast.49.first_ref.second_ref, ...), custom_call_target="tpu_custom_call" | custom-call | flops 8589934592 | bytes 33554432 | tf_op jit(solution)/shard_map/feed_forward/pallas_call | solution.py:310
  377.2 25.1 %all-gather.15.cloned.1.call-done = bf16[2176,1024]{1,0:T(8,128)(2,1)} async-done(((bf16[272,1024]{1,0:T(8,128)(2,1)}), bf16[2176,1024]{1,0:T(8,128)(2,1)}) %all-gather.15.cloned.1.call-update) | async-done | bytes 4456464 | tf_op jit(solution)/shard_map/all_gather | solution.py:1014
  410.1 16.6 %head_logits.2 = (f32[4,1000,1024]{2,1,0:T(8,128)}, f32[1,1024]{1,0:T(1,128)}, f32[1,1024]{1,0:T(1,128)}, f32[1,1024]{1,0:T(1,128)}) custom-call(bf16[1024,1024]{1,0:T(8,128)(2,1)} %bitcast.298, bf16[4,1000,1024]{2,1,0:T(8,128)(2,1)} %bitcast.4.table_ref, s32[1,1024]{1,0:T(1,128)} %get-tuple-element.451.wanted_ref.refs_3_), custom_call_target="tpu_custom_call" | custom-call | flops 8388608000 | bytes 24576000 | tf_op jit(solution)/shard_map/head_logits/pallas_call | solution.py:643
  427.8 16.6 %head_logits.3 = (f32[4,1000,1024]{2,1,0:T(8,128)}, f32[1,1024]{1,0:T(1,128)}, f32[1,1024]{1,0:T(1,128)}, f32[1,1024]{1,0:T(1,128)}) custom-call(bf16[1024,1024]{1,0:T(8,128)(2,1)} %bitcast.296, bf16[4,1000,1024]{2,1,0:T(8,128)(2,1)} %bitcast.4.table_ref, s32[1,1024]{1,0:T(1,128)} %get-tuple-element.452.wanted_ref.refs_8_), custom_call_target="tpu_custom_call" | custom-call | flops 8388608000 | bytes 24576000 | tf_op jit(solution)/shard_map/head_logits/pallas_call | solution.py:643
  453.5 15.5 %head_row_grads.2 = bf16[1024,1024]{1,0:T(8,128)(2,1)} custom-call(f32[4,1000,1024]{2,1,0:T(8,128)} %get-tuple-element.182.logits_ref.refs_0_, f32[1,1024]{1,0:T(1,128)} %log_add_fusion.1.log_norm_ref.refs_1_, f32[1,1024]{1,0:T(1,128)} %bitcast.325, s32[1,1024]{1,0:T(1,128)} %get-tuple-element.451.wanted_ref.refs_3_, ...), custom_call_target="tpu_custom_call" | custom-call | flops 8388608000 | bytes 24576000 | tf_op jit(solution)/shard_map/head_row_grads/pallas_call | solution.py:698
  480.9 15.6 %head_row_grads.3 = bf16[1024,1024]{1,0:T(8,128)(2,1)} custom-call(f32[4,1000,1024]{2,1,0:T(8,128)} %get-tuple-element.190.logits_ref.refs_5_, f32[1,1024]{1,0:T(1,128)} %get-tuple-element.374.log_norm_ref.refs_6_, f32[1,1024]{1,0:T(1,128)} %bitcast.329, s32[1,1024]{1,0:T(1,128)} %get-tuple-element.452.wanted_ref.refs_8_, ...), custom_call_target="tpu_custom_call" | custom-call | flops 8388608000 | bytes 24576000 | tf_op jit(solution)/shard_map/head_row_grads/pallas_call | solution.py:698
  496.5 27.0 %head_table_grads.1.refs_2_ = f32[4,1000,1024]{2,1,0:T(8,128)} custom-call(f32[4,1000,1024]{2,1,0:T(8,128)} %get-tuple-element.182.logits_ref.refs_0_, f32[1,1024]{1,0:T(1,128)} %log_add_fusion.1.log_norm_ref.refs_1_, f32[1,1024]{1,0:T(1,128)} %bitcast.326, s32[1,1024]{1,0:T(1,128)} %get-tuple-element.451.wanted_ref.refs_3_, bf16[1024,1024]{1,0:T(8,128)(2,1)} %bitcast.299, ...), custom_call_target="tpu_custom_call" | custom-call | flops 16777216000 | bytes 49152000 | tf_op jit(solution)/shard_map/head_table_grads/pallas_call | solution.py:750
  523.5 17.1 %reduce-scatter.8.cloned.1.call-done = bf16[128,1024]{1,0:T(8,128)(2,1)} async-done(((bf16[1024,1024]{1,0:T(8,128)(2,1)}), bf16[128,1024]{1,0:T(8,128)(2,1)}) %reduce-scatter.8.cloned.1.call-update) | async-done | bytes 262160 | tf_op jit(solution)/shard_map/reduce_scatter | solution.py:1058
  546.8 18.9 %feed_forward_back.1 = (bf16[512,4096]{1,0:T(8,128)(2,1)}, f32[512,1024]{1,0:T(8,128)}) custom-call(bf16[512,1024]{1,0:T(8,128)(2,1)} %get-tuple-element.377.grad_ref, f32[512,4096]{1,0:T(8,128)} %get-tuple-element.194.pre_ref, bf16[32,256,1024]{2,1,0:T(8,128)(2,1)} %bitcast.49.first_ref.second_ref, bf16[32,256,1024]{2,1,0:T(8,128)(2,1)} %bitcast.49.first_ref.second_ref), custom_call_target="tpu_custom_call" | custom-call | flops 8589934592 | bytes 33554432 | tf_op jit(solution)/shard_map/feed_forward_back/pallas_call | solution.py:360
  574.8 26.8 %attention_backward.1 = (bf16[512,1024]{1,0:T(8,128)(2,1)S(1)}, bf16[2,512,1024]{2,1,0:T(8,128)(2,1)S(1)}, bf16[2,1152,1024]{2,1,0:T(8,128)(2,1)}) custom-call(bf16[512,3072]{1,0:T(8,128)(2,1)} %copy-done.7, bf16[512,3072]{1,0:T(8,128)(2,1)} %copy-done.7, bf16[512,3072]{1,0:T(8,128)(2,1)} %copy-done.7, bf16[1152,2048]{1,0:T(8,128)(2,1)} %matmul_packed.5.refs_3_.refs_4_, ...), custom_call_target="tpu_custom_call" | custom-call | flops 8724152320 | bytes 25165824 | tf_op jit(solution)/shard_map/attention_backward/pallas_call | solution.py:172
  601.6 9.1 matmul_packed_back.4
  713.2 9.1 gradient_piece.12
  722.3 9.0 gradient_piece.13
  741.6 19.1 %collective-permute-done.58 = f32[3200]{0:T(1024)S(1)} collective-permute-done((f32[3200]{0:T(1024)S(1)}, f32[3200]{0:T(1024)S(1)}, u32[]{:S(2)}, u32[]{:S(2)}) %collective-permute-start.58) | collective-permute-done | bytes 12832 | tf_op jit(solution)/shard_map/ppermute | solution.py:561
  773.1 9.1 gradient_piece.15
  788.5 24.9 %spread_piece.2 = (bf16[2,1000,512]{2,1,0:T(8,128)(2,1)S(1)}, bf16[2,1000,512]{2,1,0:T(8,128)(2,1)S(1)}) custom-call(s32[1,4096]{1,0:T(1,128)S(1)} %bitcast.262, bf16[4096,1024]{1,0:T(8,128)(2,1)} %all-gather.9.cloned.1.call-done.refs_1_, f32[4,1000,1024]{2,1,0:T(8,128)} %head_table_grads.1.refs_2_), custom_call_target="tpu_custom_call" | custom-call | flops 16777216000 | bytes 25165824 | tf_op jit(solution)/shard_map/spread_piece/pallas_call | solution.py:794
  846.3 26.5 %spread_piece.3 = (f32[2,1000,512]{2,1,0:T(8,128)S(1)}, f32[2,1000,512]{2,1,0:T(8,128)}) custom-call(s32[1,4096]{1,0:T(1,128)S(1)} %bitcast.263, bf16[4096,1024]{1,0:T(8,128)(2,1)} %all-gather.9.cloned.1.call-done.refs_1_, f32[4,1000,1024]{2,1,0:T(8,128)} %head_table_grads.1.refs_2_), custom_call_target="tpu_custom_call" | custom-call | flops 16777216000 | bytes 25165824 | tf_op jit(solution)/shard_map/spread_piece/pallas_call | solution.py:794
  934.4 8.6 collective-permute-done.83
  (715 shorter events, 519.2 us)
Async XLA Ops:
  7.2 56.6 %all-gather.11.cloned.1.call-start = ((), (), s32[]{:S(2)}) async-start(), calls=%async_computation.7 | async-start | bytes 2457600 | tf_op jit(solution)/shard_map/all_gather | solution.py:570
  12.0 116.1 %all-gather.13.cloned.1.call-start = ((), (), s32[]{:S(2)}) async-start(), calls=%async_computation.8 | async-start | bytes 2621440 | tf_op jit(solution)/shard_map/all_gather | solution.py:570
  20.1 213.5 %reduce-scatter.4.cloned.1.call-start = ((), (), s32[]{:S(2)}) async-start(), calls=%async_computation.3 | async-start | bytes 9437184 | tf_op jit(solution)/shard_map/reduce_scatter | solution.py:913
  69.7 64.4 %collective-permute-start.4 = (bf16[4,240,1024]{2,1,0:T(8,128)(2,1)}, bf16[4,240,1024]{2,1,0:T(8,128)(2,1)}, u32[]{:S(2)}, u32[]{:S(2)}) collective-permute-start(bf16[4,240,1024]{2,1,0:T(8,128)(2,1)} %bitcast.2), channel_id=1, source_target_pairs={{0,2},{2,0},{1,3},{3,1},{4,6},{6,4},{5,7},{7,5},{8,10},{10,8},{9,1... | collective-permute-start | bytes 5898248 | tf_op jit(solution)/shard_map/ppermute | solution.py:210
  71.3 62.9 %collective-permute-start.5 = (bf16[4,240,1024]{2,1,0:T(8,128)(2,1)}, bf16[4,240,1024]{2,1,0:T(8,128)(2,1)}, u32[]{:S(2)}, u32[]{:S(2)}) collective-permute-start(bf16[4,240,1024]{2,1,0:T(8,128)(2,1)} %bitcast.2), channel_id=1, source_target_pairs={{0,4},{4,0},{1,5},{5,1},{2,6},{6,2},{3,7},{7,3},{8,12},{12,8},{9,1... | collective-permute-start | bytes 5898248 | tf_op jit(solution)/shard_map/ppermute | solution.py:210
  134.2 268.0 %all-gather.15.cloned.1.call-start = ((), (), s32[]{:S(2)}) async-start(), calls=%async_computation.9 | async-start | bytes 5013504 | tf_op jit(solution)/shard_map/all_gather | solution.py:1014
  153.1 58.7 %collective-permute-start.11 = (bf16[4,240,1024]{2,1,0:T(8,128)(2,1)}, bf16[4,240,1024]{2,1,0:T(8,128)(2,1)}, u32[]{:S(2)}, u32[]{:S(2)}) collective-permute-start(bf16[4,240,1024]{2,1,0:T(8,128)(2,1)} %collective-permute-done.4), channel_id=1, source_target_pairs={{0,1},{1,0},{2,3},{3,2},{4,5},{5,4},{6,7},{7,6},{8,9},{9,8},{10,11... | collective-permute-start | bytes 5898248 | tf_op jit(solution)/shard_map/ppermute | solution.py:210
  180.9 51.4 %collective-permute-start.8 = (bf16[4,256,1024]{2,1,0:T(8,128)(2,1)}, bf16[4,256,1024]{2,1,0:T(8,128)(2,1)}, u32[]{:S(2)}, u32[]{:S(2)}) collective-permute-start(bf16[4,256,1024]{2,1,0:T(8,128)(2,1)} %bitcast.3), channel_id=1, source_target_pairs={{0,2},{2,0},{1,3},{3,1},{4,6},{6,4},{5,7},{7,5},{8,10},{10,8},{9,1... | collective-permute-start | bytes 6291464 | tf_op jit(solution)/shard_map/ppermute | solution.py:210
  183.0 58.6 %collective-permute-start.20 = (bf16[4,256,1024]{2,1,0:T(8,128)(2,1)}, bf16[4,256,1024]{2,1,0:T(8,128)(2,1)}, u32[]{:S(2)}, u32[]{:S(2)}) collective-permute-start(bf16[4,256,1024]{2,1,0:T(8,128)(2,1)} %bitcast.3), channel_id=1, source_target_pairs={{0,1},{1,0},{2,3},{3,2},{4,5},{5,4},{6,7},{7,6},{8,9},{9,8},{10,11... | collective-permute-start | bytes 6291464 | tf_op jit(solution)/shard_map/ppermute | solution.py:210
  247.8 72.4 %collective-permute-start.21 = (bf16[4,256,1024]{2,1,0:T(8,128)(2,1)}, bf16[4,256,1024]{2,1,0:T(8,128)(2,1)}, u32[]{:S(2)}, u32[]{:S(2)}) collective-permute-start(bf16[4,256,1024]{2,1,0:T(8,128)(2,1)} %collective-permute-done.8), channel_id=1, source_target_pairs={{0,1},{1,0},{2,3},{3,2},{4,5},{5,4},{6,7},{7,6},{8,9},{9,8},{10,11... | collective-permute-start | bytes 6291464 | tf_op jit(solution)/shard_map/ppermute | solution.py:210
  351.4 172.2 %reduce-scatter.6.cloned.1.call-start = ((), (), s32[]{:S(2)}) async-start(), calls=%async_computation.4 | async-start | bytes 2359296 | tf_op jit(solution)/shard_map/reduce_scatter | solution.py:1058
  358.0 51.4 %collective-permute-start.32 = (bf16[4,512,512]{2,1,0:T(8,128)(2,1)}, bf16[4,512,512]{2,1,0:T(8,128)(2,1)}, u32[]{:S(2)}, u32[]{:S(2)}) collective-permute-start(bf16[4,512,512]{2,1,0:T(8,128)(2,1)} %get-tuple-element.403), channel_id=1, source_target_pairs={{0,1},{1,0},{2,3},{3,2},{4,5},{5,4},{6,7},{7,6},{8,9},{9,8},{10,11... | collective-permute-start | bytes 6291464 | tf_op jit(solution)/shard_map/ppermute | solution.py:210
  469.1 71.6 %reduce-scatter.8.cloned.1.call-start = ((), (), s32[]{:S(2)}) async-start(), calls=%async_computation.5 | async-start | bytes 2359296 | tf_op jit(solution)/shard_map/reduce_scatter | solution.py:1058
  496.5 292.0 %all-gather.9.cloned.1.call-start = ((), (), s32[]{:S(2)}) async-start(), calls=%async_computation.6 | async-start | bytes 9437184 | tf_op jit(solution)/shard_map/all_gather | solution.py:1138
  565.8 61.9 %collective-permute-start.46 = (bf16[1,512,4096]{2,1,0:T(8,128)(2,1)}, bf16[1,512,4096]{2,1,0:T(8,128)(2,1)}, u32[]{:S(2)}, u32[]{:S(2)}) collective-permute-start(bf16[1,512,4096]{2,1,0:T(8,128)(2,1)} %bitcast.273), channel_id=1, source_target_pairs={{0,1},{1,0},{2,3},{3,2},{4,5},{5,4},{6,7},{7,6},{8,9},{9,8},{10,11... | collective-permute-start | bytes 12582920 | tf_op jit(solution)/shard_map/ppermute | solution.py:210
  565.9 59.1 %collective-permute-start.47 = (bf16[1,512,1024]{2,1,0:T(8,128)(2,1)}, bf16[1,512,1024]{2,1,0:T(8,128)(2,1)S(1)}, u32[]{:S(2)}, u32[]{:S(2)}) collective-permute-start(bf16[1,512,1024]{2,1,0:T(8,128)(2,1)} %bitcast.250), channel_id=1, source_target_pairs={{0,1},{1,0},{2,3},{3,2},{4,5},{5,4},{6,7},{7,6},{8,9},{9,8},{10,11... | collective-permute-start | bytes 3145736 | tf_op jit(solution)/shard_map/ppermute | solution.py:210
  572.3 54.0 %collective-permute-start.48 = (bf16[1,512,1024]{2,1,0:T(8,128)(2,1)S(1)}, bf16[1,512,1024]{2,1,0:T(8,128)(2,1)S(1)}, u32[]{:S(2)}, u32[]{:S(2)}) collective-permute-start(bf16[1,512,1024]{2,1,0:T(8,128)(2,1)S(1)} %get-tuple-element.375.refs_16_), channel_id=1, source_target_pairs={{0,1},{1,0},{2,3},{3,2},{4,5},{5,4},{6,7},{7,6},{8,9},{9,8},{10,11... | collective-permute-start | bytes 3145736 | tf_op jit(solution)/shard_map/ppermute | solution.py:210
  672.2 59.0 %collective-permute-start.56 = (bf16[9,256,512]{2,1,0:T(8,128)(2,1)}, bf16[9,256,512]{2,1,0:T(8,128)(2,1)}, u32[]{:S(2)}, u32[]{:S(2)}) collective-permute-start(bf16[9,256,512]{2,1,0:T(8,128)(2,1)} %copy-done.44), channel_id=1, source_target_pairs={{0,2},{2,0},{1,3},{3,1},{4,6},{6,4},{5,7},{7,5},{8,10},{10,8},{9,1... | collective-permute-start | bytes 7077896 | tf_op jit(solution)/shard_map/ppermute | solution.py:210
  675.0 62.2 %collective-permute-start.57 = (bf16[9,256,512]{2,1,0:T(8,128)(2,1)}, bf16[9,256,512]{2,1,0:T(8,128)(2,1)}, u32[]{:S(2)}, u32[]{:S(2)}) collective-permute-start(bf16[9,256,512]{2,1,0:T(8,128)(2,1)} %copy-done.43), channel_id=1, source_target_pairs={{0,4},{4,0},{1,5},{5,1},{2,6},{6,2},{3,7},{7,3},{8,12},{12,8},{9,1... | collective-permute-start | bytes 7077896 | tf_op jit(solution)/shard_map/ppermute | solution.py:210
  709.8 72.4 %collective-permute-start.59 = (bf16[6,256,512]{2,1,0:T(8,128)(2,1)S(1)}, bf16[6,256,512]{2,1,0:T(8,128)(2,1)S(1)}, u32[]{:S(2)}, u32[]{:S(2)}) collective-permute-start(bf16[6,256,512]{2,1,0:T(8,128)(2,1)S(1)} %gradient_piece.10), channel_id=1, source_target_pairs={{0,2},{2,0},{1,3},{3,1},{4,6},{6,4},{5,7},{7,5},{8,10},{10,8},{9,1... | collective-permute-start | bytes 4718600 | tf_op jit(solution)/shard_map/ppermute | solution.py:210
  713.1 70.8 %collective-permute-start.60 = (bf16[6,256,512]{2,1,0:T(8,128)(2,1)S(1)}, bf16[6,256,512]{2,1,0:T(8,128)(2,1)}, u32[]{:S(2)}, u32[]{:S(2)}) collective-permute-start(bf16[6,256,512]{2,1,0:T(8,128)(2,1)S(1)} %gradient_piece.11), channel_id=1, source_target_pairs={{0,4},{4,0},{1,5},{5,1},{2,6},{6,2},{3,7},{7,3},{8,12},{12,8},{9,1... | collective-permute-start | bytes 4718600 | tf_op jit(solution)/shard_map/ppermute | solution.py:210
  760.7 52.7 %collective-permute-start.62 = (bf16[9,128,512]{2,1,0:T(8,128)(2,1)}, bf16[9,128,512]{2,1,0:T(8,128)(2,1)}, u32[]{:S(2)}, u32[]{:S(2)}) collective-permute-start(bf16[9,128,512]{2,1,0:T(8,128)(2,1)} %get-tuple-element.235), channel_id=1, source_target_pairs={{0,4},{4,0},{1,5},{5,1},{2,6},{6,2},{3,7},{7,3},{8,12},{12,8},{9,1... | collective-permute-start | bytes 3538952 | tf_op jit(solution)/shard_map/ppermute | solution.py:210
  818.8 54.1 %collective-permute-start.67 = (bf16[2,1000,512]{2,1,0:T(8,128)(2,1)S(1)}, bf16[2,1000,512]{2,1,0:T(8,128)(2,1)S(1)}, u32[]{:S(2)}, u32[]{:S(2)}) collective-permute-start(bf16[2,1000,512]{2,1,0:T(8,128)(2,1)S(1)} %get-tuple-element.243), channel_id=1, source_target_pairs={{0,2},{2,0},{1,3},{3,1},{4,6},{6,4},{5,7},{7,5},{8,10},{10,8},{9,1... | collective-permute-start | bytes 6144008 | tf_op jit(solution)/shard_map/ppermute | solution.py:210
  820.6 52.3 %collective-permute-start.68 = (bf16[2,1000,512]{2,1,0:T(8,128)(2,1)S(1)}, bf16[2,1000,512]{2,1,0:T(8,128)(2,1)}, u32[]{:S(2)}, u32[]{:S(2)}) collective-permute-start(bf16[2,1000,512]{2,1,0:T(8,128)(2,1)S(1)} %get-tuple-element.244), channel_id=1, source_target_pairs={{0,4},{4,0},{1,5},{5,1},{2,6},{6,2},{3,7},{7,3},{8,12},{12,8},{9,1... | collective-permute-start | bytes 6144008 | tf_op jit(solution)/shard_map/ppermute | solution.py:210
  (197 other events, 2533.0 us)
Sparse Core Ops, SparseCore 0:
  12.1 46.3 all-gather.10
  60.6 44.7 all-gather.12
  134.3 88.9 reduce-scatter.3
  351.5 50.6 all-gather.14
  469.2 34.6 reduce-scatter.5
  506.0 34.5 reduce-scatter.7
  665.2 87.6 all-gather.8

commit v4 on v3

--- a/solution.py
+++ b/solution.py
@@ -490,7 +490,7 @@
 
 def line_close(state):
     while state[3] > 0:
-        state = line_move(state, line_sends(state))
+        state = line_move(state, lax.optimization_barrier(line_sends(state)))
     value, upward, downward, _ = state
     total = lax.dynamic_index_in_dim(value, lax.axis_index(LINE), 0, False)
     return total + upward.astype(F32) + downward.astype(F32)
@@ -549,11 +549,12 @@
     def __init__(self, value):
         count = lax.axis_size(LINE)
         self.value = value
-        self.steps = [("core", 1), ("x", 1), ("y", 1)]
+        self.steps = [("core", 1)]
         step = 1
         while step < count:
             self.steps.append((LINE, step))
             step *= 2
+        self.steps += [("x", 1), ("y", 1)]
 
     def exchange(self):
         axis, step = self.steps.pop(0)
@@ -763,52 +764,44 @@
     )(*[value for group in groups for value in group])
 
 
-def spread_body(row_of, token_row, grads, table_grad, *refs):
-    outs, total = refs[:2], refs[2]
-    task, step = pl.program_id(0), pl.program_id(1)
-    rows, tokens = total.shape[0], grads.shape[0]
-    first = row_of(task) * rows
-
-    @pl.when(step == 0)
-    def _():
-        total[...] = table_grad[0]
-
-    wanted = token_row[...] - first
-    hit = lax.broadcasted_iota(jnp.int32, (rows, tokens), 0) == wanted
-    total[...] += matmul(jnp.where(hit, 1.0, 0.0).astype(BF16), grads[...])
-
-    for side in (0, 1):
-
-        @pl.when((step == pl.num_programs(1) - 1) & (task // 2 == side))
+def spread_piece(token_row, grads, table_grad, side, rows_of, dtype):
+    part_rows = table_grad.shape[1]
+    tokens = 1024
+    first, second = rows_of
+
+    def row_of(task):
+        return first + task * (second - first)
+
+    def body(token_ref, grads_ref, table_ref, out, total):
+        step = pl.program_id(1)
+
+        @pl.when(step == 0)
         def _():
-            outs[side][0] = total[...].astype(outs[side].dtype)
-
-
-def spread_piece(token_row, grads, table_grad, row_of, dtype):
-    blocks, rows, width = table_grad.shape
-    tokens = 1024
-
-    def body(*refs):
-        spread_body(row_of, *refs)
+            total[...] = table_ref[0]
+
+        wanted = token_ref[...] - row_of(pl.program_id(0)) * part_rows
+        hit = lax.broadcasted_iota(jnp.int32, (part_rows, tokens), 0) == wanted
+        total[...] += matmul(jnp.where(hit, 1.0, 0.0).astype(BF16), grads_ref[...])
+
+        @pl.when(step == pl.num_programs(1) - 1)
+        def _():
+            out[0] = total[...].astype(dtype)
 
     return pl.pallas_call(
         body,
-        grid=(4, grads.shape[0] // tokens),
+        grid=(2, grads.shape[0] // tokens),
         in_specs=[
             pl.BlockSpec((1, tokens), lambda task, step: (0, step)),
-            pl.BlockSpec((tokens, PIECE), lambda task, step: (step, task // 2)),
-            pl.BlockSpec((1, rows, PIECE), lambda task, step: (row_of(task), 0, task // 2)),
-        ],
-        out_specs=[
-            pl.BlockSpec((1, rows, PIECE), lambda task, step: (jnp.minimum(task, 1), 0, 0)),
-            pl.BlockSpec((1, rows, PIECE), lambda task, step: (jnp.maximum(task - 2, 0), 0, 0)),
-        ],
-        out_shape=[jax.ShapeDtypeStruct((2, rows, PIECE), dtype)] * 2,
-        scratch_shapes=[pltpu.VMEM((rows, PIECE), F32)],
+            pl.BlockSpec((tokens, PIECE), lambda task, step: (step, side)),
+            pl.BlockSpec((1, part_rows, PIECE), lambda task, step: (row_of(task), 0, side)),
+        ],
+        out_specs=pl.BlockSpec((1, part_rows, PIECE), lambda task, step: (task, 0, 0)),
+        out_shape=jax.ShapeDtypeStruct((2, part_rows, PIECE), dtype),
+        scratch_shapes=[pltpu.VMEM((part_rows, PIECE), F32)],
         compiler_params=pltpu.CompilerParams(vmem_limit_bytes=48 << 20),
         cost_estimate=pl.CostEstimate(
-            flops=4 * 2 * rows * PIECE * grads.shape[0],
-            bytes_accessed=24 << 20,
+            flops=4 * part_rows * PIECE * grads.shape[0],
+            bytes_accessed=12 << 20,
             transcendentals=0,
         ),
         name="spread_piece",
@@ -1011,8 +1004,8 @@
     )
     side_rows = jnp.zeros((16 * width,), BF16).at[: 5 * keep].set(side).reshape(16, width)
     half = keep // 2
-    head_all = lax.all_gather(
-        jnp.concatenate([picked_rows, side_rows], 0), SHARE, axis=0, tiled=False
+    head_one = lax.all_gather(
+        jnp.concatenate([picked_rows[:half], side_rows], 0), SHARE, axis=0, tiled=False
     )
     slot_spare = -slots % BLOCK
     slot_tall = jnp.concatenate([slot_rows, jnp.zeros((slot_spare, 3 * width), BF16)], 0)
@@ -1027,10 +1020,10 @@
             grouped_transpose(attended),
         )
     ]
-    rows_one = head_all[:, :half].reshape(share_count * half, width)
-    rows_two = head_all[:, half:keep].reshape(share_count * half, width)
-    side_all = head_all[:, keep:].reshape(share_count, 16 * width)[:, : 5 * keep]
-    rows_one, rows_two, halves = lax.optimization_barrier((rows_one, rows_two, halves))
+    rows_one = head_one[:, :half].reshape(share_count * half, width)
+    side_all = head_one[:, half:].reshape(share_count, 16 * width)[:, : 5 * keep]
+    rows_one, next_rows, halves = lax.optimization_barrier((rows_one, picked_rows[half:], halves))
+    rows_two = lax.all_gather(next_rows, SHARE, axis=0, tiled=True)
     side_all = side_all.reshape(share_count, 5, 2, half).astype(F32)
     side_all = side_all.transpose(1, 2, 0, 3).reshape(5, 2, share_count * half)
     wanted_all = (side_all[0] * 256.0 + side_all[1]).astype(jnp.int32)
@@ -1074,15 +1067,19 @@
         grad = grad if grad.ndim == 3 else grad[None]
         return grad, swapped(grad, "core")
 
-    ffn_weights = [
-        ([product(halves[0], with_other(grad_pre))], ffn_in_m.shape[1] // width, True),
+    out_weights = [
         (
             [product(halves[1], with_other(grad_branch))],
             rows_ffn_out * device_count // width,
             False,
         ),
     ]
-    ffn_rows = rows_ffn + rows_ffn_out
+    ffn_weights = [
+        ([product(halves[0], with_other(grad_pre))], ffn_in_m.shape[1] // width, True),
+    ]
+    out_sends = gradient_sends(out_weights, chip_place())
+    out_sends, grad_norm_two = lax.optimization_barrier((out_sends, grad_norm_two))
+    out_arrived = [swapped(send, axis) for send, axis in zip(out_sends, ("x", "y"))]
     grad_res_two, grad_gain_two = norm_backward(grad_norm_two, unit_two, scale_two, gains[:, 1])
     grad_residual = grad_output_rows + grad_res_two
 
@@ -1092,6 +1089,7 @@
     grad_query, grad_own, grad_other = attention_backward(
         projected, memory_pairs, marks, log_total, grad_attended
     )
+    grad_other, out_arrived = lax.optimization_barrier((grad_other, out_arrived))
     grad_other_rows = matmul_packed_back(grad_other, mixer_all, thin, 1).astype(BF16)
     back_memory = passed_along(grad_other_rows[:segment], -1)
     returned = []
@@ -1121,66 +1119,78 @@
     query_pair, own_pair = with_other(grad_query), with_other(grad_own)
     other_pair = with_other(grad_other)
     slot_pair = with_other(jnp.pad(grad_compressed, ((0, slot_spare), (0, 0))))
+    small = jnp.concatenate(
+        [
+            jnp.stack([grad_gain_one, grad_gain_two, grad_gain_three], 1).reshape(-1),
+            jnp.full((128,), loss_local, F32),
+        ]
+    )
+    grad_scaled, place, query_pair, own_pair, other_pair = lax.optimization_barrier(
+        (grad_scaled, place, query_pair, own_pair, other_pair)
+    )
+    small = SmallSum(small)
+    share_grads = lax.all_gather(grad_scaled, SHARE, axis=0, tiled=True)
     mixer_weights = [
         ([product(halves[2], query_pair)], 1, True),
         ([product(halves[2], own_pair, 0), product(halves[3], other_pair, 0)], 1, True),
         ([product(halves[2], own_pair, 1), product(halves[3], other_pair, 1)], 1, True),
         ([product(halves[4], slot_pair)], 3, False),
     ]
-    small = jnp.concatenate(
-        [
-            jnp.stack([grad_gain_one, grad_gain_two, grad_gain_three], 1).reshape(-1),
-            jnp.full((128,), loss_local, F32),
-        ]
-    )
-    grad_scaled, place = lax.optimization_barrier((grad_scaled, place))
-    small = SmallSum(small)
-    share_grads = lax.all_gather(grad_scaled, SHARE, axis=0, tiled=True)
     mixer_sends = gradient_sends(mixer_weights, place)
     mixer_sends, place, arrived = lax.optimization_barrier(
         (mixer_sends, place, small.exchange())
     )
     small.value += arrived
     mixer_arrived = [swapped(send, axis) for send, axis in zip(mixer_sends, ("x", "y"))]
-    ffn_sums = plane_sums(ffn_arrived, gradient_keeps(ffn_weights, place))
-    ffn_sums, place, arrived = lax.optimization_barrier((ffn_sums, place, small.exchange()))
+    out_sums = plane_sums(out_arrived, gradient_keeps(out_weights, place))
+    out_sums, place, arrived = lax.optimization_barrier((out_sums, place, small.exchange()))
     small.value += arrived
+    ffn_keeps = gradient_keeps(ffn_weights, place)
+    ffn_keeps, place = lax.optimization_barrier((ffn_keeps, place))
     mixer_keeps = gradient_keeps(mixer_weights, place)
+    ffn_arrived, mixer_keeps = lax.optimization_barrier((ffn_arrived, mixer_keeps))
+    ffn_sums = plane_sums(ffn_arrived, ffn_keeps)
     mixer_sums = plane_sums(mixer_arrived, mixer_keeps)
-    token_row, mixer_sums, arrived = lax.optimization_barrier(
-        (share_row[None, :], mixer_sums, small.exchange())
+    token_row, ffn_sums, mixer_sums, arrived = lax.optimization_barrier(
+        (share_row[None, :], ffn_sums, mixer_sums, small.exchange())
     )
     small.value += arrived
-    table_sends = spread_piece(
-        token_row, share_grads, grad_table, lambda t: jnp.where(t < 2, 2 * t + 1, t), BF16
-    )
-    ffn_others, mixer_others = plane_others(ffn_sums), plane_others(mixer_sums)
-    table_sends, token_row, ffn_others, mixer_others, arrived = lax.optimization_barrier(
-        (table_sends, token_row, ffn_others, mixer_others, small.exchange())
-    )
-    small.value += arrived
-    table_arrived = [swapped(send, axis) for send, axis in zip(table_sends, ("x", "y"))]
-    lines = [
-        line_open(line_parts(ffn_weights, ffn_sums, ffn_others)),
-        line_open(line_parts(mixer_weights, mixer_sums, mixer_others)),
-    ]
-    lines = [line_move(line, line_sends(line)) for line in lines]
-    table_keeps = spread_piece(
-        token_row, share_grads, grad_table, lambda t: jnp.where(t < 2, 2 * t, t - 2), F32
-    )
-    table_keeps, table_arrived, moved, arrived = lax.optimization_barrier(
-        (table_keeps, table_arrived, [line[1:3] for line in lines], small.exchange())
-    )
-    small.value += arrived
-    lines = [(line[0], *pair, line[3]) for line, pair in zip(lines, moved)]
-    lines = [line_move(line, line_sends(line)) for line in lines]
-    summed, mixer_grads = [line_close(line) for line in lines]
-    ffn_grads, attn_out_grad = summed[:ffn_rows], summed[ffn_rows : ffn_rows + rows_out]
+    def spread(token_row, side, rows_of, dtype):
+        piece = spread_piece(token_row, share_grads, grad_table, side, rows_of, dtype)
+        return lax.optimization_barrier((piece, token_row))
+
+    send_one, token_row = spread(token_row, 0, (1, 3), BF16)
+    send_two, token_row = spread(token_row, 1, (2, 3), BF16)
+    table_arrived = [swapped(send_one, "x"), swapped(send_two, "y")]
+    others = [plane_others(sums) for sums in (out_sums, ffn_sums, mixer_sums)]
+    others, token_row = lax.optimization_barrier((others, token_row))
+    line = line_open(
+        jnp.concatenate(
+            [
+                line_parts(out_weights, out_sums, others[0]),
+                line_parts(ffn_weights, ffn_sums, others[1]),
+                line_parts(mixer_weights, mixer_sums, others[2]),
+            ],
+            1,
+        )
+    )
+    moves, token_row = lax.optimization_barrier((line_sends(line), token_row))
+    line = line_move(line, moves)
+    keep_one, token_row = spread(token_row, 0, (0, 2), F32)
+    keep_two, token_row = spread(token_row, 1, (0, 1), F32)
+    table_keeps = [keep_one, keep_two]
+    table_keeps, table_arrived, moved = lax.optimization_barrier(
+        (table_keeps, table_arrived, line[1:3])
+    )
+    summed = line_close((line[0], *moved, line[3]))
+    ends = (rows_ffn_out, rows_ffn_out + rows_ffn, rows_ffn_out + rows_ffn + rows_out)
+    ffn_out_grad, ffn_in_grad, attn_out_grad, mixer_grads = jnp.split(summed, ends)
     halves_new = []
     for arrived, keep_part, axis in zip(table_arrived, table_keeps, ("y", "x")):
         other = (keep_part[1] + arrived[1].astype(F32)).astype(BF16)
         mine = keep_part[0] + arrived[0].astype(F32)
         halves_new.append(mine + swapped(other, axis).astype(F32))
+    halves_new, small.value = lax.optimization_barrier((halves_new, small.value))
     grad_table = jnp.concatenate(halves_new, 1)
     if lax.axis_size("far") > 1:
         grad_table = lax.psum_scatter(
@@ -1201,8 +1211,8 @@
         side_by_side(mixer_grads[:low], 3),
         attn_out_grad,
         mixer_grads[low:high],
-        side_by_side(ffn_grads[:rows_ffn], rows_ffn // attn_in_m.shape[0]),
-        ffn_grads[rows_ffn:],
+        side_by_side(ffn_in_grad, rows_ffn // attn_in_m.shape[0]),
+        ffn_out_grad,
         gain_grads.reshape(gains_m.shape),
     )
     results = []

time: 965 us -> 925 us (0.959)
  waiting for transfers between devices: 167 us -> 134 us
    ppermute x5, waiting for transfers between devices: 25.8 us -> 1.93 us  [exchange(): return lax.ppermute(self.value, axis, [(i, i ^ step) for i in range(size)])]
    all_gather x1 -> x2, waiting for transfers between devices: 25.1 us -> 2.72 us  [the longest x1 2.72 us: per_device(): lax.all_gather(jnp.concatenate([picked_rows[:half], side_rows], 0), SHARE...]
    ppermute x6 -> x3, starting transfers between devices: 23.5 us -> 11.4 us  [line_move(): upward = lax.ppermute(sends[0], LINE, up)]
    ppermute x6 -> x3, waiting for transfers between devices: 2.53 us -> 14.4 us  [line_move(): upward = lax.ppermute(sends[0], LINE, up)]
    ppermute x50 -> x54, starting transfers between devices: 43.8 us -> 50.8 us  [swapped(): return lax.ppermute(value, axis, [(0, 1), (1, 0)])]
    unnamed x272 -> x225, local copies, waits for them, and re-layouts: 32.9 us -> 27.9 us
    ppermute x50 -> x54, waiting for transfers between devices: 66.5 us -> 69.9 us  [swapped(): return lax.ppermute(value, axis, [(0, 1), (1, 0)])]
    pallas_call x2 -> x4, Pallas kernels: 51.3 us -> 53.7 us  [spread_piece(): pl.pallas_call(body, grid=(2, grads.shape[0] // tokens), in_specs=[pl.Blo...]
  transfers between devices with their start and end apart: 91 -> 90, of which waited for: 22 -> 25; matrix products, arithmetic and copies ran while one was open for 27% -> 28% of each run, Pallas kernels for 28% -> 31%
where the time goes in v4:
time: 925 us; the launch traced here: 915 us
  Pallas kernels  332 us (36%)
  local copies, waits for them, and re-layouts  207 us (22%)
  waiting for transfers between devices  134 us (14%)
  other arithmetic  101 us (11%)
  starting transfers between devices  100 us (11%)
  between operations  19.2 us (2%)
  blocking collectives  13.2 us (1%)
    ppermute x54, waiting for transfers between devices, swapped(): return lax.ppermute(value, axis, [(0, 1), (1, 0)])  69.9 us
    pallas_call x12, Pallas kernels, gradient_piece(): pl.pallas_call(body, grid_spec=pltpu.PrefetchScalarGridSpec(num_scalar_pr...  67.6 us
    pallas_call x4, Pallas kernels, spread_piece(): pl.pallas_call(body, grid=(2, grads.shape[0] // tokens), in_specs=[pl.Blo...  53.7 us
    ppermute x54, starting transfers between devices, swapped(): return lax.ppermute(value, axis, [(0, 1), (1, 0)])  50.8 us
    dynamic_update_slice x20, local copies, waits for them, and re-layouts, plane_gather(): result = lax.dynamic_update_slice(result, part[:, None, None, None], start)  44.2 us
    pallas_call x2, Pallas kernels, head_logits(): pl.pallas_call(body, grid=(parts,), in_specs=[pl.BlockSpec((count, width)...  33.2 us
    pallas_call x2, Pallas kernels, head_row_grads(): pl.pallas_call(body, grid=(parts,), in_specs=[pl.BlockSpec((1, part_rows,...  30.9 us
    unnamed x225, local copies, waits for them, and re-layouts  27.9 us
  transfers between devices with their start and end apart: 90, of which 25 were waited for; matrix products, arithmetic and copies ran while one was open for 28% of the time, Pallas kernels for 31%

profile of v4, /device:TPU:0, one launch (start us, length us, event | category | flops | bytes accessed | tf_op | source)
XLA Modules:
  0.0 914.9 jit_solution(15960733128782441253)
XLA Ops:
  20.2 13.2 %all-gather = s32[1,4096]{1,0:T(1,128)S(1)} all-gather(s32[1,512]{1,0:T(1,128)S(1)} %copy-done.96), channel_id=2, replica_groups=mesh['batch'=4,'far'=1,'y'=2,'x'=2,'core'=2] {'batch','core'}, dimensions={1}, use_global_device_ids=true | all-gather | bytes 18432 | tf_op jit(solution)/shard_map/all_gather | solution.py:841
  33.3 29.0 %collective-permute-done = bf16[1000,1024]{1,0:T(8,128)(2,1)} collective-permute-done((bf16[1000,1024]{1,0:T(8,128)(2,1)S(1)}, bf16[1000,1024]{1,0:T(8,128)(2,1)}, u32[]{:S(2)}, u32[]{:S(2)}) %collective-permute-start) | collective-permute-done | bytes 2048032 | tf_op jit(solution)/shard_map/ppermute | solution.py:210
  82.8 9.0 collective-permute-done.2
  95.6 25.2 %gather_fusion = bf16[4096,1024]{1,0:T(8,128)(2,1)} fusion(bf16[4000,1024]{1,0:T(8,128)(2,1)} %constant_dynamic-update-slice_fusion.12, s32[4096]{0:T(1024)S(1)} %maximum_clamp_fusion), kind=kCustom, calls=%fused_computation | custom fusion | bytes 16793600 | tf_op jit(solution)/shard_map/gather | solution.py:893
  183.1 11.4 %copy.173 = bf16[4,1000,1024]{1,2,0:T(8,128)(2,1)} copy(bf16[4,1000,1024]{2,1,0:T(8,128)(2,1)} %bitcast.4.table_ref) | data formatting | bytes 16384000 | tf_op jit(solution)/shard_map/reshape | solution.py:908
  293.9 17.3 %attention_forward.1 = (bf16[512,1024]{1,0:T(8,128)(2,1)S(1)}, f32[8,1,512]{2,1,0:T(1,128)S(1)}) custom-call(bf16[512,3072]{1,0:T(8,128)(2,1)S(1)} %matmul_packed.3.refs_0_.refs_1_.refs_2_, bf16[512,3072]{1,0:T(8,128)(2,1)S(1)} %matmul_packed.3.refs_0_.refs_1_.refs_2_, bf16[512,3072]{1,0:T(8,128)(2,1)S(1)} %matmul_packed.3.refs_0_.refs_1_.refs_2_, ...), custom_call_target="tpu_custom_call" | custom-call | flops 3489660928 | bytes 12582912 | tf_op jit(solution)/shard_map/attention_forward/pallas_call | solution.py:141
  329.6 16.7 %feed_forward.1 = (f32[512,1024]{1,0:T(8,128)}, f32[512,4096]{1,0:T(8,128)}, bf16[8,512,512]{2,1,0:T(8,128)(2,1)}) custom-call(bf16[512,1024]{1,0:T(8,128)(2,1)} %multiply_convert_fusion.2.value_ref, bf16[32,256,1024]{2,1,0:T(8,128)(2,1)} %bitcast.49.first_ref.second_ref, bf16[32,256,1024]{2,1,0:T(8,128)(2,1)} %bitcast.49.first_ref.second_ref, ...), custom_call_target="tpu_custom_call" | custom-call | flops 8589934592 | bytes 33554432 | tf_op jit(solution)/shard_map/feed_forward/pallas_call | solution.py:310
  390.7 16.6 %head_logits.2 = (f32[4,1000,1024]{2,1,0:T(8,128)}, f32[1,1024]{1,0:T(1,128)}, f32[1,1024]{1,0:T(1,128)}, f32[1,1024]{1,0:T(1,128)}) custom-call(bf16[1024,1024]{1,0:T(8,128)(2,1)} %bitcast.265, bf16[4,1000,1024]{2,1,0:T(8,128)(2,1)} %bitcast.4.table_ref, s32[1,1024]{1,0:T(1,128)} %get-tuple-element.517.wanted_ref.refs_3_), custom_call_target="tpu_custom_call" | custom-call | flops 8388608000 | bytes 24576000 | tf_op jit(solution)/shard_map/head_logits/pallas_call | solution.py:644
  419.7 16.6 %head_logits.3 = (f32[4,1000,1024]{2,1,0:T(8,128)}, f32[1,1024]{1,0:T(1,128)}, f32[1,1024]{1,0:T(1,128)}, f32[1,1024]{1,0:T(1,128)}) custom-call(bf16[1024,1024]{1,0:T(8,128)(2,1)} %all-gather.10.cloned.1.call-done.rows_ref.refs_9_, bf16[4,1000,1024]{2,1,0:T(8,128)(2,1)} %bitcast.4.table_ref, s32[1,1024]{1,0:T(1,128)} %get-tuple-element.518.wanted_ref.refs_8_), custom_call_target="tpu_custom_call" | custom-call | flops 8388608000 | bytes 24576000 | tf_op jit(solution)/shard_map/head_logits/pallas_call | solution.py:644
  436.3 15.4 %head_row_grads.2 = bf16[1024,1024]{1,0:T(8,128)(2,1)} custom-call(f32[4,1000,1024]{2,1,0:T(8,128)} %get-tuple-element.214.logits_ref.refs_0_, f32[1,1024]{1,0:T(1,128)} %log_add_fusion.1.log_norm_ref.refs_1_, f32[1,1024]{1,0:T(1,128)} %bitcast.292, s32[1,1024]{1,0:T(1,128)} %get-tuple-element.517.wanted_ref.refs_3_, ...), custom_call_target="tpu_custom_call" | custom-call | flops 8388608000 | bytes 24576000 | tf_op jit(solution)/shard_map/head_row_grads/pallas_call | solution.py:699
  463.6 15.5 %head_row_grads.3 = bf16[1024,1024]{1,0:T(8,128)(2,1)} custom-call(f32[4,1000,1024]{2,1,0:T(8,128)} %get-tuple-element.222.logits_ref.refs_5_, f32[1,1024]{1,0:T(1,128)} %get-tuple-element.438.log_norm_ref.refs_6_, f32[1,1024]{1,0:T(1,128)} %bitcast.296, s32[1,1024]{1,0:T(1,128)} %get-tuple-element.518.wanted_ref.refs_8_, ...), custom_call_target="tpu_custom_call" | custom-call | flops 8388608000 | bytes 24576000 | tf_op jit(solution)/shard_map/head_row_grads/pallas_call | solution.py:699
  479.2 26.8 %head_table_grads.1.table_ref = f32[4,1000,1024]{2,1,0:T(8,128)} custom-call(f32[4,1000,1024]{2,1,0:T(8,128)} %get-tuple-element.214.logits_ref.refs_0_, f32[1,1024]{1,0:T(1,128)} %log_add_fusion.1.log_norm_ref.refs_1_, f32[1,1024]{1,0:T(1,128)} %bitcast.293, s32[1,1024]{1,0:T(1,128)} %get-tuple-element.517.wanted_ref.refs_3_, bf16[1024,1024]{1,0:T(8,128)(2,1)} %bitcast.266, ...), custom_call_target="tpu_custom_call" | custom-call | flops 16777216000 | bytes 49152000 | tf_op jit(solution)/shard_map/head_table_grads/pallas_call | solution.py:751
  506.0 18.1 %reduce-scatter.8.cloned.1.call-done = bf16[128,1024]{1,0:T(8,128)(2,1)} async-done(((bf16[1024,1024]{1,0:T(8,128)(2,1)}), bf16[128,1024]{1,0:T(8,128)(2,1)}) %reduce-scatter.8.cloned.1.call-update) | async-done | bytes 262160 | tf_op jit(solution)/shard_map/reduce_scatter | solution.py:1051
  530.9 18.7 %feed_forward_back.1 = (bf16[512,4096]{1,0:T(8,128)(2,1)}, f32[512,1024]{1,0:T(8,128)}) custom-call(bf16[512,1024]{1,0:T(8,128)(2,1)} %copy-done.11, f32[512,4096]{1,0:T(8,128)} %get-tuple-element.228.pre_ref, bf16[32,256,1024]{2,1,0:T(8,128)(2,1)} %bitcast.49.first_ref.second_ref, bf16[32,256,1024]{2,1,0:T(8,128)(2,1)} %bitcast.49.first_ref.second_ref), custom_call_target="tpu_custom_call" | custom-call | flops 8589934592 | bytes 33554432 | tf_op jit(solution)/shard_map/feed_forward_back/pallas_call | solution.py:360
  568.0 26.0 %attention_backward.1 = (bf16[512,1024]{1,0:T(8,128)(2,1)}, bf16[2,512,1024]{2,1,0:T(8,128)(2,1)}, bf16[2,1152,1024]{2,1,0:T(8,128)(2,1)}) custom-call(bf16[512,3072]{1,0:T(8,128)(2,1)} %copy-done.6, bf16[512,3072]{1,0:T(8,128)(2,1)} %copy-done.6, bf16[512,3072]{1,0:T(8,128)(2,1)} %copy-done.6, bf16[1152,2048]{1,0:T(8,128)(2,1)} %matmul_packed.5.refs_3_.refs_4_, ...), custom_call_target="tpu_custom_call" | custom-call | flops 8724152320 | bytes 25165824 | tf_op jit(solution)/shard_map/attention_backward/pallas_call | solution.py:172
  659.3 11.0 %collective-permute-start.56 = (bf16[1,256,1024]{2,1,0:T(8,128)(2,1)}, bf16[1,256,1024]{2,1,0:T(8,128)(2,1)}, u32[]{:S(2)}, u32[]{:S(2)}) collective-permute-start(bf16[1,256,1024]{2,1,0:T(8,128)(2,1)} %pad_bitcast_fusion.1.refs_34_), channel_id=1, source_target_pairs={{0,1},{1,0},{2,3},{3,2},{4,5},{5,4},{6,7},{7,6},{8,9},{9,8},{10,11... | collective-permute-start | bytes 1572872 | tf_op jit(solution)/shard_map/ppermute | solution.py:210
  680.0 8.4 gradient_piece.16
  720.9 9.3 %gradient_piece.22 = f32[6,256,512]{2,1,0:T(8,128)} custom-call(s32[1]{0:T(128)} %bitcast.80.me, bf16[4,128,512]{2,1,0:T(8,128)(2,1)S(1)} %get-tuple-element.249.refs_0_.refs_1_.refs_6_.refs_7_.refs_18_.refs_19_, bf16[4,128,512]{2,1,0:T(8,128)(2,1)S(1)} %get-tuple-element.249.refs_0_.refs_1_.refs_6_.refs_7_.refs_18_.refs_19_, ...), custom_call_target="tpu_custom_call" | custom-call | flops 1610612736 | bytes 18874368 | tf_op jit(solution)/shard_map/gradient_piece/pallas_call | solution.py:448
  730.1 9.2 %gradient_piece.23 = f32[6,256,512]{2,1,0:T(8,128)} custom-call(s32[1]{0:T(128)} %bitcast.80.me, bf16[4,128,512]{2,1,0:T(8,128)(2,1)S(1)} %get-tuple-element.249.refs_0_.refs_1_.refs_6_.refs_7_.refs_18_.refs_19_, bf16[4,128,512]{2,1,0:T(8,128)(2,1)S(1)} %get-tuple-element.249.refs_0_.refs_1_.refs_6_.refs_7_.refs_18_.refs_19_, ...), custom_call_target="tpu_custom_call" | custom-call | flops 1610612736 | bytes 18874368 | tf_op jit(solution)/shard_map/gradient_piece/pallas_call | solution.py:448
  757.8 13.2 %spread_piece.4 = bf16[2,1000,512]{2,1,0:T(8,128)(2,1)S(1)} custom-call(s32[1,4096]{1,0:T(1,128)S(1)} %bitcast.236, bf16[4096,1024]{1,0:T(8,128)(2,1)} %all-gather.12.cloned.1.call-done.grads_ref, f32[4,1000,1024]{2,1,0:T(8,128)} %head_table_grads.1.table_ref), custom_call_target="tpu_custom_call" | custom-call | flops 8388608000 | bytes 12582912 | tf_op jit(solution)/shard_map/spread_piece/pallas_call | solution.py:790
  772.8 13.0 %spread_piece.5 = bf16[2,1000,512]{2,1,0:T(8,128)(2,1)S(1)} custom-call(s32[1,4096]{1,0:T(1,128)S(1)} %bitcast.237, bf16[4096,1024]{1,0:T(8,128)(2,1)} %all-gather.12.cloned.1.call-done.grads_ref, f32[4,1000,1024]{2,1,0:T(8,128)} %head_table_grads.1.table_ref), custom_call_target="tpu_custom_call" | custom-call | flops 8388608000 | bytes 12582912 | tf_op jit(solution)/shard_map/spread_piece/pallas_call | solution.py:790
  808.7 13.0 %spread_piece.6 = f32[2,1000,512]{2,1,0:T(8,128)S(1)} custom-call(s32[1,4096]{1,0:T(1,128)S(1)} %bitcast.238, bf16[4096,1024]{1,0:T(8,128)(2,1)} %all-gather.12.cloned.1.call-done.grads_ref, f32[4,1000,1024]{2,1,0:T(8,128)} %head_table_grads.1.table_ref), custom_call_target="tpu_custom_call" | custom-call | flops 8388608000 | bytes 12582912 | tf_op jit(solution)/shard_map/spread_piece/pallas_call | solution.py:790
  821.7 14.5 %spread_piece.7 = f32[2,1000,512]{2,1,0:T(8,128)S(1)} custom-call(s32[1,4096]{1,0:T(1,128)S(1)} %bitcast.239, bf16[4096,1024]{1,0:T(8,128)(2,1)} %all-gather.12.cloned.1.call-done.grads_ref, f32[4,1000,1024]{2,1,0:T(8,128)} %head_table_grads.1.table_ref), custom_call_target="tpu_custom_call" | custom-call | flops 8388608000 | bytes 12582912 | tf_op jit(solution)/shard_map/spread_piece/pallas_call | solution.py:790
  855.1 13.3 %collective-permute-done.78 = bf16[480,1024]{1,0:T(8,128)(2,1)} collective-permute-done((bf16[480,1024]{1,0:T(8,128)(2,1)}, bf16[480,1024]{1,0:T(8,128)(2,1)}, u32[]{:S(2)}, u32[]{:S(2)}) %collective-permute-start.78) | collective-permute-done | bytes 983072 | tf_op jit(solution)/shard_map/ppermute | solution.py:486
  (670 shorter events, 515.3 us)
Async XLA Ops:
  7.2 56.6 %all-gather.14.cloned.1.call-start = ((), (), s32[]{:S(2)}) async-start(), calls=%async_computation.8 | async-start | bytes 2457600 | tf_op jit(solution)/shard_map/all_gather | solution.py:571
  12.0 116.1 %all-gather.16.cloned.1.call-start = ((), (), s32[]{:S(2)}) async-start(), calls=%async_computation.9 | async-start | bytes 2621440 | tf_op jit(solution)/shard_map/all_gather | solution.py:571
  20.1 213.6 %reduce-scatter.4.cloned.1.call-start = ((), (), s32[]{:S(2)}) async-start(), calls=%async_computation.3 | async-start | bytes 9437184 | tf_op jit(solution)/shard_map/reduce_scatter | solution.py:906
  69.7 64.4 %collective-permute-start.4 = (bf16[4,240,1024]{2,1,0:T(8,128)(2,1)}, bf16[4,240,1024]{2,1,0:T(8,128)(2,1)}, u32[]{:S(2)}, u32[]{:S(2)}) collective-permute-start(bf16[4,240,1024]{2,1,0:T(8,128)(2,1)} %bitcast.2), channel_id=1, source_target_pairs={{0,2},{2,0},{1,3},{3,1},{4,6},{6,4},{5,7},{7,5},{8,10},{10,8},{9,1... | collective-permute-start | bytes 5898248 | tf_op jit(solution)/shard_map/ppermute | solution.py:210
  71.3 62.9 %collective-permute-start.5 = (bf16[4,240,1024]{2,1,0:T(8,128)(2,1)}, bf16[4,240,1024]{2,1,0:T(8,128)(2,1)}, u32[]{:S(2)}, u32[]{:S(2)}) collective-permute-start(bf16[4,240,1024]{2,1,0:T(8,128)(2,1)} %bitcast.2), channel_id=1, source_target_pairs={{0,4},{4,0},{1,5},{5,1},{2,6},{6,2},{3,7},{7,3},{8,12},{12,8},{9,1... | collective-permute-start | bytes 5898248 | tf_op jit(solution)/shard_map/ppermute | solution.py:210
  134.2 251.3 %all-gather.18.cloned.1.call-start = ((), (), s32[]{:S(2)}) async-start(), calls=%async_computation.10 | async-start | bytes 2654208 | tf_op jit(solution)/shard_map/all_gather | solution.py:1007
  153.2 58.7 %collective-permute-start.11 = (bf16[4,240,1024]{2,1,0:T(8,128)(2,1)}, bf16[4,240,1024]{2,1,0:T(8,128)(2,1)}, u32[]{:S(2)}, u32[]{:S(2)}) collective-permute-start(bf16[4,240,1024]{2,1,0:T(8,128)(2,1)} %collective-permute-done.4), channel_id=1, source_target_pairs={{0,1},{1,0},{2,3},{3,2},{4,5},{5,4},{6,7},{7,6},{8,9},{9,8},{10,11... | collective-permute-start | bytes 5898248 | tf_op jit(solution)/shard_map/ppermute | solution.py:210
  167.7 50.8 %collective-permute-start.12 = (bf16[4,240,1024]{2,1,0:T(8,128)(2,1)}, bf16[4,240,1024]{2,1,0:T(8,128)(2,1)}, u32[]{:S(2)}, u32[]{:S(2)}) collective-permute-start(bf16[4,240,1024]{2,1,0:T(8,128)(2,1)} %collective-permute-done.5), channel_id=1, source_target_pairs={{0,1},{1,0},{2,3},{3,2},{4,5},{5,4},{6,7},{7,6},{8,9},{9,8},{10,11... | collective-permute-start | bytes 5898248 | tf_op jit(solution)/shard_map/ppermute | solution.py:210
  181.0 51.3 %collective-permute-start.8 = (bf16[4,256,1024]{2,1,0:T(8,128)(2,1)}, bf16[4,256,1024]{2,1,0:T(8,128)(2,1)}, u32[]{:S(2)}, u32[]{:S(2)}) collective-permute-start(bf16[4,256,1024]{2,1,0:T(8,128)(2,1)} %bitcast.3), channel_id=1, source_target_pairs={{0,2},{2,0},{1,3},{3,1},{4,6},{6,4},{5,7},{7,5},{8,10},{10,8},{9,1... | collective-permute-start | bytes 6291464 | tf_op jit(solution)/shard_map/ppermute | solution.py:210
  182.2 50.1 %collective-permute-start.9 = (bf16[4,256,1024]{2,1,0:T(8,128)(2,1)}, bf16[4,256,1024]{2,1,0:T(8,128)(2,1)S(1)}, u32[]{:S(2)}, u32[]{:S(2)}) collective-permute-start(bf16[4,256,1024]{2,1,0:T(8,128)(2,1)} %bitcast.3), channel_id=1, source_target_pairs={{0,4},{4,0},{1,5},{5,1},{2,6},{6,2},{3,7},{7,3},{8,12},{12,8},{9,1... | collective-permute-start | bytes 6291464 | tf_op jit(solution)/shard_map/ppermute | solution.py:210
  183.1 57.8 %collective-permute-start.20 = (bf16[4,256,1024]{2,1,0:T(8,128)(2,1)}, bf16[4,256,1024]{2,1,0:T(8,128)(2,1)}, u32[]{:S(2)}, u32[]{:S(2)}) collective-permute-start(bf16[4,256,1024]{2,1,0:T(8,128)(2,1)} %bitcast.3), channel_id=1, source_target_pairs={{0,1},{1,0},{2,3},{3,2},{4,5},{5,4},{6,7},{7,6},{8,9},{9,8},{10,11... | collective-permute-start | bytes 6291464 | tf_op jit(solution)/shard_map/ppermute | solution.py:210
  246.3 70.2 %collective-permute-start.21 = (bf16[4,256,1024]{2,1,0:T(8,128)(2,1)}, bf16[4,256,1024]{2,1,0:T(8,128)(2,1)}, u32[]{:S(2)}, u32[]{:S(2)}) collective-permute-start(bf16[4,256,1024]{2,1,0:T(8,128)(2,1)} %collective-permute-done.8), channel_id=1, source_target_pairs={{0,1},{1,0},{2,3},{3,2},{4,5},{5,4},{6,7},{7,6},{8,9},{9,8},{10,11... | collective-permute-start | bytes 6291464 | tf_op jit(solution)/shard_map/ppermute | solution.py:210
  273.3 47.7 %collective-permute-start.22 = (bf16[4,256,1024]{2,1,0:T(8,128)(2,1)S(1)}, bf16[4,256,1024]{2,1,0:T(8,128)(2,1)}, u32[]{:S(2)}, u32[]{:S(2)}) collective-permute-start(bf16[4,256,1024]{2,1,0:T(8,128)(2,1)S(1)} %copy-done.54), channel_id=1, source_target_pairs={{0,1},{1,0},{2,3},{3,2},{4,5},{5,4},{6,7},{7,6},{8,9},{9,8},{10,11... | collective-permute-start | bytes 6291464 | tf_op jit(solution)/shard_map/ppermute | solution.py:210
  352.5 67.2 %all-gather.10.cloned.1.call-start = ((), (), s32[]{:S(2)}) async-start(), calls=%async_computation.4 | async-start | bytes 2359296 | tf_op jit(solution)/shard_map/all_gather | solution.py:1026
  388.7 117.3 %reduce-scatter.6.cloned.1.call-start = ((), (), s32[]{:S(2)}) async-start(), calls=%async_computation.5 | async-start | bytes 2359296 | tf_op jit(solution)/shard_map/reduce_scatter | solution.py:1051
  451.8 72.3 %reduce-scatter.8.cloned.1.call-start = ((), (), s32[]{:S(2)}) async-start(), calls=%async_computation.6 | async-start | bytes 2359296 | tf_op jit(solution)/shard_map/reduce_scatter | solution.py:1051
  479.1 278.7 %all-gather.12.cloned.1.call-start = ((), (), s32[]{:S(2)}) async-start(), calls=%async_computation.7 | async-start | bytes 9437184 | tf_op jit(solution)/shard_map/all_gather | solution.py:1132
  549.6 63.8 %collective-permute-start.49 = (bf16[1,512,4096]{2,1,0:T(8,128)(2,1)}, bf16[1,512,4096]{2,1,0:T(8,128)(2,1)}, u32[]{:S(2)}, u32[]{:S(2)}) collective-permute-start(bf16[1,512,4096]{2,1,0:T(8,128)(2,1)} %bitcast.225), channel_id=1, source_target_pairs={{0,1},{1,0},{2,3},{3,2},{4,5},{5,4},{6,7},{7,6},{8,9},{9,8},{10,11... | collective-permute-start | bytes 12582920 | tf_op jit(solution)/shard_map/ppermute | solution.py:210
  594.0 63.5 %collective-permute-start.55 = (bf16[2,1152,1024]{2,1,0:T(8,128)(2,1)}, bf16[2,1152,1024]{2,1,0:T(8,128)(2,1)}, u32[]{:S(2)}, u32[]{:S(2)}) collective-permute-start(bf16[2,1152,1024]{2,1,0:T(8,128)(2,1)} %get-tuple-element.257.grad_ref.refs_16_.refs_28_), channel_id=1, source_target_pairs={{0,1},{1,0},{2,3},{3,2},{4,5},{5,4},{6,7},{7,6},{8,9},{9,8},{10,11... | collective-permute-start | bytes 14155784 | tf_op jit(solution)/shard_map/ppermute | solution.py:210
  673.5 65.8 %collective-permute-start.61 = (bf16[5,256,512]{2,1,0:T(8,128)(2,1)}, bf16[5,256,512]{2,1,0:T(8,128)(2,1)}, u32[]{:S(2)}, u32[]{:S(2)}) collective-permute-start(bf16[5,256,512]{2,1,0:T(8,128)(2,1)} %copy-done.31), channel_id=1, source_target_pairs={{0,2},{2,0},{1,3},{3,1},{4,6},{6,4},{5,7},{7,5},{8,10},{10,8},{9,1... | collective-permute-start | bytes 3932168 | tf_op jit(solution)/shard_map/ppermute | solution.py:210
  676.3 65.0 %collective-permute-start.62 = (bf16[5,256,512]{2,1,0:T(8,128)(2,1)}, bf16[5,256,512]{2,1,0:T(8,128)(2,1)}, u32[]{:S(2)}, u32[]{:S(2)}) collective-permute-start(bf16[5,256,512]{2,1,0:T(8,128)(2,1)} %copy-done.30), channel_id=1, source_target_pairs={{0,4},{4,0},{1,5},{5,1},{2,6},{6,2},{3,7},{7,3},{8,12},{12,8},{9,1... | collective-permute-start | bytes 3932168 | tf_op jit(solution)/shard_map/ppermute | solution.py:210
  696.7 52.9 %collective-permute-start.63 = (bf16[6,256,512]{2,1,0:T(8,128)(2,1)S(1)}, bf16[6,256,512]{2,1,0:T(8,128)(2,1)}, u32[]{:S(2)}, u32[]{:S(2)}) collective-permute-start(bf16[6,256,512]{2,1,0:T(8,128)(2,1)S(1)} %gradient_piece.16), channel_id=1, source_target_pairs={{0,2},{2,0},{1,3},{3,1},{4,6},{6,4},{5,7},{7,5},{8,10},{10,8},{9,1... | collective-permute-start | bytes 4718600 | tf_op jit(solution)/shard_map/ppermute | solution.py:210
  697.0 55.6 %collective-permute-start.64 = (bf16[6,256,512]{2,1,0:T(8,128)(2,1)S(1)}, bf16[6,256,512]{2,1,0:T(8,128)(2,1)}, u32[]{:S(2)}, u32[]{:S(2)}) collective-permute-start(bf16[6,256,512]{2,1,0:T(8,128)(2,1)S(1)} %gradient_piece.17), channel_id=1, source_target_pairs={{0,4},{4,0},{1,5},{5,1},{2,6},{6,2},{3,7},{7,3},{8,12},{12,8},{9,1... | collective-permute-start | bytes 4718600 | tf_op jit(solution)/shard_map/ppermute | solution.py:210
  711.4 59.7 %collective-permute-start.59 = (bf16[4,128,512]{2,1,0:T(8,128)(2,1)}, bf16[4,128,512]{2,1,0:T(8,128)(2,1)}, u32[]{:S(2)}, u32[]{:S(2)}) collective-permute-start(bf16[4,128,512]{2,1,0:T(8,128)(2,1)} %get-tuple-element.268), channel_id=1, source_target_pairs={{0,4},{4,0},{1,5},{5,1},{2,6},{6,2},{3,7},{7,3},{8,12},{12,8},{9,1... | collective-permute-start | bytes 1572872 | tf_op jit(solution)/shard_map/ppermute | solution.py:210
  (170 other events, 1966.0 us)
Sparse Core Ops, SparseCore 0:
  12.1 46.3 all-gather.13
  60.6 44.7 all-gather.15
  134.3 89.0 reduce-scatter.3
  352.6 32.8 all-gather.17
  388.8 28.0 all-gather.9
  451.9 35.0 reduce-scatter.5
  489.9 34.1 reduce-scatter.7
  657.6 92.6 all-gather.11

commit v5 on v4

--- a/solution.py
+++ b/solution.py
@@ -29,6 +29,8 @@
 BLOCK = 128
 GROUPS = 32
 CHUNK = 256
+TOGETHER = 2
+STRIP = TOGETHER * HEAD
 BF16 = jnp.bfloat16
 F32 = jnp.float32
 
@@ -87,15 +89,17 @@
     def _():
         fill_bias(bias, *marks)
 
-    keys = jnp.concatenate([own_k[...], mem_k[...]], 0)
-    values = jnp.concatenate([own_v[...], mem_v[...]], 0)
-    scores = matmul_nt(keys, query[...]) * HEAD ** (-0.5) + bias[...]
-    top = jnp.max(scores, 0, keepdims=True)
-    probs = jnp.exp(scores - top)
-    total = jnp.sum(probs, 0, keepdims=True)
-    log_total[0] = top + jnp.log(total)
-    probs = (probs * (1.0 / total)).astype(BF16)
-    out[...] = matmul_tn(values, probs).T.astype(BF16)
+    for index in range(TOGETHER):
+        head = slice(index * HEAD, (index + 1) * HEAD)
+        keys = jnp.concatenate([own_k[:, head], mem_k[:, head]], 0)
+        values = jnp.concatenate([own_v[:, head], mem_v[:, head]], 0)
+        scores = matmul_nt(keys, query[:, head]) * HEAD ** (-0.5) + bias[...]
+        top = jnp.max(scores, 0, keepdims=True)
+        probs = jnp.exp(scores - top)
+        total = jnp.sum(probs, 0, keepdims=True)
+        log_total[index] = top + jnp.log(total)
+        probs = (probs * (1.0 / total)).astype(BF16)
+        out[:, head] = matmul_tn(values, probs).T.astype(BF16)
 
 
 def attention_backward_body(*refs):
@@ -107,26 +111,31 @@
     def _():
         fill_bias(bias, *marks)
 
-    keys = jnp.concatenate([own_k[...], mem_k[...]], 0)
-    values = jnp.concatenate([own_v[...], mem_v[...]], 0)
-    scores = matmul_nt(keys, query[...]) * HEAD ** (-0.5) + bias[...]
-    probs = jnp.exp(scores - log_total[0])
-    grad_probs = matmul_nt(values, grad_out[...])
-    inner = jnp.sum(probs * grad_probs, 0, keepdims=True)
-    grad_scores = (probs * (grad_probs - inner) * HEAD ** (-0.5)).astype(BF16)
-    grad_query[...] = matmul_tn(keys, grad_scores).T.astype(BF16)
-    pair = (matmul(grad_scores, query[...]), matmul(probs.astype(BF16), grad_out[...]))
-    at = 0
-    for part in (grad_own, grad_mem):
-        count = part.shape[1]
-        for side in (0, 1):
-            part[side] = pair[side][at : at + count].astype(part.dtype)
-        at += count
+    for index in range(TOGETHER):
+        head = slice(index * HEAD, (index + 1) * HEAD)
+        keys = jnp.concatenate([own_k[:, head], mem_k[:, head]], 0)
+        values = jnp.concatenate([own_v[:, head], mem_v[:, head]], 0)
+        scores = matmul_nt(keys, query[:, head]) * HEAD ** (-0.5) + bias[...]
+        probs = jnp.exp(scores - log_total[index])
+        grad_probs = matmul_nt(values, grad_out[:, head])
+        inner = jnp.sum(probs * grad_probs, 0, keepdims=True)
+        grad_scores = (probs * (grad_probs - inner) * HEAD ** (-0.5)).astype(BF16)
+        grad_query[:, head] = matmul_tn(keys, grad_scores).T.astype(BF16)
+        pair = (
+            matmul(grad_scores, query[:, head]),
+            matmul(probs.astype(BF16), grad_out[:, head]),
+        )
+        at = 0
+        for part in (grad_own, grad_mem):
+            count = part.shape[1]
+            for side in (0, 1):
+                part[side, :, head] = pair[side][at : at + count].astype(part.dtype)
+            at += count
 
 
 def attention_specs(segment, others):
     def column(rows, shift):
-        return pl.BlockSpec((rows, HEAD), lambda h: (0, h + shift * HEADS))
+        return pl.BlockSpec((rows, STRIP), lambda h: (0, h + shift * HEADS // TOGETHER))
 
     mark_k = pl.BlockSpec((segment + others, 1), lambda h: (0, 0))
     mark_q = pl.BlockSpec((1, segment), lambda h: (0, 0))
@@ -140,18 +149,18 @@
     keys = segment + others
     return pl.pallas_call(
         attention_forward_body,
-        grid=(HEADS,),
+        grid=(HEADS // TOGETHER,),
         in_specs=attention_specs(segment, others),
         out_specs=[
-            pl.BlockSpec((segment, HEAD), lambda h: (0, h)),
-            pl.BlockSpec((1, 1, segment), lambda h: (h, 0, 0)),
+            pl.BlockSpec((segment, STRIP), lambda h: (0, h)),
+            pl.BlockSpec((TOGETHER, 1, segment), lambda h: (h, 0, 0)),
         ],
         out_shape=[
             jax.ShapeDtypeStruct((segment, HEADS * HEAD), BF16),
             jax.ShapeDtypeStruct((HEADS, 1, segment), F32),
         ],
         scratch_shapes=[pltpu.VMEM((keys, segment), F32)],
-        compiler_params=pltpu.CompilerParams(vmem_limit_bytes=48 << 20),
+        compiler_params=pltpu.CompilerParams(vmem_limit_bytes=56 << 20),
         cost_estimate=pl.CostEstimate(
             flops=4 * HEADS * keys * segment * HEAD,
             bytes_accessed=12 << 20,
@@ -167,17 +176,17 @@
     width = HEADS * HEAD
 
     def pair_spec(rows):
-        return pl.BlockSpec((2, rows, HEAD), lambda h: (0, 0, h))
+        return pl.BlockSpec((2, rows, STRIP), lambda h: (0, 0, h))
 
     return pl.pallas_call(
         attention_backward_body,
-        grid=(HEADS,),
+        grid=(HEADS // TOGETHER,),
         in_specs=attention_specs(segment, others)
         + [
-            pl.BlockSpec((1, 1, segment), lambda h: (h, 0, 0)),
-            pl.BlockSpec((segment, HEAD), lambda h: (0, h)),
-        ],
-        out_specs=[pl.BlockSpec((segment, HEAD), lambda h: (0, h))]
+            pl.BlockSpec((TOGETHER, 1, segment), lambda h: (h, 0, 0)),
+            pl.BlockSpec((segment, STRIP), lambda h: (0, h)),
+        ],
+        out_specs=[pl.BlockSpec((segment, STRIP), lambda h: (0, h))]
         + [pair_spec(segment), pair_spec(others)],
         out_shape=[
             jax.ShapeDtypeStruct((segment, width), BF16),
@@ -185,7 +194,7 @@
             jax.ShapeDtypeStruct((2, others, width), BF16),
         ],
         scratch_shapes=[pltpu.VMEM((keys, segment), F32)],
-        compiler_params=pltpu.CompilerParams(vmem_limit_bytes=48 << 20),
+        compiler_params=pltpu.CompilerParams(vmem_limit_bytes=56 << 20),
         cost_estimate=pl.CostEstimate(
             flops=10 * HEADS * keys * segment * HEAD,
             bytes_accessed=24 << 20,
@@ -290,16 +299,20 @@
     lines = width // (8 * chunk)
 
     def body(value_ref, first_ref, second_ref, residual_ref, out, pre, turned):
-        hidden = matmul(value_ref[...], first_ref[...].reshape(width, width))
-        pre[...] = hidden
-        inner = jnp.tanh(GELU_SCALE * (hidden + GELU_CUBE * hidden * hidden * hidden))
-        active = (0.5 * hidden * (1.0 + inner)).astype(BF16)
-
         @pl.when(pl.program_id(0) == 0)
         def _():
             out[...] = residual_ref[...]
 
-        out[...] += matmul(active, second_ref[...].reshape(width, width))
+        parts = []
+        for at in range(0, size, CHUNK):
+            span = slice(at, at + CHUNK)
+            hidden = matmul(value_ref[span], first_ref[...].reshape(width, width))
+            pre[span] = hidden
+            inner = jnp.tanh(GELU_SCALE * (hidden + GELU_CUBE * hidden * hidden * hidden))
+            active = (0.5 * hidden * (1.0 + inner)).astype(BF16)
+            out[span] += matmul(active, second_ref[...].reshape(width, width))
+            parts.append(active)
+        active = jnp.concatenate(parts, 0)
         columns = active.T
         for line in range(lines):
             for place in range(8):
@@ -341,21 +354,22 @@
     blocks = pre.shape[1] // width
 
     def body(grad_ref, pre_ref, first_ref, second_ref, grad_pre, out):
-        grad_active = matmul_nt(grad_ref[...], second_ref[...].reshape(width, width))
-        hidden = pre_ref[...]
-        square = hidden * hidden
-        inner = jnp.tanh(GELU_SCALE * hidden * (1.0 + GELU_CUBE * square))
-        slope = 0.5 * (1.0 + inner) + 0.5 * hidden * (1.0 - inner * inner) * GELU_SCALE * (
-            1.0 + 3.0 * GELU_CUBE * square
-        )
-        back = (grad_active * slope).astype(BF16)
-        grad_pre[...] = back
-
         @pl.when(pl.program_id(0) == 0)
         def _():
             out[...] = jnp.zeros(out.shape, F32)
 
-        out[...] += matmul_nt(back, first_ref[...].reshape(width, width))
+        for at in range(0, size, CHUNK):
+            span = slice(at, at + CHUNK)
+            grad_active = matmul_nt(grad_ref[span], second_ref[...].reshape(width, width))
+            hidden = pre_ref[span]
+            square = hidden * hidden
+            inner = jnp.tanh(GELU_SCALE * hidden * (1.0 + GELU_CUBE * square))
+            slope = 0.5 * (1.0 + inner) + 0.5 * hidden * (1.0 - inner * inner) * GELU_SCALE * (
+                1.0 + 3.0 * GELU_CUBE * square
+            )
+            back = (grad_active * slope).astype(BF16)
+            grad_pre[span] = back
+            out[span] += matmul_nt(back, first_ref[...].reshape(width, width))
 
     return pl.pallas_call(
         body,
@@ -780,8 +794,12 @@
             total[...] = table_ref[0]
 
         wanted = token_ref[...] - row_of(pl.program_id(0)) * part_rows
-        hit = lax.broadcasted_iota(jnp.int32, (part_rows, tokens), 0) == wanted
-        total[...] += matmul(jnp.where(hit, 1.0, 0.0).astype(BF16), grads_ref[...])
+        for at in range(0, part_rows, CHUNK):
+            count = min(CHUNK, part_rows - at)
+            hit = lax.broadcasted_iota(jnp.int32, (count, tokens), 0) == wanted - at
+            total[at : at + count] += matmul(
+                jnp.where(hit, 1.0, 0.0).astype(BF16), grads_ref[...]
+            )
 
         @pl.when(step == pl.num_programs(1) - 1)
         def _():

time: 925 us -> 924 us (level)
    unnamed x225 -> x213, local copies, waits for them, and re-layouts: 27.9 us -> 25.1 us
  transfers between devices with their start and end apart: 90 -> 90, of which waited for: 25 -> 25; matrix products, arithmetic and copies ran while one was open for 28% -> 29% of each run, Pallas kernels for 31% -> 31%
where the time goes in v5:
time: 924 us; the launch traced here: 913 us
  Pallas kernels  331 us (36%)
  local copies, waits for them, and re-layouts  207 us (22%)
  waiting for transfers between devices  132 us (14%)
  starting transfers between devices  101 us (11%)
  other arithmetic  101 us (11%)
  between operations  19.1 us (2%)
  blocking collectives  13.2 us (1%)
    ppermute x54, waiting for transfers between devices, swapped(): return lax.ppermute(value, axis, [(0, 1), (1, 0)])  70.1 us
    pallas_call x12, Pallas kernels, gradient_piece(): pl.pallas_call(body, grid_spec=pltpu.PrefetchScalarGridSpec(num_scalar_pr...  68.5 us
    pallas_call x4, Pallas kernels, spread_piece(): pl.pallas_call(body, grid=(2, grads.shape[0] // tokens), in_specs=[pl.Blo...  53.8 us
    ppermute x54, starting transfers between devices, swapped(): return lax.ppermute(value, axis, [(0, 1), (1, 0)])  50.5 us
    dynamic_update_slice x20, local copies, waits for them, and re-layouts, plane_gather(): result = lax.dynamic_update_slice(result, part[:, None, None, None], start)  45.7 us
    pallas_call x2, Pallas kernels, head_logits(): pl.pallas_call(body, grid=(parts,), in_specs=[pl.BlockSpec((count, width)...  33.2 us
    pallas_call x2, Pallas kernels, head_row_grads(): pl.pallas_call(body, grid=(parts,), in_specs=[pl.BlockSpec((1, part_rows,...  30.9 us
    pallas_call x1, Pallas kernels, head_table_grads(): pl.pallas_call(body, grid=(parts,), in_specs=specs * len(groups), out_spe...  26.8 us
  transfers between devices with their start and end apart: 90, of which 25 were waited for; matrix products, arithmetic and copies ran while one was open for 29% of the time, Pallas kernels for 31%

profile of v5, /device:TPU:0, one launch (start us, length us, event | category | flops | bytes accessed | tf_op | source)
XLA Modules:
  0.0 913.3 jit_solution(15753666624480242365)
XLA Ops:
  20.2 13.2 %all-gather = s32[1,4096]{1,0:T(1,128)S(1)} all-gather(s32[1,512]{1,0:T(1,128)S(1)} %copy-done.90), channel_id=2, replica_groups=mesh['batch'=4,'far'=1,'y'=2,'x'=2,'core'=2] {'batch','core'}, dimensions={1}, use_global_device_ids=true | all-gather | bytes 18432 | tf_op jit(solution)/shard_map/all_gather | solution.py:859
  33.3 29.0 %collective-permute-done = bf16[1000,1024]{1,0:T(8,128)(2,1)} collective-permute-done((bf16[1000,1024]{1,0:T(8,128)(2,1)S(1)}, bf16[1000,1024]{1,0:T(8,128)(2,1)}, u32[]{:S(2)}, u32[]{:S(2)}) %collective-permute-start) | collective-permute-done | bytes 2048032 | tf_op jit(solution)/shard_map/ppermute | solution.py:219
  82.8 9.0 collective-permute-done.2
  95.7 25.3 %gather_fusion = bf16[4096,1024]{1,0:T(8,128)(2,1)} fusion(bf16[4000,1024]{1,0:T(8,128)(2,1)} %constant_dynamic-update-slice_fusion.12, s32[4096]{0:T(1024)S(1)} %maximum_clamp_fusion), kind=kCustom, calls=%fused_computation | custom fusion | bytes 16793600 | tf_op jit(solution)/shard_map/gather | solution.py:911
  183.3 11.4 %copy.173 = bf16[4,1000,1024]{1,2,0:T(8,128)(2,1)} copy(bf16[4,1000,1024]{2,1,0:T(8,128)(2,1)} %bitcast.4.table_ref) | data formatting | bytes 16384000 | tf_op jit(solution)/shard_map/reshape | solution.py:926
  292.6 17.2 %attention_forward.1 = (bf16[512,1024]{1,0:T(8,128)(2,1)}, f32[8,1,512]{2,1,0:T(1,128)}) custom-call(bf16[512,3072]{1,0:T(8,128)(2,1)} %copy-done.6, bf16[512,3072]{1,0:T(8,128)(2,1)} %copy-done.6, bf16[512,3072]{1,0:T(8,128)(2,1)} %copy-done.6, bf16[1152,2048]{1,0:T(8,128)(2,1)} %matmul_packed.5.refs_3_.refs_4_, ...), custom_call_target="tpu_custom_call" | custom-call | flops 3489660928 | bytes 12582912 | tf_op jit(solution)/shard_map/attention_forward/pallas_call | solution.py:150
  330.3 16.1 %feed_forward.1 = (f32[512,1024]{1,0:T(8,128)}, f32[512,4096]{1,0:T(8,128)}, bf16[8,512,512]{2,1,0:T(8,128)(2,1)}) custom-call(bf16[512,1024]{1,0:T(8,128)(2,1)} %multiply_convert_fusion.2.value_ref, bf16[32,256,1024]{2,1,0:T(8,128)(2,1)} %bitcast.49.first_ref.second_ref, bf16[32,256,1024]{2,1,0:T(8,128)(2,1)} %bitcast.49.first_ref.second_ref, ...), custom_call_target="tpu_custom_call" | custom-call | flops 8589934592 | bytes 33554432 | tf_op jit(solution)/shard_map/feed_forward/pallas_call | solution.py:323
  390.7 16.6 %head_logits.2 = (f32[4,1000,1024]{2,1,0:T(8,128)}, f32[1,1024]{1,0:T(1,128)}, f32[1,1024]{1,0:T(1,128)}, f32[1,1024]{1,0:T(1,128)}) custom-call(bf16[1024,1024]{1,0:T(8,128)(2,1)} %bitcast.269, bf16[4,1000,1024]{2,1,0:T(8,128)(2,1)} %bitcast.4.table_ref, s32[1,1024]{1,0:T(1,128)} %get-tuple-element.517.wanted_ref.refs_3_), custom_call_target="tpu_custom_call" | custom-call | flops 8388608000 | bytes 24576000 | tf_op jit(solution)/shard_map/head_logits/pallas_call | solution.py:658
  419.7 16.6 %head_logits.3 = (f32[4,1000,1024]{2,1,0:T(8,128)}, f32[1,1024]{1,0:T(1,128)}, f32[1,1024]{1,0:T(1,128)}, f32[1,1024]{1,0:T(1,128)}) custom-call(bf16[1024,1024]{1,0:T(8,128)(2,1)} %all-gather.10.cloned.1.call-done.rows_ref.refs_9_, bf16[4,1000,1024]{2,1,0:T(8,128)(2,1)} %bitcast.4.table_ref, s32[1,1024]{1,0:T(1,128)} %get-tuple-element.518.wanted_ref.refs_8_), custom_call_target="tpu_custom_call" | custom-call | flops 8388608000 | bytes 24576000 | tf_op jit(solution)/shard_map/head_logits/pallas_call | solution.py:658
  436.3 15.4 %head_row_grads.2 = bf16[1024,1024]{1,0:T(8,128)(2,1)} custom-call(f32[4,1000,1024]{2,1,0:T(8,128)} %get-tuple-element.214.logits_ref.refs_0_, f32[1,1024]{1,0:T(1,128)} %log_add_fusion.1.log_norm_ref.refs_1_, f32[1,1024]{1,0:T(1,128)} %bitcast.296, s32[1,1024]{1,0:T(1,128)} %get-tuple-element.517.wanted_ref.refs_3_, ...), custom_call_target="tpu_custom_call" | custom-call | flops 8388608000 | bytes 24576000 | tf_op jit(solution)/shard_map/head_row_grads/pallas_call | solution.py:713
  463.6 15.5 %head_row_grads.3 = bf16[1024,1024]{1,0:T(8,128)(2,1)} custom-call(f32[4,1000,1024]{2,1,0:T(8,128)} %get-tuple-element.222.logits_ref.refs_5_, f32[1,1024]{1,0:T(1,128)} %get-tuple-element.438.log_norm_ref.refs_6_, f32[1,1024]{1,0:T(1,128)} %bitcast.300, s32[1,1024]{1,0:T(1,128)} %get-tuple-element.518.wanted_ref.refs_8_, ...), custom_call_target="tpu_custom_call" | custom-call | flops 8388608000 | bytes 24576000 | tf_op jit(solution)/shard_map/head_row_grads/pallas_call | solution.py:713
  479.2 26.8 %head_table_grads.1.table_ref = f32[4,1000,1024]{2,1,0:T(8,128)} custom-call(f32[4,1000,1024]{2,1,0:T(8,128)} %get-tuple-element.214.logits_ref.refs_0_, f32[1,1024]{1,0:T(1,128)} %log_add_fusion.1.log_norm_ref.refs_1_, f32[1,1024]{1,0:T(1,128)} %bitcast.297, s32[1,1024]{1,0:T(1,128)} %get-tuple-element.517.wanted_ref.refs_3_, bf16[1024,1024]{1,0:T(8,128)(2,1)} %bitcast.270, ...), custom_call_target="tpu_custom_call" | custom-call | flops 16777216000 | bytes 49152000 | tf_op jit(solution)/shard_map/head_table_grads/pallas_call | solution.py:765
  506.0 18.3 %reduce-scatter.8.cloned.1.call-done = bf16[128,1024]{1,0:T(8,128)(2,1)} async-done(((bf16[1024,1024]{1,0:T(8,128)(2,1)}), bf16[128,1024]{1,0:T(8,128)(2,1)}) %reduce-scatter.8.cloned.1.call-update) | async-done | bytes 262160 | tf_op jit(solution)/shard_map/reduce_scatter | solution.py:1069
  531.1 16.9 %feed_forward_back.1 = (bf16[512,4096]{1,0:T(8,128)(2,1)}, f32[512,1024]{1,0:T(8,128)}) custom-call(bf16[512,1024]{1,0:T(8,128)(2,1)} %copy-done.11, f32[512,4096]{1,0:T(8,128)} %get-tuple-element.228.pre_ref, bf16[32,256,1024]{2,1,0:T(8,128)(2,1)} %bitcast.49.first_ref.second_ref, bf16[32,256,1024]{2,1,0:T(8,128)(2,1)} %bitcast.49.first_ref.second_ref), custom_call_target="tpu_custom_call" | custom-call | flops 8589934592 | bytes 33554432 | tf_op jit(solution)/shard_map/feed_forward_back/pallas_call | solution.py:374
  567.3 26.3 %attention_backward.1 = (bf16[512,1024]{1,0:T(8,128)(2,1)}, bf16[2,512,1024]{2,1,0:T(8,128)(2,1)}, bf16[2,1152,1024]{2,1,0:T(8,128)(2,1)}) custom-call(bf16[512,3072]{1,0:T(8,128)(2,1)} %copy-done.6, bf16[512,3072]{1,0:T(8,128)(2,1)} %copy-done.6, bf16[512,3072]{1,0:T(8,128)(2,1)} %copy-done.6, bf16[1152,2048]{1,0:T(8,128)(2,1)} %matmul_packed.5.refs_3_.refs_4_, ...), custom_call_target="tpu_custom_call" | custom-call | flops 8724152320 | bytes 25165824 | tf_op jit(solution)/shard_map/attention_backward/pallas_call | solution.py:181
  660.0 10.9 %collective-permute-start.56 = (bf16[1,256,1024]{2,1,0:T(8,128)(2,1)}, bf16[1,256,1024]{2,1,0:T(8,128)(2,1)}, u32[]{:S(2)}, u32[]{:S(2)}) collective-permute-start(bf16[1,256,1024]{2,1,0:T(8,128)(2,1)} %pad_bitcast_fusion.1.refs_34_), channel_id=1, source_target_pairs={{0,1},{1,0},{2,3},{3,2},{4,5},{5,4},{6,7},{7,6},{8,9},{9,8},{10,11... | collective-permute-start | bytes 1572872 | tf_op jit(solution)/shard_map/ppermute | solution.py:219
  680.5 8.4 gradient_piece.16
  721.4 9.2 %gradient_piece.22 = f32[6,256,512]{2,1,0:T(8,128)} custom-call(s32[1]{0:T(128)} %bitcast.80.me, bf16[4,128,512]{2,1,0:T(8,128)(2,1)S(1)} %get-tuple-element.249.refs_0_.refs_1_.refs_6_.refs_7_.refs_18_.refs_19_, bf16[4,128,512]{2,1,0:T(8,128)(2,1)S(1)} %get-tuple-element.249.refs_0_.refs_1_.refs_6_.refs_7_.refs_18_.refs_19_, ...), custom_call_target="tpu_custom_call" | custom-call | flops 1610612736 | bytes 18874368 | tf_op jit(solution)/shard_map/gradient_piece/pallas_call | solution.py:462
  730.6 9.2 %gradient_piece.23 = f32[6,256,512]{2,1,0:T(8,128)} custom-call(s32[1]{0:T(128)} %bitcast.80.me, bf16[4,128,512]{2,1,0:T(8,128)(2,1)S(1)} %get-tuple-element.249.refs_0_.refs_1_.refs_6_.refs_7_.refs_18_.refs_19_, bf16[4,128,512]{2,1,0:T(8,128)(2,1)S(1)} %get-tuple-element.249.refs_0_.refs_1_.refs_6_.refs_7_.refs_18_.refs_19_, ...), custom_call_target="tpu_custom_call" | custom-call | flops 1610612736 | bytes 18874368 | tf_op jit(solution)/shard_map/gradient_piece/pallas_call | solution.py:462
  758.2 13.2 %spread_piece.4 = bf16[2,1000,512]{2,1,0:T(8,128)(2,1)S(1)} custom-call(s32[1,4096]{1,0:T(1,128)S(1)} %bitcast.236, bf16[4096,1024]{1,0:T(8,128)(2,1)} %all-gather.12.cloned.1.call-done.grads_ref, f32[4,1000,1024]{2,1,0:T(8,128)} %head_table_grads.1.table_ref), custom_call_target="tpu_custom_call" | custom-call | flops 8388608000 | bytes 12582912 | tf_op jit(solution)/shard_map/spread_piece/pallas_call | solution.py:808
  773.5 13.0 %spread_piece.5 = bf16[2,1000,512]{2,1,0:T(8,128)(2,1)S(1)} custom-call(s32[1,4096]{1,0:T(1,128)S(1)} %bitcast.237, bf16[4096,1024]{1,0:T(8,128)(2,1)} %all-gather.12.cloned.1.call-done.grads_ref, f32[4,1000,1024]{2,1,0:T(8,128)} %head_table_grads.1.table_ref), custom_call_target="tpu_custom_call" | custom-call | flops 8388608000 | bytes 12582912 | tf_op jit(solution)/shard_map/spread_piece/pallas_call | solution.py:808
  807.9 13.0 %spread_piece.6 = f32[2,1000,512]{2,1,0:T(8,128)S(1)} custom-call(s32[1,4096]{1,0:T(1,128)S(1)} %bitcast.238, bf16[4096,1024]{1,0:T(8,128)(2,1)} %all-gather.12.cloned.1.call-done.grads_ref, f32[4,1000,1024]{2,1,0:T(8,128)} %head_table_grads.1.table_ref), custom_call_target="tpu_custom_call" | custom-call | flops 8388608000 | bytes 12582912 | tf_op jit(solution)/shard_map/spread_piece/pallas_call | solution.py:808
  821.0 14.5 %spread_piece.7 = f32[2,1000,512]{2,1,0:T(8,128)S(1)} custom-call(s32[1,4096]{1,0:T(1,128)S(1)} %bitcast.239, bf16[4096,1024]{1,0:T(8,128)(2,1)} %all-gather.12.cloned.1.call-done.grads_ref, f32[4,1000,1024]{2,1,0:T(8,128)} %head_table_grads.1.table_ref), custom_call_target="tpu_custom_call" | custom-call | flops 8388608000 | bytes 12582912 | tf_op jit(solution)/shard_map/spread_piece/pallas_call | solution.py:808
  855.4 12.0 %collective-permute-done.78 = bf16[480,1024]{1,0:T(8,128)(2,1)} collective-permute-done((bf16[480,1024]{1,0:T(8,128)(2,1)}, bf16[480,1024]{1,0:T(8,128)(2,1)}, u32[]{:S(2)}, u32[]{:S(2)}) %collective-permute-start.78) | collective-permute-done | bytes 983072 | tf_op jit(solution)/shard_map/ppermute | solution.py:500
  (658 shorter events, 517.1 us)
Async XLA Ops:
  7.2 56.6 %all-gather.14.cloned.1.call-start = ((), (), s32[]{:S(2)}) async-start(), calls=%async_computation.8 | async-start | bytes 2457600 | tf_op jit(solution)/shard_map/all_gather | solution.py:585
  12.0 116.2 %all-gather.16.cloned.1.call-start = ((), (), s32[]{:S(2)}) async-start(), calls=%async_computation.9 | async-start | bytes 2621440 | tf_op jit(solution)/shard_map/all_gather | solution.py:585
  20.1 212.1 %reduce-scatter.4.cloned.1.call-start = ((), (), s32[]{:S(2)}) async-start(), calls=%async_computation.3 | async-start | bytes 9437184 | tf_op jit(solution)/shard_map/reduce_scatter | solution.py:924
  69.7 64.4 %collective-permute-start.4 = (bf16[4,240,1024]{2,1,0:T(8,128)(2,1)}, bf16[4,240,1024]{2,1,0:T(8,128)(2,1)}, u32[]{:S(2)}, u32[]{:S(2)}) collective-permute-start(bf16[4,240,1024]{2,1,0:T(8,128)(2,1)} %bitcast.2), channel_id=1, source_target_pairs={{0,2},{2,0},{1,3},{3,1},{4,6},{6,4},{5,7},{7,5},{8,10},{10,8},{9,1... | collective-permute-start | bytes 5898248 | tf_op jit(solution)/shard_map/ppermute | solution.py:219
  71.3 62.9 %collective-permute-start.5 = (bf16[4,240,1024]{2,1,0:T(8,128)(2,1)}, bf16[4,240,1024]{2,1,0:T(8,128)(2,1)}, u32[]{:S(2)}, u32[]{:S(2)}) collective-permute-start(bf16[4,240,1024]{2,1,0:T(8,128)(2,1)} %bitcast.2), channel_id=1, source_target_pairs={{0,4},{4,0},{1,5},{5,1},{2,6},{6,2},{3,7},{7,3},{8,12},{12,8},{9,1... | collective-permute-start | bytes 5898248 | tf_op jit(solution)/shard_map/ppermute | solution.py:219
  134.2 251.4 %all-gather.18.cloned.1.call-start = ((), (), s32[]{:S(2)}) async-start(), calls=%async_computation.10 | async-start | bytes 2654208 | tf_op jit(solution)/shard_map/all_gather | solution.py:1025
  154.3 56.3 %collective-permute-start.11 = (bf16[4,240,1024]{2,1,0:T(8,128)(2,1)}, bf16[4,240,1024]{2,1,0:T(8,128)(2,1)}, u32[]{:S(2)}, u32[]{:S(2)}) collective-permute-start(bf16[4,240,1024]{2,1,0:T(8,128)(2,1)} %collective-permute-done.4), channel_id=1, source_target_pairs={{0,1},{1,0},{2,3},{3,2},{4,5},{5,4},{6,7},{7,6},{8,9},{9,8},{10,11... | collective-permute-start | bytes 5898248 | tf_op jit(solution)/shard_map/ppermute | solution.py:219
  168.7 48.4 %collective-permute-start.12 = (bf16[4,240,1024]{2,1,0:T(8,128)(2,1)}, bf16[4,240,1024]{2,1,0:T(8,128)(2,1)}, u32[]{:S(2)}, u32[]{:S(2)}) collective-permute-start(bf16[4,240,1024]{2,1,0:T(8,128)(2,1)} %collective-permute-done.5), channel_id=1, source_target_pairs={{0,1},{1,0},{2,3},{3,2},{4,5},{5,4},{6,7},{7,6},{8,9},{9,8},{10,11... | collective-permute-start | bytes 5898248 | tf_op jit(solution)/shard_map/ppermute | solution.py:219
  181.2 51.1 %collective-permute-start.8 = (bf16[4,256,1024]{2,1,0:T(8,128)(2,1)S(1)}, bf16[4,256,1024]{2,1,0:T(8,128)(2,1)}, u32[]{:S(2)}, u32[]{:S(2)}) collective-permute-start(bf16[4,256,1024]{2,1,0:T(8,128)(2,1)S(1)} %bitcast.263), channel_id=1, source_target_pairs={{0,2},{2,0},{1,3},{3,1},{4,6},{6,4},{5,7},{7,5},{8,10},{10,8},{9,1... | collective-permute-start | bytes 6291464 | tf_op jit(solution)/shard_map/ppermute | solution.py:219
  182.3 49.9 %collective-permute-start.9 = (bf16[4,256,1024]{2,1,0:T(8,128)(2,1)S(1)}, bf16[4,256,1024]{2,1,0:T(8,128)(2,1)}, u32[]{:S(2)}, u32[]{:S(2)}) collective-permute-start(bf16[4,256,1024]{2,1,0:T(8,128)(2,1)S(1)} %bitcast.264), channel_id=1, source_target_pairs={{0,4},{4,0},{1,5},{5,1},{2,6},{6,2},{3,7},{7,3},{8,12},{12,8},{9,1... | collective-permute-start | bytes 6291464 | tf_op jit(solution)/shard_map/ppermute | solution.py:219
  183.3 56.1 %collective-permute-start.20 = (bf16[4,256,1024]{2,1,0:T(8,128)(2,1)S(1)}, bf16[4,256,1024]{2,1,0:T(8,128)(2,1)}, u32[]{:S(2)}, u32[]{:S(2)}) collective-permute-start(bf16[4,256,1024]{2,1,0:T(8,128)(2,1)S(1)} %bitcast.265), channel_id=1, source_target_pairs={{0,1},{1,0},{2,3},{3,2},{4,5},{5,4},{6,7},{7,6},{8,9},{9,8},{10,11... | collective-permute-start | bytes 6291464 | tf_op jit(solution)/shard_map/ppermute | solution.py:219
  244.5 71.0 %collective-permute-start.21 = (bf16[4,256,1024]{2,1,0:T(8,128)(2,1)}, bf16[4,256,1024]{2,1,0:T(8,128)(2,1)}, u32[]{:S(2)}, u32[]{:S(2)}) collective-permute-start(bf16[4,256,1024]{2,1,0:T(8,128)(2,1)} %collective-permute-done.8), channel_id=1, source_target_pairs={{0,1},{1,0},{2,3},{3,2},{4,5},{5,4},{6,7},{7,6},{8,9},{9,8},{10,11... | collective-permute-start | bytes 6291464 | tf_op jit(solution)/shard_map/ppermute | solution.py:219
  270.9 50.7 %collective-permute-start.22 = (bf16[4,256,1024]{2,1,0:T(8,128)(2,1)}, bf16[4,256,1024]{2,1,0:T(8,128)(2,1)}, u32[]{:S(2)}, u32[]{:S(2)}) collective-permute-start(bf16[4,256,1024]{2,1,0:T(8,128)(2,1)} %collective-permute-done.9), channel_id=1, source_target_pairs={{0,1},{1,0},{2,3},{3,2},{4,5},{5,4},{6,7},{7,6},{8,9},{9,8},{10,11... | collective-permute-start | bytes 6291464 | tf_op jit(solution)/shard_map/ppermute | solution.py:219
  352.5 67.2 %all-gather.10.cloned.1.call-start = ((), (), s32[]{:S(2)}) async-start(), calls=%async_computation.4 | async-start | bytes 2359296 | tf_op jit(solution)/shard_map/all_gather | solution.py:1044
  388.7 117.3 %reduce-scatter.6.cloned.1.call-start = ((), (), s32[]{:S(2)}) async-start(), calls=%async_computation.5 | async-start | bytes 2359296 | tf_op jit(solution)/shard_map/reduce_scatter | solution.py:1069
  451.8 72.5 %reduce-scatter.8.cloned.1.call-start = ((), (), s32[]{:S(2)}) async-start(), calls=%async_computation.6 | async-start | bytes 2359296 | tf_op jit(solution)/shard_map/reduce_scatter | solution.py:1069
  479.2 279.0 %all-gather.12.cloned.1.call-start = ((), (), s32[]{:S(2)}) async-start(), calls=%async_computation.7 | async-start | bytes 9437184 | tf_op jit(solution)/shard_map/all_gather | solution.py:1150
  548.0 66.1 %collective-permute-start.49 = (bf16[1,512,4096]{2,1,0:T(8,128)(2,1)}, bf16[1,512,4096]{2,1,0:T(8,128)(2,1)}, u32[]{:S(2)}, u32[]{:S(2)}) collective-permute-start(bf16[1,512,4096]{2,1,0:T(8,128)(2,1)} %bitcast.225), channel_id=1, source_target_pairs={{0,1},{1,0},{2,3},{3,2},{4,5},{5,4},{6,7},{7,6},{8,9},{9,8},{10,11... | collective-permute-start | bytes 12582920 | tf_op jit(solution)/shard_map/ppermute | solution.py:219
  594.6 63.5 %collective-permute-start.55 = (bf16[2,1152,1024]{2,1,0:T(8,128)(2,1)}, bf16[2,1152,1024]{2,1,0:T(8,128)(2,1)}, u32[]{:S(2)}, u32[]{:S(2)}) collective-permute-start(bf16[2,1152,1024]{2,1,0:T(8,128)(2,1)} %get-tuple-element.257.grad_ref.refs_16_.refs_28_), channel_id=1, source_target_pairs={{0,1},{1,0},{2,3},{3,2},{4,5},{5,4},{6,7},{7,6},{8,9},{9,8},{10,11... | collective-permute-start | bytes 14155784 | tf_op jit(solution)/shard_map/ppermute | solution.py:219
  674.1 65.7 %collective-permute-start.61 = (bf16[5,256,512]{2,1,0:T(8,128)(2,1)}, bf16[5,256,512]{2,1,0:T(8,128)(2,1)}, u32[]{:S(2)}, u32[]{:S(2)}) collective-permute-start(bf16[5,256,512]{2,1,0:T(8,128)(2,1)} %copy-done.27), channel_id=1, source_target_pairs={{0,2},{2,0},{1,3},{3,1},{4,6},{6,4},{5,7},{7,5},{8,10},{10,8},{9,1... | collective-permute-start | bytes 3932168 | tf_op jit(solution)/shard_map/ppermute | solution.py:219
  676.9 65.0 %collective-permute-start.62 = (bf16[5,256,512]{2,1,0:T(8,128)(2,1)}, bf16[5,256,512]{2,1,0:T(8,128)(2,1)}, u32[]{:S(2)}, u32[]{:S(2)}) collective-permute-start(bf16[5,256,512]{2,1,0:T(8,128)(2,1)} %copy-done.26), channel_id=1, source_target_pairs={{0,4},{4,0},{1,5},{5,1},{2,6},{6,2},{3,7},{7,3},{8,12},{12,8},{9,1... | collective-permute-start | bytes 3932168 | tf_op jit(solution)/shard_map/ppermute | solution.py:219
  697.3 52.9 %collective-permute-start.63 = (bf16[6,256,512]{2,1,0:T(8,128)(2,1)S(1)}, bf16[6,256,512]{2,1,0:T(8,128)(2,1)}, u32[]{:S(2)}, u32[]{:S(2)}) collective-permute-start(bf16[6,256,512]{2,1,0:T(8,128)(2,1)S(1)} %gradient_piece.16), channel_id=1, source_target_pairs={{0,2},{2,0},{1,3},{3,1},{4,6},{6,4},{5,7},{7,5},{8,10},{10,8},{9,1... | collective-permute-start | bytes 4718600 | tf_op jit(solution)/shard_map/ppermute | solution.py:219
  697.6 55.7 %collective-permute-start.64 = (bf16[6,256,512]{2,1,0:T(8,128)(2,1)S(1)}, bf16[6,256,512]{2,1,0:T(8,128)(2,1)}, u32[]{:S(2)}, u32[]{:S(2)}) collective-permute-start(bf16[6,256,512]{2,1,0:T(8,128)(2,1)S(1)} %gradient_piece.17), channel_id=1, source_target_pairs={{0,4},{4,0},{1,5},{5,1},{2,6},{6,2},{3,7},{7,3},{8,12},{12,8},{9,1... | collective-permute-start | bytes 4718600 | tf_op jit(solution)/shard_map/ppermute | solution.py:219
  710.7 60.8 %collective-permute-start.59 = (bf16[4,128,512]{2,1,0:T(8,128)(2,1)}, bf16[4,128,512]{2,1,0:T(8,128)(2,1)}, u32[]{:S(2)}, u32[]{:S(2)}) collective-permute-start(bf16[4,128,512]{2,1,0:T(8,128)(2,1)} %get-tuple-element.268), channel_id=1, source_target_pairs={{0,4},{4,0},{1,5},{5,1},{2,6},{6,2},{3,7},{7,3},{8,12},{12,8},{9,1... | collective-permute-start | bytes 1572872 | tf_op jit(solution)/shard_map/ppermute | solution.py:219
  (164 other events, 1915.7 us)
Sparse Core Ops, SparseCore 0:
  12.1 46.3 all-gather.13
  60.6 44.7 all-gather.15
  134.3 89.0 reduce-scatter.3
  352.7 32.8 all-gather.17
  388.8 28.0 all-gather.9
  451.9 34.9 reduce-scatter.5
  489.8 34.4 reduce-scatter.7
  658.3 92.6 all-gather.11

commit v6 on v5

--- a/solution.py
+++ b/solution.py
@@ -1109,12 +1109,13 @@
     )
     grad_other, out_arrived = lax.optimization_barrier((grad_other, out_arrived))
     grad_other_rows = matmul_packed_back(grad_other, mixer_all, thin, 1).astype(BF16)
+    grad_other_rows, grad_query = lax.optimization_barrier((grad_other_rows, grad_query))
     back_memory = passed_along(grad_other_rows[:segment], -1)
     returned = []
     for hop in (2, 3, 4):
         first_row = segment + (hop - 2) * slots
         returned.append(passed_along(grad_other_rows[first_row : first_row + slots], -hop))
-    place, grad_query = lax.optimization_barrier((chip_place(), grad_query))
+    place = chip_place()
     ffn_sends = gradient_sends(ffn_weights, place)
     grad_input = matmul_packed_back(grad_query[None], mixer_all, thin, 0)
     grad_input = matmul_packed_back(grad_own, mixer_all, thin, 1, grad_input)

time: 924 us -> 919 us (level)
  transfers between devices with their start and end apart: 90 -> 90, of which waited for: 25 -> 24; matrix products, arithmetic and copies ran while one was open for 29% -> 29% of each run, Pallas kernels for 31% -> 31%
where the time goes in v6:
time: 919 us; the launch traced here: 909 us
  Pallas kernels  331 us (36%)
  local copies, waits for them, and re-layouts  207 us (23%)
  waiting for transfers between devices  127 us (14%)
  starting transfers between devices  102 us (11%)
  other arithmetic  101 us (11%)
  between operations  19.1 us (2%)
  blocking collectives  13.2 us (1%)
    ppermute x54, waiting for transfers between devices, swapped(): return lax.ppermute(value, axis, [(0, 1), (1, 0)])  70.1 us
    pallas_call x12, Pallas kernels, gradient_piece(): pl.pallas_call(body, grid_spec=pltpu.PrefetchScalarGridSpec(num_scalar_pr...  68.5 us
    pallas_call x4, Pallas kernels, spread_piece(): pl.pallas_call(body, grid=(2, grads.shape[0] // tokens), in_specs=[pl.Blo...  53.8 us
    ppermute x54, starting transfers between devices, swapped(): return lax.ppermute(value, axis, [(0, 1), (1, 0)])  50.5 us
    dynamic_update_slice x20, local copies, waits for them, and re-layouts, plane_gather(): result = lax.dynamic_update_slice(result, part[:, None, None, None], start)  45.7 us
    pallas_call x2, Pallas kernels, head_logits(): pl.pallas_call(body, grid=(parts,), in_specs=[pl.BlockSpec((count, width)...  33.2 us
    pallas_call x2, Pallas kernels, head_row_grads(): pl.pallas_call(body, grid=(parts,), in_specs=[pl.BlockSpec((1, part_rows,...  30.9 us
    pallas_call x1, Pallas kernels, head_table_grads(): pl.pallas_call(body, grid=(parts,), in_specs=specs * len(groups), out_spe...  26.8 us
  transfers between devices with their start and end apart: 90, of which 24 were waited for; matrix products, arithmetic and copies ran while one was open for 29% of the time, Pallas kernels for 31%

profile of v6, /device:TPU:0, one launch (start us, length us, event | category | flops | bytes accessed | tf_op | source)
XLA Modules:
  0.0 908.5 jit_solution(5578759316790619818)
XLA Ops:
  20.2 13.2 %all-gather = s32[1,4096]{1,0:T(1,128)S(1)} all-gather(s32[1,512]{1,0:T(1,128)S(1)} %copy-done.90), channel_id=2, replica_groups=mesh['batch'=4,'far'=1,'y'=2,'x'=2,'core'=2] {'batch','core'}, dimensions={1}, use_global_device_ids=true | all-gather | bytes 18432 | tf_op jit(solution)/shard_map/all_gather | solution.py:859
  33.3 29.0 %collective-permute-done = bf16[1000,1024]{1,0:T(8,128)(2,1)} collective-permute-done((bf16[1000,1024]{1,0:T(8,128)(2,1)S(1)}, bf16[1000,1024]{1,0:T(8,128)(2,1)}, u32[]{:S(2)}, u32[]{:S(2)}) %collective-permute-start) | collective-permute-done | bytes 2048032 | tf_op jit(solution)/shard_map/ppermute | solution.py:219
  82.8 9.0 collective-permute-done.2
  95.7 25.3 %gather_fusion = bf16[4096,1024]{1,0:T(8,128)(2,1)} fusion(bf16[4000,1024]{1,0:T(8,128)(2,1)} %constant_dynamic-update-slice_fusion.12, s32[4096]{0:T(1024)S(1)} %maximum_clamp_fusion), kind=kCustom, calls=%fused_computation | custom fusion | bytes 16793600 | tf_op jit(solution)/shard_map/gather | solution.py:911
  183.3 11.4 %copy.173 = bf16[4,1000,1024]{1,2,0:T(8,128)(2,1)} copy(bf16[4,1000,1024]{2,1,0:T(8,128)(2,1)} %bitcast.4.table_ref) | data formatting | bytes 16384000 | tf_op jit(solution)/shard_map/reshape | solution.py:926
  292.6 17.2 %attention_forward.1 = (bf16[512,1024]{1,0:T(8,128)(2,1)}, f32[8,1,512]{2,1,0:T(1,128)}) custom-call(bf16[512,3072]{1,0:T(8,128)(2,1)} %copy-done.6, bf16[512,3072]{1,0:T(8,128)(2,1)} %copy-done.6, bf16[512,3072]{1,0:T(8,128)(2,1)} %copy-done.6, bf16[1152,2048]{1,0:T(8,128)(2,1)} %matmul_packed.5.refs_3_.refs_4_, ...), custom_call_target="tpu_custom_call" | custom-call | flops 3489660928 | bytes 12582912 | tf_op jit(solution)/shard_map/attention_forward/pallas_call | solution.py:150
  330.3 16.1 %feed_forward.1 = (f32[512,1024]{1,0:T(8,128)}, f32[512,4096]{1,0:T(8,128)}, bf16[8,512,512]{2,1,0:T(8,128)(2,1)}) custom-call(bf16[512,1024]{1,0:T(8,128)(2,1)} %multiply_convert_fusion.2.value_ref, bf16[32,256,1024]{2,1,0:T(8,128)(2,1)} %bitcast.49.first_ref.second_ref, bf16[32,256,1024]{2,1,0:T(8,128)(2,1)} %bitcast.49.first_ref.second_ref, ...), custom_call_target="tpu_custom_call" | custom-call | flops 8589934592 | bytes 33554432 | tf_op jit(solution)/shard_map/feed_forward/pallas_call | solution.py:323
  390.7 16.6 %head_logits.2 = (f32[4,1000,1024]{2,1,0:T(8,128)}, f32[1,1024]{1,0:T(1,128)}, f32[1,1024]{1,0:T(1,128)}, f32[1,1024]{1,0:T(1,128)}) custom-call(bf16[1024,1024]{1,0:T(8,128)(2,1)} %bitcast.269, bf16[4,1000,1024]{2,1,0:T(8,128)(2,1)} %bitcast.4.table_ref, s32[1,1024]{1,0:T(1,128)} %get-tuple-element.517.wanted_ref.refs_3_), custom_call_target="tpu_custom_call" | custom-call | flops 8388608000 | bytes 24576000 | tf_op jit(solution)/shard_map/head_logits/pallas_call | solution.py:658
  419.7 16.6 %head_logits.3 = (f32[4,1000,1024]{2,1,0:T(8,128)}, f32[1,1024]{1,0:T(1,128)}, f32[1,1024]{1,0:T(1,128)}, f32[1,1024]{1,0:T(1,128)}) custom-call(bf16[1024,1024]{1,0:T(8,128)(2,1)} %all-gather.10.cloned.1.call-done.rows_ref.refs_9_, bf16[4,1000,1024]{2,1,0:T(8,128)(2,1)} %bitcast.4.table_ref, s32[1,1024]{1,0:T(1,128)} %get-tuple-element.518.wanted_ref.refs_8_), custom_call_target="tpu_custom_call" | custom-call | flops 8388608000 | bytes 24576000 | tf_op jit(solution)/shard_map/head_logits/pallas_call | solution.py:658
  436.3 15.4 %head_row_grads.2 = bf16[1024,1024]{1,0:T(8,128)(2,1)} custom-call(f32[4,1000,1024]{2,1,0:T(8,128)} %get-tuple-element.214.logits_ref.refs_0_, f32[1,1024]{1,0:T(1,128)} %log_add_fusion.1.log_norm_ref.refs_1_, f32[1,1024]{1,0:T(1,128)} %bitcast.296, s32[1,1024]{1,0:T(1,128)} %get-tuple-element.517.wanted_ref.refs_3_, ...), custom_call_target="tpu_custom_call" | custom-call | flops 8388608000 | bytes 24576000 | tf_op jit(solution)/shard_map/head_row_grads/pallas_call | solution.py:713
  463.6 15.5 %head_row_grads.3 = bf16[1024,1024]{1,0:T(8,128)(2,1)} custom-call(f32[4,1000,1024]{2,1,0:T(8,128)} %get-tuple-element.222.logits_ref.refs_5_, f32[1,1024]{1,0:T(1,128)} %get-tuple-element.438.log_norm_ref.refs_6_, f32[1,1024]{1,0:T(1,128)} %bitcast.300, s32[1,1024]{1,0:T(1,128)} %get-tuple-element.518.wanted_ref.refs_8_, ...), custom_call_target="tpu_custom_call" | custom-call | flops 8388608000 | bytes 24576000 | tf_op jit(solution)/shard_map/head_row_grads/pallas_call | solution.py:713
  479.2 26.8 %head_table_grads.1.table_ref = f32[4,1000,1024]{2,1,0:T(8,128)} custom-call(f32[4,1000,1024]{2,1,0:T(8,128)} %get-tuple-element.214.logits_ref.refs_0_, f32[1,1024]{1,0:T(1,128)} %log_add_fusion.1.log_norm_ref.refs_1_, f32[1,1024]{1,0:T(1,128)} %bitcast.297, s32[1,1024]{1,0:T(1,128)} %get-tuple-element.517.wanted_ref.refs_3_, bf16[1024,1024]{1,0:T(8,128)(2,1)} %bitcast.270, ...), custom_call_target="tpu_custom_call" | custom-call | flops 16777216000 | bytes 49152000 | tf_op jit(solution)/shard_map/head_table_grads/pallas_call | solution.py:765
  506.0 18.3 %reduce-scatter.8.cloned.1.call-done = bf16[128,1024]{1,0:T(8,128)(2,1)} async-done(((bf16[1024,1024]{1,0:T(8,128)(2,1)}), bf16[128,1024]{1,0:T(8,128)(2,1)}) %reduce-scatter.8.cloned.1.call-update) | async-done | bytes 262160 | tf_op jit(solution)/shard_map/reduce_scatter | solution.py:1069
  531.1 16.9 %feed_forward_back.1 = (bf16[512,4096]{1,0:T(8,128)(2,1)}, f32[512,1024]{1,0:T(8,128)}) custom-call(bf16[512,1024]{1,0:T(8,128)(2,1)} %copy-done.11, f32[512,4096]{1,0:T(8,128)} %get-tuple-element.228.pre_ref, bf16[32,256,1024]{2,1,0:T(8,128)(2,1)} %bitcast.49.first_ref.second_ref, bf16[32,256,1024]{2,1,0:T(8,128)(2,1)} %bitcast.49.first_ref.second_ref), custom_call_target="tpu_custom_call" | custom-call | flops 8589934592 | bytes 33554432 | tf_op jit(solution)/shard_map/feed_forward_back/pallas_call | solution.py:374
  567.3 26.3 %attention_backward.1 = (bf16[512,1024]{1,0:T(8,128)(2,1)}, bf16[2,512,1024]{2,1,0:T(8,128)(2,1)}, bf16[2,1152,1024]{2,1,0:T(8,128)(2,1)}) custom-call(bf16[512,3072]{1,0:T(8,128)(2,1)} %copy-done.6, bf16[512,3072]{1,0:T(8,128)(2,1)} %copy-done.6, bf16[512,3072]{1,0:T(8,128)(2,1)} %copy-done.6, bf16[1152,2048]{1,0:T(8,128)(2,1)} %matmul_packed.5.refs_3_.refs_4_, ...), custom_call_target="tpu_custom_call" | custom-call | flops 8724152320 | bytes 25165824 | tf_op jit(solution)/shard_map/attention_backward/pallas_call | solution.py:181
  656.0 10.2 %collective-permute-start.56 = (bf16[1,256,1024]{2,1,0:T(8,128)(2,1)}, bf16[1,256,1024]{2,1,0:T(8,128)(2,1)}, u32[]{:S(2)}, u32[]{:S(2)}) collective-permute-start(bf16[1,256,1024]{2,1,0:T(8,128)(2,1)} %pad_bitcast_fusion.1.refs_34_), channel_id=1, source_target_pairs={{0,1},{1,0},{2,3},{3,2},{4,5},{5,4},{6,7},{7,6},{8,9},{9,8},{10,11... | collective-permute-start | bytes 1572872 | tf_op jit(solution)/shard_map/ppermute | solution.py:219
  675.8 8.4 gradient_piece.16
  716.6 9.2 %gradient_piece.22 = f32[6,256,512]{2,1,0:T(8,128)} custom-call(s32[1]{0:T(128)} %bitcast.80.me, bf16[4,128,512]{2,1,0:T(8,128)(2,1)S(1)} %get-tuple-element.249.refs_0_.refs_1_.refs_6_.refs_7_.refs_18_.refs_19_, bf16[4,128,512]{2,1,0:T(8,128)(2,1)S(1)} %get-tuple-element.249.refs_0_.refs_1_.refs_6_.refs_7_.refs_18_.refs_19_, ...), custom_call_target="tpu_custom_call" | custom-call | flops 1610612736 | bytes 18874368 | tf_op jit(solution)/shard_map/gradient_piece/pallas_call | solution.py:462
  725.9 9.2 %gradient_piece.23 = f32[6,256,512]{2,1,0:T(8,128)} custom-call(s32[1]{0:T(128)} %bitcast.80.me, bf16[4,128,512]{2,1,0:T(8,128)(2,1)S(1)} %get-tuple-element.249.refs_0_.refs_1_.refs_6_.refs_7_.refs_18_.refs_19_, bf16[4,128,512]{2,1,0:T(8,128)(2,1)S(1)} %get-tuple-element.249.refs_0_.refs_1_.refs_6_.refs_7_.refs_18_.refs_19_, ...), custom_call_target="tpu_custom_call" | custom-call | flops 1610612736 | bytes 18874368 | tf_op jit(solution)/shard_map/gradient_piece/pallas_call | solution.py:462
  753.5 13.2 %spread_piece.4 = bf16[2,1000,512]{2,1,0:T(8,128)(2,1)S(1)} custom-call(s32[1,4096]{1,0:T(1,128)S(1)} %bitcast.236, bf16[4096,1024]{1,0:T(8,128)(2,1)} %all-gather.12.cloned.1.call-done.grads_ref, f32[4,1000,1024]{2,1,0:T(8,128)} %head_table_grads.1.table_ref), custom_call_target="tpu_custom_call" | custom-call | flops 8388608000 | bytes 12582912 | tf_op jit(solution)/shard_map/spread_piece/pallas_call | solution.py:808
  768.8 13.0 %spread_piece.5 = bf16[2,1000,512]{2,1,0:T(8,128)(2,1)S(1)} custom-call(s32[1,4096]{1,0:T(1,128)S(1)} %bitcast.237, bf16[4096,1024]{1,0:T(8,128)(2,1)} %all-gather.12.cloned.1.call-done.grads_ref, f32[4,1000,1024]{2,1,0:T(8,128)} %head_table_grads.1.table_ref), custom_call_target="tpu_custom_call" | custom-call | flops 8388608000 | bytes 12582912 | tf_op jit(solution)/shard_map/spread_piece/pallas_call | solution.py:808
  803.2 13.0 %spread_piece.6 = f32[2,1000,512]{2,1,0:T(8,128)S(1)} custom-call(s32[1,4096]{1,0:T(1,128)S(1)} %bitcast.238, bf16[4096,1024]{1,0:T(8,128)(2,1)} %all-gather.12.cloned.1.call-done.grads_ref, f32[4,1000,1024]{2,1,0:T(8,128)} %head_table_grads.1.table_ref), custom_call_target="tpu_custom_call" | custom-call | flops 8388608000 | bytes 12582912 | tf_op jit(solution)/shard_map/spread_piece/pallas_call | solution.py:808
  816.2 14.5 %spread_piece.7 = f32[2,1000,512]{2,1,0:T(8,128)S(1)} custom-call(s32[1,4096]{1,0:T(1,128)S(1)} %bitcast.239, bf16[4096,1024]{1,0:T(8,128)(2,1)} %all-gather.12.cloned.1.call-done.grads_ref, f32[4,1000,1024]{2,1,0:T(8,128)} %head_table_grads.1.table_ref), custom_call_target="tpu_custom_call" | custom-call | flops 8388608000 | bytes 12582912 | tf_op jit(solution)/shard_map/spread_piece/pallas_call | solution.py:808
  850.6 12.0 %collective-permute-done.78 = bf16[480,1024]{1,0:T(8,128)(2,1)} collective-permute-done((bf16[480,1024]{1,0:T(8,128)(2,1)}, bf16[480,1024]{1,0:T(8,128)(2,1)}, u32[]{:S(2)}, u32[]{:S(2)}) %collective-permute-start.78) | collective-permute-done | bytes 983072 | tf_op jit(solution)/shard_map/ppermute | solution.py:500
  (658 shorter events, 513.1 us)
Async XLA Ops:
  7.2 56.6 %all-gather.14.cloned.1.call-start = ((), (), s32[]{:S(2)}) async-start(), calls=%async_computation.8 | async-start | bytes 2457600 | tf_op jit(solution)/shard_map/all_gather | solution.py:585
  12.0 116.2 %all-gather.16.cloned.1.call-start = ((), (), s32[]{:S(2)}) async-start(), calls=%async_computation.9 | async-start | bytes 2621440 | tf_op jit(solution)/shard_map/all_gather | solution.py:585
  20.1 212.1 %reduce-scatter.4.cloned.1.call-start = ((), (), s32[]{:S(2)}) async-start(), calls=%async_computation.3 | async-start | bytes 9437184 | tf_op jit(solution)/shard_map/reduce_scatter | solution.py:924
  69.7 64.4 %collective-permute-start.4 = (bf16[4,240,1024]{2,1,0:T(8,128)(2,1)}, bf16[4,240,1024]{2,1,0:T(8,128)(2,1)}, u32[]{:S(2)}, u32[]{:S(2)}) collective-permute-start(bf16[4,240,1024]{2,1,0:T(8,128)(2,1)} %bitcast.2), channel_id=1, source_target_pairs={{0,2},{2,0},{1,3},{3,1},{4,6},{6,4},{5,7},{7,5},{8,10},{10,8},{9,1... | collective-permute-start | bytes 5898248 | tf_op jit(solution)/shard_map/ppermute | solution.py:219
  71.3 62.9 %collective-permute-start.5 = (bf16[4,240,1024]{2,1,0:T(8,128)(2,1)}, bf16[4,240,1024]{2,1,0:T(8,128)(2,1)}, u32[]{:S(2)}, u32[]{:S(2)}) collective-permute-start(bf16[4,240,1024]{2,1,0:T(8,128)(2,1)} %bitcast.2), channel_id=1, source_target_pairs={{0,4},{4,0},{1,5},{5,1},{2,6},{6,2},{3,7},{7,3},{8,12},{12,8},{9,1... | collective-permute-start | bytes 5898248 | tf_op jit(solution)/shard_map/ppermute | solution.py:219
  134.2 251.4 %all-gather.18.cloned.1.call-start = ((), (), s32[]{:S(2)}) async-start(), calls=%async_computation.10 | async-start | bytes 2654208 | tf_op jit(solution)/shard_map/all_gather | solution.py:1025
  154.3 56.3 %collective-permute-start.11 = (bf16[4,240,1024]{2,1,0:T(8,128)(2,1)}, bf16[4,240,1024]{2,1,0:T(8,128)(2,1)}, u32[]{:S(2)}, u32[]{:S(2)}) collective-permute-start(bf16[4,240,1024]{2,1,0:T(8,128)(2,1)} %collective-permute-done.4), channel_id=1, source_target_pairs={{0,1},{1,0},{2,3},{3,2},{4,5},{5,4},{6,7},{7,6},{8,9},{9,8},{10,11... | collective-permute-start | bytes 5898248 | tf_op jit(solution)/shard_map/ppermute | solution.py:219
  168.7 48.4 %collective-permute-start.12 = (bf16[4,240,1024]{2,1,0:T(8,128)(2,1)}, bf16[4,240,1024]{2,1,0:T(8,128)(2,1)}, u32[]{:S(2)}, u32[]{:S(2)}) collective-permute-start(bf16[4,240,1024]{2,1,0:T(8,128)(2,1)} %collective-permute-done.5), channel_id=1, source_target_pairs={{0,1},{1,0},{2,3},{3,2},{4,5},{5,4},{6,7},{7,6},{8,9},{9,8},{10,11... | collective-permute-start | bytes 5898248 | tf_op jit(solution)/shard_map/ppermute | solution.py:219
  181.2 51.1 %collective-permute-start.8 = (bf16[4,256,1024]{2,1,0:T(8,128)(2,1)S(1)}, bf16[4,256,1024]{2,1,0:T(8,128)(2,1)}, u32[]{:S(2)}, u32[]{:S(2)}) collective-permute-start(bf16[4,256,1024]{2,1,0:T(8,128)(2,1)S(1)} %bitcast.263), channel_id=1, source_target_pairs={{0,2},{2,0},{1,3},{3,1},{4,6},{6,4},{5,7},{7,5},{8,10},{10,8},{9,1... | collective-permute-start | bytes 6291464 | tf_op jit(solution)/shard_map/ppermute | solution.py:219
  182.3 49.9 %collective-permute-start.9 = (bf16[4,256,1024]{2,1,0:T(8,128)(2,1)S(1)}, bf16[4,256,1024]{2,1,0:T(8,128)(2,1)}, u32[]{:S(2)}, u32[]{:S(2)}) collective-permute-start(bf16[4,256,1024]{2,1,0:T(8,128)(2,1)S(1)} %bitcast.264), channel_id=1, source_target_pairs={{0,4},{4,0},{1,5},{5,1},{2,6},{6,2},{3,7},{7,3},{8,12},{12,8},{9,1... | collective-permute-start | bytes 6291464 | tf_op jit(solution)/shard_map/ppermute | solution.py:219
  183.3 56.1 %collective-permute-start.20 = (bf16[4,256,1024]{2,1,0:T(8,128)(2,1)S(1)}, bf16[4,256,1024]{2,1,0:T(8,128)(2,1)}, u32[]{:S(2)}, u32[]{:S(2)}) collective-permute-start(bf16[4,256,1024]{2,1,0:T(8,128)(2,1)S(1)} %bitcast.265), channel_id=1, source_target_pairs={{0,1},{1,0},{2,3},{3,2},{4,5},{5,4},{6,7},{7,6},{8,9},{9,8},{10,11... | collective-permute-start | bytes 6291464 | tf_op jit(solution)/shard_map/ppermute | solution.py:219
  244.5 71.0 %collective-permute-start.21 = (bf16[4,256,1024]{2,1,0:T(8,128)(2,1)}, bf16[4,256,1024]{2,1,0:T(8,128)(2,1)}, u32[]{:S(2)}, u32[]{:S(2)}) collective-permute-start(bf16[4,256,1024]{2,1,0:T(8,128)(2,1)} %collective-permute-done.8), channel_id=1, source_target_pairs={{0,1},{1,0},{2,3},{3,2},{4,5},{5,4},{6,7},{7,6},{8,9},{9,8},{10,11... | collective-permute-start | bytes 6291464 | tf_op jit(solution)/shard_map/ppermute | solution.py:219
  270.9 50.7 %collective-permute-start.22 = (bf16[4,256,1024]{2,1,0:T(8,128)(2,1)}, bf16[4,256,1024]{2,1,0:T(8,128)(2,1)}, u32[]{:S(2)}, u32[]{:S(2)}) collective-permute-start(bf16[4,256,1024]{2,1,0:T(8,128)(2,1)} %collective-permute-done.9), channel_id=1, source_target_pairs={{0,1},{1,0},{2,3},{3,2},{4,5},{5,4},{6,7},{7,6},{8,9},{9,8},{10,11... | collective-permute-start | bytes 6291464 | tf_op jit(solution)/shard_map/ppermute | solution.py:219
  352.5 67.2 %all-gather.10.cloned.1.call-start = ((), (), s32[]{:S(2)}) async-start(), calls=%async_computation.4 | async-start | bytes 2359296 | tf_op jit(solution)/shard_map/all_gather | solution.py:1044
  388.7 117.3 %reduce-scatter.6.cloned.1.call-start = ((), (), s32[]{:S(2)}) async-start(), calls=%async_computation.5 | async-start | bytes 2359296 | tf_op jit(solution)/shard_map/reduce_scatter | solution.py:1069
  451.8 72.5 %reduce-scatter.8.cloned.1.call-start = ((), (), s32[]{:S(2)}) async-start(), calls=%async_computation.6 | async-start | bytes 2359296 | tf_op jit(solution)/shard_map/reduce_scatter | solution.py:1069
  479.2 274.3 %all-gather.12.cloned.1.call-start = ((), (), s32[]{:S(2)}) async-start(), calls=%async_computation.7 | async-start | bytes 9437184 | tf_op jit(solution)/shard_map/all_gather | solution.py:1151
  548.0 66.1 %collective-permute-start.49 = (bf16[1,512,4096]{2,1,0:T(8,128)(2,1)}, bf16[1,512,4096]{2,1,0:T(8,128)(2,1)}, u32[]{:S(2)}, u32[]{:S(2)}) collective-permute-start(bf16[1,512,4096]{2,1,0:T(8,128)(2,1)} %bitcast.225), channel_id=1, source_target_pairs={{0,1},{1,0},{2,3},{3,2},{4,5},{5,4},{6,7},{7,6},{8,9},{9,8},{10,11... | collective-permute-start | bytes 12582920 | tf_op jit(solution)/shard_map/ppermute | solution.py:219
  594.6 59.6 %collective-permute-start.55 = (bf16[2,1152,1024]{2,1,0:T(8,128)(2,1)}, bf16[2,1152,1024]{2,1,0:T(8,128)(2,1)}, u32[]{:S(2)}, u32[]{:S(2)}) collective-permute-start(bf16[2,1152,1024]{2,1,0:T(8,128)(2,1)} %get-tuple-element.257.grad_ref.refs_16_.refs_28_), channel_id=1, source_target_pairs={{0,1},{1,0},{2,3},{3,2},{4,5},{5,4},{6,7},{7,6},{8,9},{9,8},{10,11... | collective-permute-start | bytes 14155784 | tf_op jit(solution)/shard_map/ppermute | solution.py:219
  669.4 65.7 %collective-permute-start.61 = (bf16[5,256,512]{2,1,0:T(8,128)(2,1)}, bf16[5,256,512]{2,1,0:T(8,128)(2,1)}, u32[]{:S(2)}, u32[]{:S(2)}) collective-permute-start(bf16[5,256,512]{2,1,0:T(8,128)(2,1)} %copy-done.27), channel_id=1, source_target_pairs={{0,2},{2,0},{1,3},{3,1},{4,6},{6,4},{5,7},{7,5},{8,10},{10,8},{9,1... | collective-permute-start | bytes 3932168 | tf_op jit(solution)/shard_map/ppermute | solution.py:219
  672.2 65.0 %collective-permute-start.62 = (bf16[5,256,512]{2,1,0:T(8,128)(2,1)}, bf16[5,256,512]{2,1,0:T(8,128)(2,1)}, u32[]{:S(2)}, u32[]{:S(2)}) collective-permute-start(bf16[5,256,512]{2,1,0:T(8,128)(2,1)} %copy-done.26), channel_id=1, source_target_pairs={{0,4},{4,0},{1,5},{5,1},{2,6},{6,2},{3,7},{7,3},{8,12},{12,8},{9,1... | collective-permute-start | bytes 3932168 | tf_op jit(solution)/shard_map/ppermute | solution.py:219
  692.6 52.9 %collective-permute-start.63 = (bf16[6,256,512]{2,1,0:T(8,128)(2,1)S(1)}, bf16[6,256,512]{2,1,0:T(8,128)(2,1)}, u32[]{:S(2)}, u32[]{:S(2)}) collective-permute-start(bf16[6,256,512]{2,1,0:T(8,128)(2,1)S(1)} %gradient_piece.16), channel_id=1, source_target_pairs={{0,2},{2,0},{1,3},{3,1},{4,6},{6,4},{5,7},{7,5},{8,10},{10,8},{9,1... | collective-permute-start | bytes 4718600 | tf_op jit(solution)/shard_map/ppermute | solution.py:219
  692.8 55.7 %collective-permute-start.64 = (bf16[6,256,512]{2,1,0:T(8,128)(2,1)S(1)}, bf16[6,256,512]{2,1,0:T(8,128)(2,1)}, u32[]{:S(2)}, u32[]{:S(2)}) collective-permute-start(bf16[6,256,512]{2,1,0:T(8,128)(2,1)S(1)} %gradient_piece.17), channel_id=1, source_target_pairs={{0,4},{4,0},{1,5},{5,1},{2,6},{6,2},{3,7},{7,3},{8,12},{12,8},{9,1... | collective-permute-start | bytes 4718600 | tf_op jit(solution)/shard_map/ppermute | solution.py:219
  705.9 60.8 %collective-permute-start.59 = (bf16[4,128,512]{2,1,0:T(8,128)(2,1)}, bf16[4,128,512]{2,1,0:T(8,128)(2,1)}, u32[]{:S(2)}, u32[]{:S(2)}) collective-permute-start(bf16[4,128,512]{2,1,0:T(8,128)(2,1)} %get-tuple-element.268), channel_id=1, source_target_pairs={{0,4},{4,0},{1,5},{5,1},{2,6},{6,2},{3,7},{7,3},{8,12},{12,8},{9,1... | collective-permute-start | bytes 1572872 | tf_op jit(solution)/shard_map/ppermute | solution.py:219
  (164 other events, 1902.2 us)
Sparse Core Ops, SparseCore 0:
  12.1 46.3 all-gather.13
  60.6 44.7 all-gather.15
  134.3 89.0 reduce-scatter.3
  352.7 32.8 all-gather.17
  388.8 28.0 all-gather.9
  451.9 34.9 reduce-scatter.5
  489.8 34.4 reduce-scatter.7
  654.3 91.8 all-gather.11
